TPU v7x, 32 devices: a whole 2x2x4 slice. The times are simulated.
32 devices in a mesh: seq: 8 (over z, y), batch: 4 (over x, core).
Axes of the slice: x: 2, y: 2, z: 4, core: 2. Of those that a mesh axis runs over, the one named last changes fastest.
Arguments:
- tokens: int32 [16, 1536], P('batch', 'seq'), may hold values from 0 to 255
- loss_mask: int32 [16, 512], P('batch', 'seq'), may hold values 0 or 1
- cotangent: bfloat16 [16, 512, 512], P('batch', 'seq'), may hold values from -6 to 6
- embed: bfloat16 [256, 512], replicated, may hold values from -6 to 6
- gain_attn: bfloat16 [2, 512], replicated, may hold values from 0.5 to 1.5
- w_qkv: bfloat16 [2, 512, 1536], replicated, may hold values from -0.25 to 0.25
- w_out: bfloat16 [2, 512, 512], replicated, may hold values from -2 to 2
- gain_ffn: bfloat16 [2, 512], replicated, may hold values from 0.5 to 1.5
- w_up: bfloat16 [2, 512, 2048], replicated, may hold values from -0.25 to 0.25
- w_down: bfloat16 [2, 2048, 512], replicated, may hold values from -0.125 to 0.125
- w_pool: bfloat16 [1536, 512], replicated, may hold values from -0.15625 to 0.15625
Outputs:
- full_out: bfloat16 [16, 1536, 512], P('batch', 'seq')
- short_out: bfloat16 [16, 512, 512], P('batch', 'seq')
- input_grad: float32 [16, 1536, 512], P('batch', 'seq')
- embed_grad: float32 [256, 512], P('batch', 'seq')
- gain_attn_grad: float32 [2, 512], replicated
- w_qkv_grad: float32 [2, 512, 1536], P(None, 'batch', 'seq')
- w_out_grad: float32 [2, 512, 512], P(None, 'batch', 'seq')
- gain_ffn_grad: float32 [2, 512], replicated
- w_up_grad: float32 [2, 512, 2048], P(None, 'batch', 'seq')
- w_down_grad: float32 [2, 2048, 512], P(None, 'batch', 'seq')
- w_pool_grad: float32 [1536, 512], P('batch', 'seq')
All inputs are finite; a program needn't handle non-finite values. No bound on the sum of `loss_mask` on one device may be relied on, other than what follows from the above.
Results may differ from a plain program's by a relative error of at most 0.02.
Values may be sent and summed in bfloat16 or wider, within the bound.
No kernel may reach another device: no remote copies, remote signals or barrier semaphores. Data moves between devices by JAX's collectives and lax.ppermute only.
A program may use at most 320 MiB of HBM per device.

v0:
```python
import jax
import jax.numpy as jnp
from jax import lax
from jax.sharding import PartitionSpec as P

D = 512
H = 8
DH = 64


epsilon = 1e-05
masked_score = -1e30


def from_behind(value, axis, steps):
    count = lax.axis_size(axis)
    first, last = (max(0, -steps), min(count, count - steps))
    return lax.ppermute(value, axis, [(source, source + steps) for source in range(first, last)])


def matmul(left, right):
    return jnp.dot(left, right, preferred_element_type=jnp.float32)


def left_grad(left, grad):
    return lax.dot_general(left, grad, (((0,), (0,)), ((), ())), preferred_element_type=jnp.float32)


def right_grad(grad, weight):
    return lax.dot_general(
        grad, weight, (((1,), (1,)), ((), ())), preferred_element_type=jnp.float32
    )


def normalize(inputs, gain):
    centred = inputs - jnp.mean(inputs, -1, keepdims=True)
    inverse = lax.rsqrt(jnp.mean(centred * centred, -1, keepdims=True) + epsilon)
    normed = centred * inverse
    return (normed * gain, normed, inverse)


def normalize_back(grad, normed, inverse, gain):
    scaled = grad * gain
    result = inverse * (
        scaled
        - jnp.mean(scaled, -1, keepdims=True)
        - normed * jnp.mean(scaled * normed, -1, keepdims=True)
    )
    return (result, jnp.sum(grad * normed, axis=(0, 1)))


def angles(positions, head_size):
    half_size = head_size // 2
    freqs = 10000.0 ** (-jnp.arange(half_size).astype(jnp.float32) / half_size)
    phase = positions.astype(jnp.float32)[:, None] * freqs[None, :]
    return (jnp.cos(phase)[:, None, :], jnp.sin(phase)[:, None, :])


def rotate(inputs, cosine, sine):
    half_size = inputs.shape[-1] // 2
    leading = inputs[..., :half_size]
    trailing = inputs[..., half_size:]
    return jnp.concatenate(
        [leading * cosine - trailing * sine, leading * sine + trailing * cosine], -1
    )


def attend_rows(queries, keys, values, query_pos):
    scores = jnp.einsum("qhd,khd->hqk", queries, keys, preferred_element_type=jnp.float32)
    allowed = jnp.arange(keys.shape[0], dtype=jnp.int32)[None, :] <= query_pos[:, None]
    scores = jnp.where(allowed[None], scores, masked_score)
    highest = jnp.max(scores, -1, keepdims=True)
    expon = jnp.exp(scores - highest)
    totals = jnp.sum(expon, -1, keepdims=True)
    probs = (expon / totals).astype(jnp.bfloat16)
    mixed = jnp.einsum("hqk,khd->qhd", probs, values, preferred_element_type=jnp.float32)
    return (mixed, (highest + jnp.log(totals))[..., 0])


def query_pass(queries, keys, values, grad_mixed, logsum, query_pos):
    scores = jnp.einsum("qhd,khd->hqk", queries, keys, preferred_element_type=jnp.float32)
    allowed = jnp.arange(keys.shape[0], dtype=jnp.int32)[None, :] <= query_pos[:, None]
    scores = jnp.where(allowed[None], scores, masked_score)
    probs = jnp.exp(scores - logsum[..., None])
    grad_probs = jnp.einsum("qhd,khd->hqk", grad_mixed, values, preferred_element_type=jnp.float32)
    delta = jnp.sum(probs * grad_probs, -1)
    grad_scores = (probs * (grad_probs - delta[..., None])).astype(jnp.bfloat16)
    grad_queries = jnp.einsum("hqk,khd->qhd", grad_scores, keys, preferred_element_type=jnp.float32)
    return (probs, grad_scores, delta, grad_queries)


def block_forward(inputs, weights):
    gain_attn, w_qkv, w_out, gain_ffn, w_up, w_down = weights
    rows, span, width = inputs.shape
    positions = lax.axis_index("seq") * span + jnp.arange(span, dtype=jnp.int32)
    cosine, sine = angles(positions, DH)
    attn_in, attn_normed, attn_inv = normalize(inputs, gain_attn)
    attn_low = attn_in.astype(jnp.bfloat16).reshape(rows * span, width)
    joined = matmul(attn_low, w_qkv).reshape(rows, span, 3, H, DH)
    queries = (rotate(joined[:, :, 0], cosine, sine) * DH ** (-0.5)).astype(jnp.bfloat16)
    keys = rotate(joined[:, :, 1], cosine, sine).astype(jnp.bfloat16)
    values = joined[:, :, 2].astype(jnp.bfloat16)
    all_keys, all_values = (
        lax.all_gather(keys, "seq", axis=1, tiled=True),
        lax.all_gather(values, "seq", axis=1, tiled=True),
    )
    mixed, logsum = lax.map(
        lambda member: attend_rows(member[0], member[1], member[2], positions),
        (queries, all_keys, all_values),
    )
    mixed_low = mixed.astype(jnp.bfloat16).reshape(rows * span, width)
    middle = inputs + matmul(mixed_low, w_out).reshape(rows, span, width)
    ffn_in, ffn_normed, ffn_inv = normalize(middle, gain_ffn)
    ffn_low = ffn_in.astype(jnp.bfloat16).reshape(rows * span, width)
    hidden = matmul(ffn_low, w_up)
    active = jax.nn.gelu(hidden, approximate=True).astype(jnp.bfloat16)
    output = middle + matmul(active, w_down).reshape(rows, span, width)
    kept = (
        positions,
        cosine,
        sine,
        attn_normed,
        attn_inv,
        attn_low,
        queries,
        keys,
        values,
        all_keys,
        all_values,
        logsum,
        mixed_low,
        ffn_normed,
        ffn_inv,
        ffn_low,
        hidden,
        active,
    )
    return (output, kept)


def block_backward(grad_out, kept, weights):
    gain_attn, w_qkv, w_out, gain_ffn, w_up, w_down = weights
    (
        positions,
        cosine,
        sine,
        attn_normed,
        attn_inv,
        attn_low,
        queries,
        keys,
        values,
        all_keys,
        all_values,
        logsum,
        mixed_low,
        ffn_normed,
        ffn_inv,
        ffn_low,
        hidden,
        active,
    ) = kept
    rows, span, width = grad_out.shape
    grad_branch_ffn = grad_out.astype(jnp.bfloat16).reshape(rows * span, width)
    grad_w_down = left_grad(active, grad_branch_ffn)
    grad_active = right_grad(grad_branch_ffn, w_down)
    unused, gelu_back = jax.vjp(lambda inner: jax.nn.gelu(inner, approximate=True), hidden)
    grad_hidden = gelu_back(grad_active)[0].astype(jnp.bfloat16)
    grad_w_up = left_grad(ffn_low, grad_hidden)
    grad_ffn_in = right_grad(grad_hidden, w_up).reshape(rows, span, width)
    grad_middle_norm, grad_gain_ffn = normalize_back(grad_ffn_in, ffn_normed, ffn_inv, gain_ffn)
    grad_middle = grad_out + grad_middle_norm
    grad_branch = grad_middle.astype(jnp.bfloat16).reshape(rows * span, width)
    grad_w_out = left_grad(mixed_low, grad_branch)
    grad_mixed = right_grad(grad_branch, w_out).astype(jnp.bfloat16).reshape(rows, span, H, DH)

    def full_pass(member):
        probs, grad_scores, delta, grad_queries = query_pass(
            member[0], member[1], member[2], member[3], member[4], positions
        )
        part_keys = jnp.einsum(
            "hqk,qhd->khd", grad_scores, member[0], preferred_element_type=jnp.float32
        )
        part_values = jnp.einsum(
            "hqk,qhd->khd",
            probs.astype(jnp.bfloat16),
            member[3],
            preferred_element_type=jnp.float32,
        )
        return (grad_queries, part_keys, part_values)

    grad_queries, part_keys, part_values = lax.map(
        full_pass, (queries, all_keys, all_values, grad_mixed, logsum)
    )
    grad_keys, grad_values = (
        lax.psum_scatter(
            part_keys.astype(jnp.bfloat16), "seq", scatter_dimension=1, tiled=True
        ).astype(jnp.float32),
        lax.psum_scatter(
            part_values.astype(jnp.bfloat16), "seq", scatter_dimension=1, tiled=True
        ).astype(jnp.float32),
    )
    grad_q_pre = rotate(grad_queries * DH ** (-0.5), cosine, -sine)
    grad_k_pre = rotate(grad_keys, cosine, -sine)
    grad_joined = jnp.stack([grad_q_pre, grad_k_pre, grad_values], 2).astype(jnp.bfloat16)
    grad_joined = grad_joined.reshape(rows * span, 3 * width)
    grad_w_qkv = left_grad(attn_low, grad_joined)
    grad_attn_in = right_grad(grad_joined, w_qkv).reshape(rows, span, width)
    grad_in_norm, grad_gain_attn = normalize_back(grad_attn_in, attn_normed, attn_inv, gain_attn)
    grad_inputs = grad_middle + grad_in_norm
    return (
        grad_inputs,
        (grad_gain_attn, grad_w_qkv, grad_w_out, grad_gain_ffn, grad_w_up, grad_w_down),
    )


def body(
    tokens, loss_mask, cotangent, embed, gain_attn, w_qkv, w_out, gain_ffn, w_up, w_down, w_pool
):
    rows, span = tokens.shape
    vocab = embed.shape[0]
    params = (gain_attn, w_qkv, w_out, gain_ffn, w_up, w_down)
    first_weights = tuple((member[0] for member in params))
    second_weights = tuple((member[1] for member in params))
    onehot = (tokens[..., None] == jnp.arange(vocab, dtype=jnp.int32)).astype(jnp.bfloat16)
    inputs = jnp.einsum("rtv,vd->rtd", onehot, embed, preferred_element_type=jnp.float32)
    first_out, first_kept = block_forward(inputs, first_weights)
    first_low = first_out.astype(jnp.bfloat16)
    edge = from_behind(first_low[:, span - 2 :, :], "seq", 1)
    shifted = jnp.concatenate([edge, first_low[:, : span - 2, :]], 1)
    grouped = shifted.reshape(rows, span // 3, 3 * D)
    pooled = jnp.einsum("rtc,cd->rtd", grouped, w_pool, preferred_element_type=jnp.float32)
    second_out, second_kept = block_forward(pooled, second_weights)
    start_grad = cotangent.astype(jnp.float32) * loss_mask.astype(jnp.float32)[..., None]
    grad_pooled, second_grads = block_backward(start_grad, second_kept, second_weights)
    grad_pooled_low = grad_pooled.astype(jnp.bfloat16)
    grad_pool = jnp.einsum(
        "rtc,rtd->cd", grouped, grad_pooled_low, preferred_element_type=jnp.float32
    )
    grad_grouped = jnp.einsum(
        "rtd,cd->rtc", grad_pooled_low, w_pool, preferred_element_type=jnp.float32
    )
    grad_shifted = grad_grouped.reshape(rows, span, D)
    carried = from_behind(grad_shifted[:, :2, :], "seq", -1)
    grad_first = jnp.concatenate([grad_shifted[:, 2:, :], carried], 1)
    grad_inputs, first_grads = block_backward(grad_first, first_kept, first_weights)
    grad_embed = lax.dot_general(
        onehot.reshape(rows * span, vocab).astype(jnp.float32),
        grad_inputs.reshape(rows * span, D),
        (((0,), (0,)), ((), ())),
        precision=lax.Precision.HIGHEST,
    )
    stacked = [jnp.stack([first_grads[number], second_grads[number]]) for number in range(6)]
    partial_sums = (
        lax.psum_scatter(
            stacked[1].astype(jnp.bfloat16), "batch", scatter_dimension=1, tiled=True
        ).astype(jnp.float32),
        lax.psum_scatter(
            stacked[2].astype(jnp.bfloat16), "batch", scatter_dimension=1, tiled=True
        ).astype(jnp.float32),
        lax.psum_scatter(
            stacked[4].astype(jnp.bfloat16), "batch", scatter_dimension=1, tiled=True
        ).astype(jnp.float32),
        lax.psum_scatter(
            stacked[5].astype(jnp.bfloat16), "batch", scatter_dimension=1, tiled=True
        ).astype(jnp.float32),
        lax.psum_scatter(
            grad_pool[None].astype(jnp.bfloat16), "batch", scatter_dimension=1, tiled=True
        ).astype(jnp.float32),
        lax.psum_scatter(
            grad_embed[None].astype(jnp.bfloat16), "batch", scatter_dimension=1, tiled=True
        ).astype(jnp.float32),
    )
    totals = (
        lax.psum_scatter(
            partial_sums[0].astype(jnp.bfloat16), "seq", scatter_dimension=2, tiled=True
        ).astype(jnp.float32),
        lax.psum_scatter(
            partial_sums[1].astype(jnp.bfloat16), "seq", scatter_dimension=2, tiled=True
        ).astype(jnp.float32),
        lax.psum_scatter(
            partial_sums[2].astype(jnp.bfloat16), "seq", scatter_dimension=2, tiled=True
        ).astype(jnp.float32),
        lax.psum_scatter(
            partial_sums[3].astype(jnp.bfloat16), "seq", scatter_dimension=2, tiled=True
        ).astype(jnp.float32),
        lax.psum_scatter(
            partial_sums[4].astype(jnp.bfloat16), "seq", scatter_dimension=2, tiled=True
        ).astype(jnp.float32),
        lax.psum_scatter(
            partial_sums[5].astype(jnp.bfloat16), "seq", scatter_dimension=2, tiled=True
        ).astype(jnp.float32),
    )
    gain_totals = lax.psum((stacked[0], stacked[3]), ("seq", "batch"))
    return (
        first_low,
        second_out.astype(jnp.bfloat16),
        grad_inputs,
        totals[5][0],
        gain_totals[0],
        totals[0],
        totals[1],
        gain_totals[1],
        totals[2],
        totals[3],
        totals[4][0],
    )


def solution(mesh):
    in_specs = (
        P("batch", "seq"),
        P("batch", "seq"),
        P("batch", "seq", None),
        P(),
        P(),
        P(),
        P(),
        P(),
        P(),
        P(),
        P(),
    )
    out_specs = (
        P("batch", "seq", None),
        P("batch", "seq", None),
        P("batch", "seq", None),
        P("batch", "seq"),
        P(),
        P(None, "batch", "seq"),
        P(None, "batch", "seq"),
        P(),
        P(None, "batch", "seq"),
        P(None, "batch", "seq"),
        P("batch", "seq"),
    )
    return jax.shard_map(body, mesh=mesh, in_specs=in_specs, out_specs=out_specs, check_vma=False)
```

profile of v0, /device:TPU:0, one launch (start us, length us, event | category | flops | bytes accessed | tf_op | source)
XLA Modules:
  0.0 1744.5 jit_solution(13508572929948378194)
XLA Ops:
  38.6 165.0 %all-gather.11.cloned.1.call-done = bf16[4,1536,1,8,64]{4,3,2,0,1:T(8,128)(2,1)} async-done(((bf16[4,192,1,8,64]{4,3,2,0,1:T(8,128)(2,1)}), bf16[4,1536,1,8,64]{4,3,2,0,1:T(8,128)(2,1)}) %all-gather.11.cloned.1.call-update) | async-done | bytes 6291472 | tf_op jit(solution)/shard_map/all_gather | solution.py:105
  217.9 162.5 %all-gather.7.cloned.1.call-done = bf16[4,1536,8,64]{3,2,0,1:T(8,128)(2,1)} async-done(((bf16[4,192,8,64]{3,2,0,1:T(8,128)(2,1)}), bf16[4,1536,8,64]{3,2,0,1:T(8,128)(2,1)}) %all-gather.7.cloned.1.call-update) | async-done | bytes 6291472 | tf_op jit(solution)/shard_map/all_gather | solution.py:104
  394.5 40.0 %while.60 = (s32[]{:T(128)}, bf16[4,192,8,64]{1,3,2,0:T(8,128)(2,1)}, f32[4,8,192]{2,1,0:T(8,128)S(1)}, bf16[4,1536,8,64]{1,3,2,0:T(8,128)(2,1)}, bf16[4,192,8,6...) while((s32[]{:T(128)}, bf16[4,192,8,64]{1,3,2,0:T(8,128)(2,1)}, ...), condition=%wide.region_5.6_spmd.clone.clone, body=%wide.region_2.5_spmd.clone.sunk.clone | while | flops 625507008 | bytes 33482324 | solution.py:107
  466.4 64.6 %all-gather.13.cloned.1.call-done = bf16[4,512,1,8,64]{4,3,2,0,1:T(8,128)(2,1)} async-done(((bf16[4,64,1,8,64]{4,3,2,0,1:T(8,128)(2,1)}), bf16[4,512,1,8,64]{4,3,2,0,1:T(8,128)(2,1)}) %all-gather.13.cloned.1.call-update) | async-done | bytes 2097168 | tf_op jit(solution)/shard_map/all_gather | solution.py:105
  536.5 68.2 %all-gather.9.cloned.1.call-done = bf16[4,512,8,64]{3,2,0,1:T(8,128)(2,1)} async-done(((bf16[4,64,8,64]{3,2,0,1:T(8,128)(2,1)}), bf16[4,512,8,64]{3,2,0,1:T(8,128)(2,1)}) %all-gather.9.cloned.1.call-update) | async-done | bytes 2097168 | tf_op jit(solution)/shard_map/all_gather | solution.py:104
  636.7 34.7 %while.62 = (s32[]{:T(128)}, f32[4,64,8,64]{1,3,2,0:T(8,128)}, bf16[4,512,8,64]{1,3,2,0:T(8,128)(2,1)}, bf16[4,512,8,64]{1,3,2,0:T(8,128)(2,1)}, bf16[4,512,8,64...) while((s32[]{:T(128)}, f32[4,64,8,64]{1,3,2,0:T(8,128)}, ...), condition=%wide.region_20.21_spmd.clone.clone, body=%wide.region_18.20_spmd.clone.sunk.clone | while | flops 169901632 | bytes 46022884 | solution.py:192
  701.3 50.2 %reduce-scatter.40.cloned.1.call-done = bf16[64,2048]{1,0:T(8,128)(2,1)} async-done(((bf16[512,2048]{1,0:T(8,128)(2,1)}), bf16[64,2048]{1,0:T(8,128)(2,1)}) %reduce-scatter.40.cloned.1.call-update) | async-done | bytes 262160
  756.5 65.1 %reduce-scatter.42.cloned.1.call-done = bf16[64,2048]{1,0:T(8,128)(2,1)} async-done(((bf16[512,2048]{1,0:T(8,128)(2,1)}), bf16[64,2048]{1,0:T(8,128)(2,1)}) %reduce-scatter.42.cloned.1.call-update) | async-done | bytes 262160
  859.9 80.7 %while.63 = (s32[]{:T(128)}, f32[4,192,8,64]{1,3,2,0:T(8,128)}, bf16[4,1536,8,64]{1,3,2,0:T(8,128)(2,1)}, bf16[4,1536,8,64]{1,3,2,0:T(8,128)(2,1)}, bf16[4,1536,...) while((s32[]{:T(128)}, f32[4,192,8,64]{1,3,2,0:T(8,128)}, ...), condition=%wide.region_29.30_spmd.clone.clone, body=%wide.region_27.29_spmd.clone.sunk.clone | while | flops 1538554624 | bytes 128635568 | solution.py:192
  940.6 18.5 %copy.114 = bf16[4,1536,8,64]{3,2,0,1:T(8,128)(2,1)} copy(bf16[4,1536,8,64]{1,3,2,0:T(8,128)(2,1)} %get-tuple-element.203) | data formatting | bytes 12582912
  977.0 18.5 %copy.116 = bf16[4,1536,8,64]{3,2,0,1:T(8,128)(2,1)} copy(bf16[4,1536,8,64]{1,3,2,0:T(8,128)(2,1)} %get-tuple-element.204) | data formatting | bytes 12582912
  995.5 18.0 %reshape.594 = bf16[1536,2048]{1,0:T(8,128)(2,1)} reshape(bf16[1536,4,8,64]{3,2,1,0:T(8,128)(2,1)} %bitcast.514) | data formatting | bytes 12582912
  1026.3 68.6 %reduce-scatter.44.cloned.1.call-done = bf16[192,2048]{1,0:T(8,128)(2,1)} async-done(((bf16[1536,2048]{1,0:T(8,128)(2,1)}), bf16[192,2048]{1,0:T(8,128)(2,1)}) %reduce-scatter.44.cloned.1.call-update) | async-done | bytes 786448
  1100.6 115.1 %reduce-scatter.46.cloned.1.call-done = bf16[192,2048]{1,0:T(8,128)(2,1)} async-done(((bf16[1536,2048]{1,0:T(8,128)(2,1)}), bf16[192,2048]{1,0:T(8,128)(2,1)}) %reduce-scatter.46.cloned.1.call-update) | async-done | bytes 786448
  1273.0 19.6 %reduce-scatter.32.cloned.1.call-done = bf16[2,128,2048]{2,1,0:T(8,128)(2,1)} async-done(((bf16[2,512,2048]{2,1,0:T(8,128)(2,1)}), bf16[2,128,2048]{2,1,0:T(8,128)(2,1)}) %reduce-scatter.32.cloned.1.call-update) | async-done | bytes 1048592 | tf_op jit(solution)/shard_map/reduce_scatter | solution.py:261
  1292.7 23.0 %reduce-scatter.26.cloned.1.call-done = bf16[1,64,512]{2,1,0:T(8,128)(2,1)} async-done(((bf16[1,256,512]{2,1,0:T(8,128)(2,1)}), bf16[1,64,512]{2,1,0:T(8,128)(2,1)}) %reduce-scatter.26.cloned.1.call-update) | async-done | bytes 65552 | tf_op jit(solution)/shard_map/reduce_scatter | solution.py:270
  1317.4 25.7 %reduce-scatter.30.cloned.1.call-done = bf16[2,128,512]{2,1,0:T(8,128)(2,1)} async-done(((bf16[2,512,512]{2,1,0:T(8,128)(2,1)}), bf16[2,128,512]{2,1,0:T(8,128)(2,1)}) %reduce-scatter.30.cloned.1.call-update) | async-done | bytes 262160 | tf_op jit(solution)/shard_map/reduce_scatter | solution.py:258
  1345.0 45.3 %reduce-scatter.36.cloned.1.call-done = bf16[2,512,512]{2,1,0:T(8,128)(2,1)} async-done(((bf16[2,2048,512]{2,1,0:T(8,128)(2,1)}), bf16[2,512,512]{2,1,0:T(8,128)(2,1)}) %reduce-scatter.36.cloned.1.call-update) | async-done | bytes 1048592 | tf_op jit(solution)/shard_map/reduce_scatter | solution.py:264
  1393.9 36.9 %reduce-scatter.28.cloned.1.call-done = bf16[2,128,1536]{2,1,0:T(8,128)(2,1)} async-done(((bf16[2,512,1536]{2,1,0:T(8,128)(2,1)}), bf16[2,128,1536]{2,1,0:T(8,128)(2,1)}) %reduce-scatter.28.cloned.1.call-update) | async-done | bytes 786448 | tf_op jit(solution)/shard_map/reduce_scatter | solution.py:255
  1438.9 56.4 %reduce-scatter.50.cloned.1.call-done = bf16[64,384]{1,0:T(8,128)(2,1)} async-done(((bf16[512,384]{1,0:T(8,128)(2,1)}), bf16[64,384]{1,0:T(8,128)(2,1)}) %reduce-scatter.50.cloned.1.call-update) | async-done | bytes 49168
  1497.1 64.4 %reduce-scatter.34.cloned.1.call-done = bf16[2,128,256]{2,1,0:T(8,128)(2,1)} async-done(((bf16[2,128,2048]{2,1,0:T(8,128)(2,1)}), bf16[2,128,256]{2,1,0:T(8,128)(2,1)}) %reduce-scatter.34.cloned.1.call-update) | async-done | bytes 131088 | tf_op jit(solution)/shard_map/reduce_scatter | solution.py:281
  1563.1 40.1 %all-reduce.3 = (f32[2,512]{1,0:T(2,128)}, f32[2,512]{1,0:T(2,128)}) all-reduce(f32[2,512]{1,0:T(2,128)S(1)} %pad_maximum_fusion.10, f32[2,512]{1,0:T(2,128)S(1)} %pad_maximum_fusion.11), channel_id=1, replica_groups=mesh['seq'=8,'batch'=4] {'seq','batch'}, use_global_device_ids=true, to_apply=%region_38.39 | all-reduce | flops 2048 | bytes 16384 | tf_op jit(solution)/shard_map/psum | solution.py:294
  1603.3 22.2 %reduce-scatter.48.cloned.1.call-done = bf16[64,64]{1,0:T(8,128)(2,1)} async-done(((bf16[512,64]{1,0:T(8,128)(2,1)}), bf16[64,64]{1,0:T(8,128)(2,1)}) %reduce-scatter.48.cloned.1.call-update) | async-done | bytes 8208
  1626.9 105.6 %all-reduce.7.cloned.1.call-done = (bf16[2,128,1536]{1,0,2:T(2,128)(2,1)}, bf16[2,128,512]{1,0,2:T(2,128)(2,1)}, bf16[2,512,512]{1,0,2:T(2,128)(2,1)}) async-done(((bf16[2,128,1536]{1,0,2:T(2,128)(2,1)}, bf16[2,128,512]{1,0,2:T(2,128)(2,1)}, bf16[2,512,512]{1,0,2:T(2,128)(2,1)}), (bf16[2,128,1536]{1,0,2:T(2,128)(2,1)}, bf16[2,128,512]{1,0,2:T(2,128)(2,1)}, ...) | async-done | bytes 2097168
  (560 shorter events, 485.6 us)
Async XLA Ops:
  7.2 444.0 %copy-start = (bf16[1536,512]{1,0:T(8,128)(2,1)S(1)}, bf16[1536,512]{1,0:T(8,128)(2,1)}, u32[]{:S(2)}) copy-start(bf16[1536,512]{1,0:T(8,128)(2,1)} %param.29) | copy-start | bytes 4718596
  7.2 196.4 %all-gather.11.cloned.1.call-start = ((), (), s32[]{:S(2)}) async-start(), calls=%async_computation.22 | async-start | bytes 14155776 | tf_op jit(solution)/shard_map/all_gather | solution.py:105
  8.9 425.6 %copy-start.2 = (f32[4,192,512]{2,1,0:T(8,128)}, f32[4,192,512]{2,1,0:T(8,128)S(1)}, u32[]{:S(2)}) copy-start(f32[4,192,512]{2,1,0:T(8,128)S(1)} %get-tuple-element.542) | copy-start | bytes 4718596
  24.3 356.1 %all-gather.7.cloned.1.call-start = ((), (), s32[]{:S(2)}) async-start(), calls=%async_computation.13 | async-start | bytes 14155776 | tf_op jit(solution)/shard_map/all_gather | solution.py:104
  34.2 496.9 %all-gather.13.cloned.1.call-start = ((), (), s32[]{:S(2)}) async-start(), calls=%async_computation.23 | async-start | bytes 4718592 | tf_op jit(solution)/shard_map/all_gather | solution.py:105
  445.0 4.5 collective-permute-start
  451.9 172.0 %copy-start.13 = (f32[4,64,512]{2,1,0:T(8,128)}, f32[4,64,512]{2,1,0:T(8,128)S(1)}, u32[]{:S(2)}) copy-start(f32[4,64,512]{2,1,0:T(8,128)S(1)} %get-tuple-element.548) | copy-start | bytes 1572868
  457.3 147.4 %all-gather.9.cloned.1.call-start = ((), (), s32[]{:S(2)}) async-start(), calls=%async_computation.14 | async-start | bytes 4718592 | tf_op jit(solution)/shard_map/all_gather | solution.py:104
  462.0 289.5 %reduce-scatter.40.cloned.1.call-start = ((), (), s32[]{:S(2)}) async-start(), calls=%async_computation.24 | async-start | bytes 2359296
  685.5 136.1 %reduce-scatter.42.cloned.1.call-start = ((), (), s32[]{:S(2)}) async-start(), calls=%async_computation.25 | async-start | bytes 2359296
  700.0 395.0 %reduce-scatter.44.cloned.1.call-start = ((), (), s32[]{:S(2)}) async-start(), calls=%async_computation.26 | async-start | bytes 7077888
  837.0 5.6 collective-permute-start.1
  976.9 238.7 %reduce-scatter.46.cloned.1.call-start = ((), (), s32[]{:S(2)}) async-start(), calls=%async_computation.27 | async-start | bytes 7077888
  1013.6 256.0 %reduce-scatter.38.cloned.1.call-start = ((), (), s32[]{:S(2)}) async-start(), calls=%async_computation.21 | async-start | bytes 1966080 | tf_op jit(solution)/shard_map/reduce_scatter | solution.py:267
  1016.6 276.0 %reduce-scatter.32.cloned.1.call-start = ((), (), s32[]{:S(2)}) async-start(), calls=%async_computation.18 | async-start | bytes 5242880 | tf_op jit(solution)/shard_map/reduce_scatter | solution.py:261
  1023.0 292.6 %reduce-scatter.26.cloned.1.call-start = ((), (), s32[]{:S(2)}) async-start(), calls=%async_computation.15 | async-start | bytes 327680 | tf_op jit(solution)/shard_map/reduce_scatter | solution.py:270
  1233.5 109.6 %reduce-scatter.30.cloned.1.call-start = ((), (), s32[]{:S(2)}) async-start(), calls=%async_computation.17 | async-start | bytes 1310720 | tf_op jit(solution)/shard_map/reduce_scatter | solution.py:258
  1239.5 150.7 %reduce-scatter.36.cloned.1.call-start = ((), (), s32[]{:S(2)}) async-start(), calls=%async_computation.20 | async-start | bytes 5242880 | tf_op jit(solution)/shard_map/reduce_scatter | solution.py:264
  1246.5 184.3 %reduce-scatter.28.cloned.1.call-start = ((), (), s32[]{:S(2)}) async-start(), calls=%async_computation.16 | async-start | bytes 3932160 | tf_op jit(solution)/shard_map/reduce_scatter | solution.py:255
  1269.5 225.8 %reduce-scatter.50.cloned.1.call-start = ((), (), s32[]{:S(2)}) async-start(), calls=%async_computation.29 | async-start | bytes 442368
  1272.9 288.6 %reduce-scatter.34.cloned.1.call-start = ((), (), s32[]{:S(2)}) async-start(), calls=%async_computation.19 | async-start | bytes 1179648 | tf_op jit(solution)/shard_map/reduce_scatter | solution.py:281
  1292.6 332.9 %reduce-scatter.48.cloned.1.call-start = ((), (), s32[]{:S(2)}) async-start(), calls=%async_computation.28 | async-start | bytes 147456
  1317.4 415.2 %all-reduce.7.cloned.1.call-start = ((), (), s32[]{:S(2)}) async-start(), calls=%async_computation.30 | async-start | bytes 4194304
  1435.8 301.6 %copy-start.1 = (bf16[1536,512]{1,0:T(8,128)(2,1)S(1)}, bf16[1536,512]{1,0:T(8,128)(2,1)}, u32[]{:S(2)}) copy-start(bf16[1536,512]{1,0:T(8,128)(2,1)} %param.29) | copy-start | bytes 4718596
  (106 other events, 752.1 us)
Sparse Core Ops, SparseCore 0:
  24.4 179.1 all-gather.10
  205.8 174.6 all-gather.6
  457.5 73.5 all-gather.12
  533.0 71.6 all-gather.8
  685.7 65.8 reduce-scatter.39
  754.9 66.6 reduce-scatter.41
  977.1 117.8 reduce-scatter.43
  1098.5 117.0 reduce-scatter.45
  1218.2 27.3 reduce-scatter.37
  1248.1 44.4 reduce-scatter.31
  1295.6 19.9 reduce-scatter.25
  1318.2 24.8 reduce-scatter.29
  1345.7 44.5 reduce-scatter.35
  1392.8 37.9 reduce-scatter.27
  1433.9 61.4 reduce-scatter.49
  1498.6 62.8 reduce-scatter.33
  1565.6 59.8 reduce-scatter.47
  1630.3 102.2 all-reduce.6
where the time goes:
time: 1760 us; the launch traced here: 1740 us
  waiting for transfers between devices  1160 us (66%)
  local copies, waits for them, and re-layouts  256 us (15%)
  matrix products  192 us (11%)
  other arithmetic  68.9 us (4%)
  blocking collectives  40.1 us (2%)
    unnamed x25, waiting for transfers between devices  484 us
    all_gather x2, waiting for transfers between devices, block_forward(): lax.all_gather(keys, 'seq', axis=1, tiled=True)  231 us
    all_gather x2, waiting for transfers between devices, block_forward(): lax.all_gather(values, 'seq', axis=1, tiled=True)  230 us
    unnamed x199, local copies, waits for them, and re-layouts  189 us
    reduce_scatter x1, waiting for transfers between devices, body(): lax.psum_scatter(partial_sums[2].astype(jnp.bfloat16), 'seq', scatter_dim...  64.4 us
    reduce_scatter x1, waiting for transfers between devices, body(): lax.psum_scatter(stacked[5].astype(jnp.bfloat16), 'batch', scatter_dimens...  45.3 us
    psum x1, blocking collectives, body(): gain_totals = lax.psum((stacked[0], stacked[3]), ('seq', 'batch'))  40.1 us
    reduce_scatter x1, waiting for transfers between devices, body(): lax.psum_scatter(stacked[1].astype(jnp.bfloat16), 'batch', scatter_dimens...  36.9 us
  transfers between devices with their start and end apart: 20, of which 18 were waited for; matrix products, arithmetic and copies ran while one was open for 11% of the time, Pallas kernels for 0%

commit v1 on v0

v1 whole, which is shorter than its diff:
```python
import jax
import jax.numpy as jnp
from jax import lax
from jax.sharding import PartitionSpec as P

D = 512
H = 8
DH = 64

epsilon = 1e-05
masked_score = -1e30
AXES = ("seq", "batch")


def matmul(left, right):
    return jnp.dot(left, right, preferred_element_type=jnp.float32)


def left_grad(left, grad):
    return lax.dot_general(left, grad, (((0,), (0,)), ((), ())), preferred_element_type=jnp.float32)


def right_grad(grad, weight):
    return lax.dot_general(
        grad, weight, (((1,), (1,)), ((), ())), preferred_element_type=jnp.float32
    )


class Plan:
    def __init__(self, rows):
        self.S = lax.axis_size("seq")
        self.B = lax.axis_size("batch")
        self.R = rows
        self.P = self.S // rows
        self.s = lax.axis_index("seq")
        self.b = lax.axis_index("batch")
        line = self.s * 2 + self.b % 2
        self.h = line % self.P
        self.row = (line // self.P) % self.R
        self.part = self.s // self.P

    def pairs(self):
        for pair in range(self.B // 2):
            for core in range(2):
                for part in range(self.R):
                    for member in range(self.P):
                        yield pair, core, part, member

    def worker(self, pair, core, row, member):
        line = (core * self.R + row) * self.P + member
        return (line // 2) * self.B + 2 * pair + line % 2

    def home(self, pair, core, part, member):
        return (self.P * part + member) * self.B + 2 * pair + core

    def to_worker(self, held):
        got = []
        for step in range(self.R):
            perm = [
                (self.home(p, c, i, h), self.worker(p, c, (step + i) % self.R, h))
                for p, c, i, h in self.pairs()
            ]
            piece = lax.dynamic_index_in_dim(held, (step + self.part) % self.R, 0, keepdims=False)
            got.append(lax.ppermute(piece, AXES, perm))
        got = jnp.stack(got[::-1] + got[::-1])
        return lax.dynamic_slice_in_dim(got, (self.R - 1 - self.row) % self.R, self.R, 0)

    def to_home(self, made):
        got = []
        for step in range(self.R):
            perm = [
                (self.worker(p, c, (step + i) % self.R, h), self.home(p, c, i, h))
                for p, c, i, h in self.pairs()
            ]
            piece = lax.dynamic_index_in_dim(made, (self.row - step) % self.R, 0, keepdims=False)
            got.append(lax.ppermute(piece, AXES, perm))
        got = jnp.stack(got + got)
        return lax.dynamic_slice_in_dim(got, (self.R - self.part) % self.R, self.R, 0)

    def shift(self, value, by):
        perm = []
        for pair, core, row, member in self.pairs():
            perm.append((
                self.worker(pair, core, row, member),
                self.worker(pair, core, row, (member + by) % self.P),
            ))
        return lax.ppermute(value, AXES, perm)

    def others(self, value):
        return [self.shift(value, by) for by in range(1, self.P)]

    def swap(self, value, axis, bit):
        count = lax.axis_size(axis)
        return lax.ppermute(value, axis, [(n, n ^ bit) for n in range(count)])

    def bits(self, axis):
        count = lax.axis_size(axis)
        return [1 << n for n in range(count.bit_length() - 1)]

    def reduce_scatter(self, blocks, order):
        nb, ns = len(self.bits("batch")), len(self.bits("seq"))
        rest = blocks.shape[2:]
        value = blocks.astype(jnp.bfloat16).reshape((2,) * (nb + ns) + rest)
        dims = [("batch", 1 << (nb - 1 - n)) for n in range(nb)]
        dims += [("seq", 1 << (ns - 1 - n)) for n in range(ns)]
        for axis, bit in order:
            where = dims.index((axis, bit))
            dims.pop(where)
            index = self.b if axis == "batch" else self.s
            mine = (index // bit) % 2
            keep = lax.dynamic_index_in_dim(value, mine, where, keepdims=False)
            send = lax.dynamic_index_in_dim(value, 1 - mine, where, keepdims=False)
            total = keep.astype(jnp.float32) + self.swap(send, axis, bit).astype(jnp.float32)
            value = total if not dims else total.astype(jnp.bfloat16)
        return value

    def all_sum(self, value):
        for axis in ("batch", "seq"):
            for bit in self.bits(axis):
                value = value + self.swap(value, axis, bit)
        return value


def normalize(inputs, gain):
    centred = inputs - jnp.mean(inputs, -1, keepdims=True)
    inverse = lax.rsqrt(jnp.mean(centred * centred, -1, keepdims=True) + epsilon)
    normed = centred * inverse
    return ((normed * gain).astype(jnp.bfloat16), normed, inverse)


def normalize_back(grad, normed, inverse, gain):
    scaled = grad * gain
    result = inverse * (
        scaled
        - jnp.mean(scaled, -1, keepdims=True)
        - normed * jnp.mean(scaled * normed, -1, keepdims=True)
    )
    return (result, jnp.sum(grad * normed, axis=0, keepdims=True))


def angles(positions):
    half_size = DH // 2
    freqs = 10000.0 ** (-jnp.arange(half_size).astype(jnp.float32) / half_size)
    phase = positions.astype(jnp.float32)[:, None] * freqs[None, :]
    cosine, sine = jnp.cos(phase), jnp.sin(phase)
    return (jnp.concatenate([cosine] * 4, 1), jnp.concatenate([-sine, sine] * 2, 1))


def rotate(inputs, cosine, sine):
    count = inputs.shape[1] // 128
    lanes = lax.broadcasted_iota(jnp.int32, inputs.shape, 1)
    other = jnp.where(lanes % 64 < 32, jnp.roll(inputs, -32, 1), jnp.roll(inputs, 32, 1))
    return inputs * jnp.concatenate([cosine] * count, 1) + other * jnp.concatenate([sine] * count, 1)


def pre_attention(inputs, gain, w_qkv, cosine, sine):
    low, unused, unused2 = normalize(inputs, gain)
    joined = matmul(low, w_qkv)
    queries = (rotate(joined[:, :D], cosine, sine) * DH ** (-0.5)).astype(jnp.bfloat16)
    keys = rotate(joined[:, D : 2 * D], cosine, sine).astype(jnp.bfloat16)
    values = joined[:, 2 * D :].astype(jnp.bfloat16)
    return (queries, jnp.stack([keys, values]))


def visible(member, members, span):
    rows = lax.broadcasted_iota(jnp.int32, (span, members * span), 0)
    columns = lax.broadcasted_iota(jnp.int32, (span, members * span), 1)
    other = (member - columns // span + members) % members
    own = columns <= rows
    return jnp.where(columns < span, own, other < member)


def gathered(own, others, parts, index):
    pieces = [value[index].reshape(parts, -1, D) for value in [own] + others]
    return jnp.stack(pieces, 1)


def heads(value):
    return value.reshape(-1, H, DH)


def attention(queries, own, others, parts, seen):
    span = queries.shape[0] // parts
    keys, values = gathered(own, others, parts, 0), gathered(own, others, parts, 1)
    width = keys.shape[1] * span
    mixed, logsum = [], []
    for part in range(parts):
        query = heads(queries[part * span : (part + 1) * span])
        key = heads(keys[: part + 1].reshape(-1, D))
        value = heads(values[: part + 1].reshape(-1, D))
        scores = jnp.einsum("qhd,khd->hqk", query, key, preferred_element_type=jnp.float32)
        last = jnp.where(seen[None], scores[..., part * width :], masked_score)
        scores = jnp.concatenate([scores[..., : part * width], last], -1)
        highest = jnp.max(scores, -1, keepdims=True)
        expon = jnp.exp(scores - highest)
        totals = jnp.sum(expon, -1, keepdims=True)
        probs = (expon / totals).astype(jnp.bfloat16)
        mixed.append(
            jnp.einsum("hqk,khd->qhd", probs, value, preferred_element_type=jnp.float32).reshape(span, D)
        )
        logsum.append((highest + jnp.log(totals))[..., 0])
    return (jnp.concatenate(mixed).astype(jnp.bfloat16), logsum)


def attention_back(queries, own, others, parts, seen, mixed, logsum, grad_mixed):
    span = queries.shape[0] // parts
    keys, values = gathered(own, others, parts, 0), gathered(own, others, parts, 1)
    members = keys.shape[1]
    width = members * span
    grad_queries = []
    grad_keys = jnp.zeros((parts * width, H, DH), jnp.float32)
    grad_values = jnp.zeros((parts * width, H, DH), jnp.float32)
    for part in range(parts):
        rows = slice(part * span, (part + 1) * span)
        query, grad = heads(queries[rows]), heads(grad_mixed[rows])
        key = heads(keys[: part + 1].reshape(-1, D))
        value = heads(values[: part + 1].reshape(-1, D))
        scores = jnp.einsum("qhd,khd->hqk", query, key, preferred_element_type=jnp.float32)
        last = jnp.where(seen[None], scores[..., part * width :], masked_score)
        scores = jnp.concatenate([scores[..., : part * width], last], -1)
        probs = jnp.exp(scores - logsum[part][..., None])
        grad_probs = jnp.einsum("qhd,khd->hqk", grad, value, preferred_element_type=jnp.float32)
        delta = jnp.sum(
            grad.astype(jnp.float32) * heads(mixed[rows]).astype(jnp.float32), -1
        ).T[..., None]
        grad_scores = (probs * (grad_probs - delta)).astype(jnp.bfloat16)
        grad_queries.append(
            jnp.einsum("hqk,khd->qhd", grad_scores, key, preferred_element_type=jnp.float32).reshape(span, D)
        )
        seen_keys = (part + 1) * width
        grad_keys = grad_keys.at[:seen_keys].add(
            jnp.einsum("hqk,qhd->khd", grad_scores, query, preferred_element_type=jnp.float32)
        )
        grad_values = grad_values.at[:seen_keys].add(
            jnp.einsum("hqk,qhd->khd", probs.astype(jnp.bfloat16), grad, preferred_element_type=jnp.float32)
        )
    both = jnp.stack([grad_keys, grad_values]).astype(jnp.bfloat16)
    both = both.reshape(2, parts, members, span, D)
    pieces = [both[:, :, member].reshape(2, parts * span, D) for member in range(members)]
    return (jnp.concatenate(grad_queries).astype(jnp.bfloat16), pieces)


def post_attention(inputs, mixed, weights):
    gain_attn, w_qkv, w_out, gain_ffn, w_up, w_down = weights
    middle = inputs + matmul(mixed, w_out)
    low, unused, unused2 = normalize(middle, gain_ffn)
    hidden = matmul(low, w_up)
    active = jax.nn.gelu(hidden, approximate=True).astype(jnp.bfloat16)
    output = middle + matmul(active, w_down)
    return (output.astype(jnp.bfloat16), middle, hidden.astype(jnp.bfloat16))


def gelu_both(hidden):
    scale = 0.7978845608028654
    square = hidden * hidden
    tanh = jnp.tanh(scale * hidden * (1.0 + 0.044715 * square))
    active = 0.5 * hidden * (1.0 + tanh)
    slope = 0.5 * (1.0 + tanh) + 0.5 * hidden * (1.0 - tanh * tanh) * scale * (
        1.0 + 3.0 * 0.044715 * square
    )
    return (active, slope)


def post_attention_back(grad_out, mixed, middle, hidden, weights):
    gain_attn, w_qkv, w_out, gain_ffn, w_up, w_down = weights
    low, normed, inverse = normalize(middle, gain_ffn)
    grad_low = grad_out.astype(jnp.bfloat16)
    active, slope = gelu_both(hidden.astype(jnp.float32))
    grad_down = left_grad(grad_low, active.astype(jnp.bfloat16))
    grad_hidden = (right_grad(grad_low, w_down) * slope).astype(jnp.bfloat16)
    grad_up = left_grad(low, grad_hidden)
    grad_norm, grad_gain = normalize_back(right_grad(grad_hidden, w_up), normed, inverse, gain_ffn)
    grad_middle = grad_out + grad_norm
    grad_branch = grad_middle.astype(jnp.bfloat16)
    grad_w_out = left_grad(grad_branch, mixed)
    grad_mixed = right_grad(grad_branch, w_out).astype(jnp.bfloat16)
    return (grad_middle, grad_mixed, grad_down, grad_up, grad_w_out, grad_gain)


def pre_attention_back(inputs, grad_queries, grad_own, grad_others, grad_middle, cosine, sine, weights):
    gain_attn, w_qkv, w_out, gain_ffn, w_up, w_down = weights
    low, normed, inverse = normalize(inputs, gain_attn)
    total = sum([member.astype(jnp.float32) for member in grad_others], grad_own.astype(jnp.float32))
    grad_joined = jnp.concatenate(
        [
            rotate(grad_queries.astype(jnp.float32) * DH ** (-0.5), cosine, -sine),
            rotate(total[0], cosine, -sine),
            total[1],
        ],
        1,
    ).astype(jnp.bfloat16)
    grad_w_qkv = left_grad(grad_joined, low)
    grad_norm, grad_gain = normalize_back(right_grad(grad_joined, w_qkv), normed, inverse, gain_attn)
    return (grad_middle + grad_norm, grad_w_qkv, grad_gain)


def blocked(value, outer, inner, swapped):
    rows, columns = value.shape
    if swapped:
        return value.reshape(inner, rows // inner, outer, columns // outer).transpose(2, 0, 1, 3)
    return value.reshape(outer, rows // outer, inner, columns // inner).transpose(0, 2, 1, 3)


def body(
    tokens, loss_mask, cotangent, embed, gain_attn, w_qkv, w_out, gain_ffn, w_up, w_down, w_pool
):
    plan = Plan(tokens.shape[0])
    rows, span = tokens.shape
    short = loss_mask.shape[1]
    members = plan.P
    vocab = embed.shape[0]
    params = (gain_attn, w_qkv, w_out, gain_ffn, w_up, w_down)
    first_weights = tuple((member[0] for member in params))
    second_weights = tuple((member[1] for member in params))

    my_tokens = plan.to_worker(tokens).reshape(rows * span)
    start_grad = plan.to_worker(cotangent * loss_mask.astype(jnp.bfloat16)[..., None]).reshape(-1, D)

    def places(length):
        block = jnp.arange(rows, dtype=jnp.int32)[:, None] * members + plan.h
        return (block * length + jnp.arange(length, dtype=jnp.int32)[None]).reshape(-1)

    first_angles, second_angles = angles(places(span)), angles(places(short))
    first_seen = visible(plan.h, members, span)
    second_seen = visible(plan.h, members, short)

    onehot = (my_tokens[:, None] == jnp.arange(vocab, dtype=jnp.int32)).astype(jnp.bfloat16)
    inputs = matmul(onehot, embed)

    def forward(value, angle, seen, weights):
        queries, own = pre_attention(value, weights[0], weights[1], *angle)
        others = plan.others(own)
        mixed, logsum = attention(queries, own, others, rows, seen)
        output, middle, hidden = post_attention(value, mixed, weights)
        return (output, (queries, own, others, mixed, logsum, middle, hidden))

    def backward(value, grad_out, kept, angle, seen, weights):
        queries, own, others, mixed, logsum, middle, hidden = kept
        grad_middle, grad_mixed, grad_down, grad_up, grad_w_out, grad_gain_ffn = post_attention_back(
            grad_out, mixed, middle, hidden, weights
        )
        grad_queries, pieces = attention_back(
            queries, own, others, rows, seen, mixed, logsum, grad_mixed
        )
        grad_others = [plan.shift(pieces[by], -by) for by in range(1, members)]
        grad_inputs, grad_qkv, grad_gain_attn = pre_attention_back(
            value, grad_queries, pieces[0], grad_others, grad_middle, *angle, weights
        )
        return (grad_inputs, (grad_qkv, grad_w_out, grad_up, grad_down), grad_gain_attn, grad_gain_ffn)

    first_low, first_kept = forward(inputs, first_angles, first_seen, first_weights)
    first_blocks = first_low.reshape(rows, span, D)
    full_out = plan.to_home(first_blocks)

    edge = plan.shift(first_blocks[:, span - 2 :], 1)
    late = jnp.concatenate([jnp.zeros_like(edge[:1]), edge[:-1]], 0)
    edge = jnp.where(plan.h == 0, late, edge)
    shifted = jnp.concatenate([edge, first_blocks[:, : span - 2]], 1)
    grouped = shifted.reshape(rows * short, 3 * D)
    pooled = matmul(grouped, w_pool)

    second_low, second_kept = forward(pooled, second_angles, second_seen, second_weights)
    short_out = plan.to_home(second_low.reshape(rows, short, D))

    grad_pooled, second_grads, gain_attn_1, gain_ffn_1 = backward(
        pooled, start_grad.astype(jnp.float32), second_kept, second_angles, second_seen, second_weights
    )
    grad_pooled_low = grad_pooled.astype(jnp.bfloat16)
    grad_pool = left_grad(grad_pooled_low, grouped)
    grad_shifted = right_grad(grad_pooled_low, w_pool).reshape(rows, span, D)
    carried = plan.shift(grad_shifted[:, :2], -1)
    early = jnp.concatenate([carried[1:], jnp.zeros_like(carried[:1])], 0)
    carried = jnp.where(plan.h == members - 1, early, carried)
    grad_first = jnp.concatenate([grad_shifted[:, 2:], carried], 1).reshape(rows * span, D)

    grad_inputs, first_grads, gain_attn_0, gain_ffn_0 = backward(
        inputs, grad_first, first_kept, first_angles, first_seen, first_weights
    )
    input_grad = plan.to_home(grad_inputs.astype(jnp.bfloat16).reshape(rows, span, D))
    grad_embed = left_grad(grad_inputs.astype(jnp.bfloat16), onehot)

    order = [("batch", bit) for bit in plan.bits("batch")] + [("seq", bit) for bit in plan.bits("seq")]

    def reduced(value, swapped):
        total = plan.reduce_scatter(blocked(value, plan.B, plan.S, swapped), order)
        return total.T if swapped else total

    def stacked(number, swapped):
        return jnp.stack([reduced(first_grads[number], swapped), reduced(second_grads[number], swapped)])

    gains = plan.all_sum(jnp.concatenate([gain_attn_0, gain_attn_1, gain_ffn_0, gain_ffn_1]))
    return (
        full_out,
        short_out,
        input_grad.astype(jnp.float32),
        reduced(grad_embed, True),
        gains[:2],
        stacked(0, True),
        stacked(1, True),
        gains[2:],
        stacked(2, False),
        stacked(3, True),
        reduced(grad_pool, True),
    )


def solution(mesh):
    in_specs = (
        P("batch", "seq"),
        P("batch", "seq"),
        P("batch", "seq", None),
        P(),
        P(),
        P(),
        P(),
        P(),
        P(),
        P(),
        P(),
    )
    out_specs = (
        P("batch", "seq", None),
        P("batch", "seq", None),
        P("batch", "seq", None),
        P("batch", "seq"),
        P(),
        P(None, "batch", "seq"),
        P(None, "batch", "seq"),
        P(),
        P(None, "batch", "seq"),
        P(None, "batch", "seq"),
        P("batch", "seq"),
    )
    return jax.shard_map(body, mesh=mesh, in_specs=in_specs, out_specs=out_specs, check_vma=False)
```

time: 1760 us -> 772 us (0.44)
  waiting for transfers between devices: 1160 us -> 112 us
  starting transfers between devices: 5.63 us -> 125 us
  matrix products: 192 us -> 128 us
  other arithmetic: 68.9 us -> 121 us
  blocking collectives: 40.1 us -> 0 us
    unnamed x25 -> x0, waiting for transfers between devices: 484 us -> none
    all_gather x4 -> x0, waiting for transfers between devices: 460 us -> none  [the longest x2 231 us: block_forward(): lax.all_gather(keys, 'seq', axis=1, tiled=True)]
    reduce_scatter x7 -> x0, waiting for transfers between devices: 215 us -> none  [the longest x1 64.4 us: body(): lax.psum_scatter(partial_sums[2].astype(jnp.bfloat16), 'seq', scatter_dim...]
    unnamed x199 -> x523, local copies, waits for them, and re-layouts: 189 us -> 53.7 us
    ppermute x2 -> x81, starting transfers between devices: 4.15 us -> 125 us  [the longest x55 56.9 us: swap(): return lax.ppermute(value, axis, [(n, n ^ bit) for n in range(count)])]
    ppermute x2 -> x81, waiting for transfers between devices: 4.06 us -> 112 us  [the longest x55 107 us: swap(): return lax.ppermute(value, axis, [(n, n ^ bit) for n in range(count)])]
    another operation x3 -> x43, local copies, waits for them, and re-layouts: 8.84 us -> 115 us  [the longest x24 62.3 us: heads(): return value.reshape(-1, H, DH)]
    dot_general x61 -> x48, matrix products: 141 us -> 75.1 us  [the longest x8 21.9 us: attention_back(): jnp.einsum('qhd,khd->hqk', grad, value, preferred_element_type=jnp.float32)]
  transfers between devices with their start and end apart: 20 -> 81, of which waited for: 18 -> 36; matrix products, arithmetic and copies ran while one was open for 11% -> 36% of each run, Pallas kernels for 0% -> 0%
where the time goes in v1:
time: 772 us; the launch traced here: 760 us
  local copies, waits for them, and re-layouts  270 us (35%)
  matrix products  128 us (17%)
  starting transfers between devices  125 us (16%)
  other arithmetic  121 us (16%)
  waiting for transfers between devices  112 us (15%)
    ppermute x55, waiting for transfers between devices, swap(): return lax.ppermute(value, axis, [(n, n ^ bit) for n in range(count)])  107 us
    another operation x24, local copies, waits for them, and re-layouts, heads(): return value.reshape(-1, H, DH)  62.3 us
    ppermute x55, starting transfers between devices, swap(): return lax.ppermute(value, axis, [(n, n ^ bit) for n in range(count)])  56.9 us
    unnamed x523, local copies, waits for them, and re-layouts  53.7 us
    another operation x16, other arithmetic, gathered(): return jnp.stack(pieces, 1)  40.7 us
    ppermute x12, starting transfers between devices, to_home(): got.append(lax.ppermute(piece, AXES, perm))  39 us
    another operation x8, local copies, waits for them, and re-layouts, attention_back(): both = jnp.stack([grad_keys, grad_values]).astype(jnp.bfloat16)  30.5 us
    ppermute x8, starting transfers between devices, to_worker(): got.append(lax.ppermute(piece, AXES, perm))  26.1 us
  transfers between devices with their start and end apart: 81, of which 36 were waited for; matrix products, arithmetic and copies ran while one was open for 36% of the time, Pallas kernels for 0%

profile of v1, /device:TPU:0, one launch (start us, length us, event | category | flops | bytes accessed | tf_op | source)
XLA Modules:
  0.0 760.0 jit_solution(15042916851959513538)
XLA Ops:
  7.1 6.0 collective-permute-start
  38.8 5.2 collective-permute-start.17
  44.1 5.9 collective-permute-start.15
  99.2 6.0 pad_maximum_fusion.45
  105.2 5.9 copy.180
  117.9 5.1 slice_maximum_fusion
  123.0 6.0 pad_maximum_fusion.46
  134.9 5.7 reshape_reshape.70
  147.7 6.0 reshape_reshape.71
  169.7 6.7 fusion.354
  210.3 5.2 collective-permute-start.6
  218.5 4.7 copy.275
  491.2 4.9 multiply_convert_fusion.1
  498.1 5.5 multiply_convert_fusion
  531.7 4.7 copy.234
  539.2 6.2 copy.235
  578.5 9.8 %collective-permute-done.62 = bf16[2,2,2,128,256]{4,3,0,1,2:T(8,128)(2,1)S(1)} collective-permute-done((bf16[2,2,2,128,256]{4,3,0,1,2:T(8,128)(2,1)S(1)}, bf16[2,2,2,128,256]{4,3,0,1,2:T(8,128)(2,1)S(1)}, u32[]{:S(2)}, u32[]{:S(2)}) %collective-permute-start.62) | collective-permute-done | bytes 524320 | tf_op jit(solution)/shard_map/ppermute | solution.py:94
  590.0 9.6 %collective-permute-done.72 = bf16[2,2,2,64,512]{4,3,0,1,2:T(8,128)(2,1)S(1)} collective-permute-done((bf16[2,2,2,64,512]{4,3,0,1,2:T(8,128)(2,1)S(1)}, bf16[2,2,2,64,512]{4,3,0,1,2:T(8,128)(2,1)S(1)}, u32[]{:S(2)}, u32[]{:S(2)}) %collective-permute-start.72) | collective-permute-done | bytes 524320 | tf_op jit(solution)/shard_map/ppermute | solution.py:94
  609.6 6.8 collective-permute-done.77
  620.4 5.5 collective-permute-done.43
  692.1 12.5 %collective-permute-start.23 = (bf16[192,512]{1,0:T(8,128)(2,1)S(1)}, bf16[192,512]{1,0:T(8,128)(2,1)S(1)}, u32[]{:S(2)}, u32[]{:S(2)}) collective-permute-start(bf16[192,512]{1,0:T(8,128)(2,1)S(1)} %get-tuple-element.339), channel_id=1, source_target_pairs={{4,0},{5,4},{8,8},{9,12},{12,16},{13,20},{0,24},{1,28},{20,1},{21,... | collective-permute-start | bytes 589832 | tf_op jit(solution)/shard_map/ppermute | solution.py:76
  704.7 4.9 collective-permute-done.23
  737.8 4.9 collective-permute-done.37
  743.3 5.4 collective-permute-done.38
  (1112 shorter events, 605.5 us)
Async XLA Ops:
  2.2 36.6 %collective-permute-start.1 = (s32[192]{0:T(256)}, s32[192]{0:T(256)}, u32[]{:S(2)}, u32[]{:S(2)}) collective-permute-start(s32[192]{0:T(256)} %bitcast.2), channel_id=1, source_target_pairs={{0,8},{4,9},{8,12},{12,13},{16,0},{20,1},{24,4},{28,5},{1,24},{5,2... | collective-permute-start | bytes 2312 | tf_op jit(solution)/shard_map/ppermute | solution.py:64
  5.2 38.8 %collective-permute-start.3 = (s32[192]{0:T(256)}, s32[192]{0:T(256)}, u32[]{:S(2)}, u32[]{:S(2)}) collective-permute-start(s32[192]{0:T(256)} %bitcast.6), channel_id=1, source_target_pairs={{0,0},{4,1},{8,4},{12,5},{16,8},{20,9},{24,12},{28,13},{1,16},{5,1... | collective-permute-start | bytes 2312 | tf_op jit(solution)/shard_map/ppermute | solution.py:64
  7.1 37.0 %collective-permute-start = (s32[192]{0:T(256)}, s32[192]{0:T(256)}, u32[]{:S(2)}, u32[]{:S(2)}) collective-permute-start(s32[192]{0:T(256)} %bitcast), channel_id=1, source_target_pairs={{0,12},{4,13},{8,0},{12,1},{16,4},{20,5},{24,8},{28,9},{1,28},{5,2... | collective-permute-start | bytes 2312 | tf_op jit(solution)/shard_map/ppermute | solution.py:64
  13.1 36.8 %collective-permute-start.2 = (s32[192]{0:T(256)}, s32[192]{0:T(256)}, u32[]{:S(2)}, u32[]{:S(2)}) collective-permute-start(s32[192]{0:T(256)} %bitcast.4), channel_id=1, source_target_pairs={{0,4},{4,5},{8,8},{12,9},{16,12},{20,13},{24,0},{28,1},{1,20},{5,2... | collective-permute-start | bytes 2312 | tf_op jit(solution)/shard_map/ppermute | solution.py:64
  17.5 59.5 %collective-permute-start.18 = (bf16[64,512]{1,0:T(8,128)(2,1)}, bf16[64,512]{1,0:T(8,128)(2,1)}, u32[]{:S(2)}, u32[]{:S(2)}) collective-permute-start(bf16[64,512]{1,0:T(8,128)(2,1)} %get-tuple-element.375), channel_id=1, source_target_pairs={{0,0},{4,1},{8,4},{12,5},{16,8},{20,9},{24,12},{28,13},{1,16},{5,1... | collective-permute-start | bytes 196616 | tf_op jit(solution)/shard_map/ppermute | solution.py:64
  38.8 37.4 %collective-permute-start.17 = (bf16[64,512]{1,0:T(8,128)(2,1)}, bf16[64,512]{1,0:T(8,128)(2,1)}, u32[]{:S(2)}, u32[]{:S(2)}) collective-permute-start(bf16[64,512]{1,0:T(8,128)(2,1)} %get-tuple-element.376), channel_id=1, source_target_pairs={{0,4},{4,5},{8,8},{12,9},{16,12},{20,13},{24,0},{28,1},{1,20},{5,2... | collective-permute-start | bytes 196616 | tf_op jit(solution)/shard_map/ppermute | solution.py:64
  208.2 38.9 %collective-permute-start.8 = (bf16[192,512]{1,0:T(8,128)(2,1)}, bf16[192,512]{1,0:T(8,128)(2,1)}, u32[]{:S(2)}, u32[]{:S(2)}) collective-permute-start(bf16[192,512]{1,0:T(8,128)(2,1)} %get-tuple-element.347), channel_id=1, source_target_pairs={{12,0},{13,4},{0,8},{1,12},{4,16},{5,20},{8,24},{9,28},{28,1},{29,... | collective-permute-start | bytes 589832 | tf_op jit(solution)/shard_map/ppermute | solution.py:76
  210.1 36.1 %collective-permute-start.7 = (bf16[192,512]{1,0:T(8,128)(2,1)}, bf16[192,512]{1,0:T(8,128)(2,1)}, u32[]{:S(2)}, u32[]{:S(2)}) collective-permute-start(bf16[192,512]{1,0:T(8,128)(2,1)} %get-tuple-element.348), channel_id=1, source_target_pairs={{8,0},{9,4},{12,8},{13,12},{0,16},{1,20},{4,24},{5,28},{24,1},{25,... | collective-permute-start | bytes 589832 | tf_op jit(solution)/shard_map/ppermute | solution.py:76
  355.9 55.8 %collective-permute-start.14 = (bf16[64,512]{1,0:T(8,128)(2,1)}, bf16[64,512]{1,0:T(8,128)(2,1)}, u32[]{:S(2)}, u32[]{:S(2)}) collective-permute-start(bf16[64,512]{1,0:T(8,128)(2,1)} %get-tuple-element.379), channel_id=1, source_target_pairs={{12,0},{13,4},{0,8},{1,12},{4,16},{5,20},{8,24},{9,28},{28,1},{29,... | collective-permute-start | bytes 196616 | tf_op jit(solution)/shard_map/ppermute | solution.py:76
  357.9 52.6 %collective-permute-start.13 = (bf16[64,512]{1,0:T(8,128)(2,1)}, bf16[64,512]{1,0:T(8,128)(2,1)}, u32[]{:S(2)}, u32[]{:S(2)}) collective-permute-start(bf16[64,512]{1,0:T(8,128)(2,1)} %get-tuple-element.380), channel_id=1, source_target_pairs={{8,0},{9,4},{12,8},{13,12},{0,16},{1,20},{4,24},{5,28},{24,1},{25,... | collective-permute-start | bytes 196616 | tf_op jit(solution)/shard_map/ppermute | solution.py:76
  360.4 49.1 %collective-permute-start.12 = (bf16[64,512]{1,0:T(8,128)(2,1)}, bf16[64,512]{1,0:T(8,128)(2,1)}, u32[]{:S(2)}, u32[]{:S(2)}) collective-permute-start(bf16[64,512]{1,0:T(8,128)(2,1)} %get-tuple-element.381), channel_id=1, source_target_pairs={{4,0},{5,4},{8,8},{9,12},{12,16},{13,20},{0,24},{1,28},{20,1},{21,... | collective-permute-start | bytes 196616 | tf_op jit(solution)/shard_map/ppermute | solution.py:76
  364.1 44.3 %collective-permute-start.11 = (bf16[64,512]{1,0:T(8,128)(2,1)}, bf16[64,512]{1,0:T(8,128)(2,1)}, u32[]{:S(2)}, u32[]{:S(2)}) collective-permute-start(bf16[64,512]{1,0:T(8,128)(2,1)} %get-tuple-element.382), channel_id=1, source_target_pairs={{0,0},{1,4},{4,8},{5,12},{8,16},{9,20},{12,24},{13,28},{16,1},{17,... | collective-permute-start | bytes 196616 | tf_op jit(solution)/shard_map/ppermute | solution.py:76
  409.5 156.6 %collective-permute-start.61 = (bf16[2,2,2,2,128,256]{5,4,1,2,3,0:T(8,128)(2,1)}, bf16[2,2,2,2,128,256]{5,4,1,2,3,0:T(8,128)(2,1)}, u32[]{:S(2)}, u32[]{:S(2)}) collective-permute-start(bf16[2,2,2,2,128,256]{5,4,1,2,3,0:T(8,128)(2,1)} %bitcast.885), channel_id=1, source_target_pairs={{0,1},{1,0},{2,3},{3,2},{4,5},{5,4},{6,7},{7,6},{8,9},{9,8},{10,11... | collective-permute-start | bytes 3145736 | tf_op jit(solution)/shard_map/ppermute | solution.py:94
  410.5 157.7 %collective-permute-start.71 = (bf16[2,2,2,2,64,512]{5,4,1,2,3,0:T(8,128)(2,1)}, bf16[2,2,2,2,64,512]{5,4,1,2,3,0:T(8,128)(2,1)}, u32[]{:S(2)}, u32[]{:S(2)}) collective-permute-start(bf16[2,2,2,2,64,512]{5,4,1,2,3,0:T(8,128)(2,1)} %bitcast.883), channel_id=1, source_target_pairs={{0,1},{1,0},{2,3},{3,2},{4,5},{5,4},{6,7},{7,6},{8,9},{9,8},{10,11... | collective-permute-start | bytes 3145736 | tf_op jit(solution)/shard_map/ppermute | solution.py:94
  458.5 115.1 %collective-permute-start.41 = (bf16[2,2,2,2,192,128]{5,4,1,2,3,0:T(8,128)(2,1)}, bf16[2,2,2,2,192,128]{5,4,1,2,3,0:T(8,128)(2,1)}, u32[]{:S(2)}, u32[]{:S(2)}) collective-permute-start(bf16[2,2,2,2,192,128]{5,4,1,2,3,0:T(8,128)(2,1)} %bitcast.887), channel_id=1, source_target_pairs={{0,1},{1,0},{2,3},{3,2},{4,5},{5,4},{6,7},{7,6},{8,9},{9,8},{10,11... | collective-permute-start | bytes 2359304 | tf_op jit(solution)/shard_map/ppermute | solution.py:94
  458.8 117.6 %collective-permute-start.76 = (bf16[2,2,2,2,64,384]{5,4,1,2,3,0:T(8,128)(2,1)}, bf16[2,2,2,2,64,384]{5,4,1,2,3,0:T(8,128)(2,1)}, u32[]{:S(2)}, u32[]{:S(2)}) collective-permute-start(bf16[2,2,2,2,64,384]{5,4,1,2,3,0:T(8,128)(2,1)} %bitcast.886), channel_id=1, source_target_pairs={{0,1},{1,0},{2,3},{3,2},{4,5},{5,4},{6,7},{7,6},{8,9},{9,8},{10,11... | collective-permute-start | bytes 2359304 | tf_op jit(solution)/shard_map/ppermute | solution.py:94
  514.2 36.4 %collective-permute-start.46 = (bf16[2,2,2,2,64,128]{5,4,3,2,1,0:T(8,128)(2,1)}, bf16[2,2,2,2,64,128]{5,4,3,2,1,0:T(8,128)(2,1)}, u32[]{:S(2)}, u32[]{:S(2)}) collective-permute-start(bf16[2,2,2,2,64,128]{5,4,3,2,1,0:T(8,128)(2,1)} %dynamic-slice_bitcast_fusion.13), channel_id=1, source_target_pairs={{0,1},{1,0},{2,3},{3,2},{4,5},{5,4},{6,7},{7,6},{8,9},{9,8},{10,11... | collective-permute-start | bytes 786440 | tf_op jit(solution)/shard_map/ppermute | solution.py:94
  566.1 36.8 %collective-permute-start.56 = (bf16[2,2,2,2,128,256]{5,4,3,2,1,0:T(8,128)(2,1)S(1)}, bf16[2,2,2,2,128,256]{5,4,3,2,1,0:T(8,128)(2,1)S(1)}, u32[]{:S(2)}, u32[]{:S(2)}) collective-permute-start(bf16[2,2,2,2,128,256]{5,4,3,2,1,0:T(8,128)(2,1)S(1)} %dynamic-slice_bitcast_fusion), channel_id=1, source_target_pairs={{0,1},{1,0},{2,3},{3,2},{4,5},{5,4},{6,7},{7,6},{8,9},{9,8},{10,11... | collective-permute-start | bytes 3145736 | tf_op jit(solution)/shard_map/ppermute | solution.py:94
  572.9 83.3 %collective-permute-start.21 = (bf16[2,768,512]{2,1,0:T(8,128)(2,1)S(1)}, bf16[2,768,512]{2,1,0:T(8,128)(2,1)S(1)}, u32[]{:S(2)}, u32[]{:S(2)}) collective-permute-start(bf16[2,768,512]{2,1,0:T(8,128)(2,1)S(1)} %bitcast.973), channel_id=1, source_target_pairs={{0,1},{1,0},{4,5},{5,4},{8,9},{9,8},{12,13},{13,12},{16,17},{17,16... | collective-permute-start | bytes 4718600 | tf_op jit(solution)/shard_map/ppermute | solution.py:87
  608.0 44.3 %collective-permute-start.67 = (bf16[2,2,2,64,512]{4,3,0,1,2:T(8,128)(2,1)S(1)}, bf16[2,2,2,64,512]{4,3,0,1,2:T(8,128)(2,1)S(1)}, u32[]{:S(2)}, u32[]{:S(2)}) collective-permute-start(bf16[2,2,2,64,512]{4,3,0,1,2:T(8,128)(2,1)S(1)} %dynamic-slice_bitcast_fusion.3), channel_id=1, source_target_pairs={{0,2},{1,3},{2,0},{3,1},{4,6},{5,7},{6,4},{7,5},{8,10},{9,11},{10,... | collective-permute-start | bytes 1572872 | tf_op jit(solution)/shard_map/ppermute | solution.py:94
  616.4 38.6 %collective-permute-start.57 = (bf16[2,2,2,128,256]{4,3,2,1,0:T(8,128)(2,1)S(1)}, bf16[2,2,2,128,256]{4,3,2,1,0:T(8,128)(2,1)S(1)}, u32[]{:S(2)}, u32[]{:S(2)}) collective-permute-start(bf16[2,2,2,128,256]{4,3,2,1,0:T(8,128)(2,1)S(1)} %dynamic-slice_bitcast_fusion.5), channel_id=1, source_target_pairs={{0,2},{1,3},{2,0},{3,1},{4,6},{5,7},{6,4},{7,5},{8,10},{9,11},{10,... | collective-permute-start | bytes 1572872 | tf_op jit(solution)/shard_map/ppermute | solution.py:94
  653.2 71.8 %collective-permute-start.68 = (bf16[2,2,64,512]{3,2,0,1:T(8,128)(2,1)}, bf16[2,2,64,512]{3,2,0,1:T(8,128)(2,1)}, u32[]{:S(2)}, u32[]{:S(2)}) collective-permute-start(bf16[2,2,64,512]{3,2,0,1:T(8,128)(2,1)} %dynamic-slice_bitcast_fusion.10), channel_id=1, source_target_pairs={{0,4},{4,0},{8,12},{12,8},{16,20},{20,16},{24,28},{28,24},{1,5},{5... | collective-permute-start | bytes 786440 | tf_op jit(solution)/shard_map/ppermute | solution.py:94
  655.9 71.3 %collective-permute-start.58 = (bf16[2,2,128,256]{3,2,1,0:T(8,128)(2,1)}, bf16[2,2,128,256]{3,2,1,0:T(8,128)(2,1)}, u32[]{:S(2)}, u32[]{:S(2)}) collective-permute-start(bf16[2,2,128,256]{3,2,1,0:T(8,128)(2,1)} %dynamic-slice_bitcast_fusion.12), channel_id=1, source_target_pairs={{0,4},{4,0},{8,12},{12,8},{16,20},{20,16},{24,28},{28,24},{1,5},{5... | collective-permute-start | bytes 786440 | tf_op jit(solution)/shard_map/ppermute | solution.py:94
  674.3 36.4 %collective-permute-start.25 = (bf16[192,512]{1,0:T(8,128)(2,1)S(1)}, bf16[192,512]{1,0:T(8,128)(2,1)S(1)}, u32[]{:S(2)}, u32[]{:S(2)}) collective-permute-start(bf16[192,512]{1,0:T(8,128)(2,1)S(1)} %get-tuple-element.337), channel_id=1, source_target_pairs={{12,0},{13,4},{0,8},{1,12},{4,16},{5,20},{8,24},{9,28},{28,1},{29,... | collective-permute-start | bytes 589832 | tf_op jit(solution)/shard_map/ppermute | solution.py:76
  (303 other events, 1867.8 us)

commit v2 on v0

v2 whole, which is shorter than its diff:
```python
import functools

import jax
import jax.numpy as jnp
from jax import lax
from jax.experimental import pallas as pl
from jax.experimental.pallas import tpu as pltpu
from jax.sharding import PartitionSpec as P

D = 512
H = 8
DH = 64

epsilon = 1e-05
masked_score = -1e30
AXES = ("seq", "batch")


VOCAB = 256
BF16 = jnp.bfloat16
F32 = jnp.float32
ANYWHERE = pl.BlockSpec(memory_space=pl.ANY)
ROOM = 56 * 1024 * 1024


def dot(left, right):
    return jnp.dot(left, right, preferred_element_type=F32)


def dot_nt(left, right):
    return lax.dot_general(left, right, (((1,), (1,)), ((), ())), preferred_element_type=F32)


def iota(shape, dim):
    return lax.broadcasted_iota(jnp.int32, shape, dim)


def picks(condition):
    return jnp.where(condition, 1.0, 0.0).astype(BF16)


def call(kernel, out_shape, grid, in_specs, out_specs, scratch=(), scalars=0, flops=0, after=()):
    held = scalars + len(in_specs)

    def inner(*refs):
        kernel(*refs[:held], *refs[held + len(after) :])

    made = pl.pallas_call(
        inner,
        out_shape=out_shape,
        grid_spec=pltpu.PrefetchScalarGridSpec(
            num_scalar_prefetch=scalars,
            grid=grid,
            in_specs=in_specs + [ANYWHERE] * len(after),
            out_specs=out_specs,
            scratch_shapes=scratch,
        ),
        compiler_params=pltpu.CompilerParams(vmem_limit_bytes=ROOM),
        cost_estimate=pl.CostEstimate(flops=flops, bytes_accessed=flops // 300, transcendentals=0),
    )
    return lambda *operands: made(*operands, *after)


def shape(dims, dtype):
    return jax.ShapeDtypeStruct(dims, dtype)


def fixed(block, index=None, buffers=1):
    place = index or (0,) * len(block)
    return pl.BlockSpec(block, lambda *unused: place, pipeline_mode=pl.Buffered(buffers))


def gain_row(ref, layer):
    return ref[...].astype(F32)[layer : layer + 1]


def normalize(inputs, gain):
    centred = inputs - jnp.mean(inputs, -1, keepdims=True)
    inverse = lax.rsqrt(jnp.mean(centred * centred, -1, keepdims=True) + epsilon)
    normed = centred * inverse
    return ((normed * gain).astype(BF16), normed, inverse)


def normalize_back(grad, normed, inverse, gain):
    scaled = grad * gain
    result = inverse * (
        scaled
        - jnp.mean(scaled, -1, keepdims=True)
        - normed * jnp.mean(scaled * normed, -1, keepdims=True)
    )
    return (result, jnp.sum(grad * normed, axis=0, keepdims=True))


def rotate(inputs, cosine, sine):
    width = inputs.shape[1]
    count = width // 128
    first = iota(inputs.shape, 1) % DH < DH // 2
    other = jnp.where(
        first, pltpu.roll(inputs, width - DH // 2, 1), pltpu.roll(inputs, DH // 2, 1)
    )
    return inputs * jnp.concatenate([cosine] * count, 1) + other * jnp.concatenate([sine] * count, 1)


def gelu_both(hidden):
    scale = 0.7978845608028654
    square = hidden * hidden
    tanh = jnp.tanh(scale * hidden * (1.0 + 0.044715 * square))
    half = 0.5 + 0.5 * tanh
    slope = half + (0.5 * scale) * hidden * (1.0 - tanh * tanh) * (1.0 + 0.134145 * square)
    return (hidden * half, slope)


def layout(blocks):
    starts, at = [], 0
    for deep, wide in blocks:
        starts.append(at)
        at += deep * -(-wide // 128)
    return starts, at


def slot_of(order, axis, apart):
    slot = 0
    for place, (name, bit) in enumerate(order):
        if name == axis:
            slot = slot + ((apart // bit) % 2) * (1 << (len(order) - 1 - place))
    return slot


def put(packed, slot, start, block):
    deep, wide = block.shape
    half = packed.shape[1]
    for tile in range(-(-wide // 128)):
        piece = block[:, tile * 128 : min(wide, (tile + 1) * 128)]
        packed[slot // half, slot % half, start + tile * deep : start + (tile + 1) * deep, : piece.shape[1]] = piece


def put_all(packed, order, me, start, made, deep, wide, swapped):
    rows, columns = made.shape
    for line in range(rows // deep):
        for column in range(columns // wide):
            batch, seq = (column, line) if swapped else (line, column)
            slot = slot_of(order, "batch", batch ^ me[1]) + slot_of(order, "seq", seq ^ me[2])
            put(packed, slot, start, made[line * deep : (line + 1) * deep, column * wide : (column + 1) * wide])


def hand_out(packed, stays, leaves, sems):
    copies = [pltpu.make_async_copy(packed.at[n], out, sems.at[n]) for n, out in enumerate((stays, leaves))]
    for copy in copies:
        copy.start()
    for copy in copies:
        copy.wait()


def packed_scratch(batches, seqs, rows):
    return [pltpu.VMEM((2, batches * seqs // 2, rows, 128), BF16), pltpu.SemaphoreType.DMA((2,))]


def packed_shapes(batches, seqs, rows):
    return (shape((batches * seqs // 2, rows, 128), BF16),) * 2


def embed_kernel(layer, tokens, embed, gain, w_qkv, cosine, sine, inputs, low, both):
    part = pl.program_id(0)

    @pl.when(part == 0)
    def first():
        onehot = picks(tokens[...] == iota((tokens.shape[0], embed.shape[0]), 1))
        value = dot(onehot, embed[...])
        inputs[...] = value.astype(BF16)
        low[...] = normalize(value, gain_row(gain, layer))[0]

    joined = dot(low[...], w_qkv[0])

    @pl.when(part == 0)
    def keys():
        both[0] = rotate(joined, cosine[...], sine[...]).astype(BF16)

    @pl.when(part == 1)
    def values():
        both[0] = joined.astype(BF16)


def embed_call(layer, tokens, embed, gain, w_qkv, cosine, sine, after=()):
    count = tokens.shape[0]
    return call(
        functools.partial(embed_kernel, layer),
        (shape((count, D), BF16), shape((count, D), BF16), shape((2, count, D), BF16)),
        grid=(2,),
        in_specs=[
            fixed(tokens.shape),
            fixed(embed.shape),
            fixed(gain.shape),
            pl.BlockSpec((1, D, D), lambda part: (layer, 0, part + 1)),
            fixed(cosine.shape),
            fixed(sine.shape),
        ],
        out_specs=(
            fixed((count, D)),
            fixed((count, D)),
            pl.BlockSpec((1, count, D), lambda part: (part, 0, 0)),
        ),
        flops=2 * count * D * (2 * D + embed.shape[0]),
        after=after,
    )(tokens, embed, gain, w_qkv, cosine, sine)


def query_kernel(low, w_qkv, cosine, sine, queries):
    joined = dot(low[...], w_qkv[0])
    queries[...] = (rotate(joined, cosine[...], sine[...]) * DH ** (-0.5)).astype(BF16)


def query_call(layer, low, w_qkv, cosine, sine, after=()):
    count = low.shape[0]
    return call(
        query_kernel,
        shape((count, D), BF16),
        grid=(1,),
        in_specs=[
            fixed((count, D)),
            fixed((1, D, D), (layer, 0, 0)),
            fixed(cosine.shape),
            fixed(sine.shape),
        ],
        out_specs=fixed((count, D)),
        flops=2 * count * D * D,
        after=after,
    )(low, w_qkv, cosine, sine)


def pool_kernel(layer, rows, members, me, first, edge, w_pool, gain, w_qkv, cosine, sine, grouped, pooled, low, both):
    span = first.shape[0] // rows
    count = pooled.shape[0]
    short = count // rows
    late = jnp.where(me[0] == 0, 1, 0)
    total = jnp.zeros((count, D), F32)
    for third in range(3):
        pick = picks(iota((short, span), 1) == 3 * iota((short, span), 0) + third - 2)
        piece = jnp.concatenate(
            [dot(pick, first[row * span : (row + 1) * span, :]) for row in range(rows)], 0
        )
        if third < 2:
            place = iota((count, 2 * rows), 0) == (iota((count, 2 * rows), 1) // 2 + late) * short
            place = picks(place & (iota((count, 2 * rows), 1) % 2 == third))
            piece = piece + dot(place, edge[...])
        piece = piece.astype(BF16)
        grouped[:, third * D : (third + 1) * D] = piece
        total = total + dot(piece, w_pool[third * D : (third + 1) * D, :])
    pooled[...] = total
    low[...] = normalize(total, gain_row(gain, layer))[0]
    both[0] = rotate(dot(low[...], w_qkv[0, :, D : 2 * D]), cosine[...], sine[...]).astype(BF16)
    both[1] = dot(low[...], w_qkv[0, :, 2 * D :]).astype(BF16)


def pool_call(layer, rows, members, me, first, edge, w_pool, gain, w_qkv, cosine, sine, after=()):
    count = cosine.shape[0]
    return call(
        functools.partial(pool_kernel, layer, rows, members),
        (
            shape((count, 3 * D), BF16),
            shape((count, D), F32),
            shape((count, D), BF16),
            shape((2, count, D), BF16),
        ),
        grid=(1,),
        scalars=1,
        in_specs=[
            fixed(first.shape),
            fixed(edge.shape),
            fixed(w_pool.shape),
            fixed(gain.shape),
            fixed((1, D, 3 * D), (layer, 0, 0)),
            fixed(cosine.shape),
            fixed(sine.shape),
        ],
        out_specs=(fixed((count, 3 * D)), fixed((count, D)), fixed((count, D)), fixed((2, count, D))),
        flops=2 * count * D * 5 * D,
        after=after,
    )(me, first, edge, w_pool, gain, w_qkv, cosine, sine)


GROUP = 256
HEADS = GROUP // DH


def fill_keys(rows, members, own, others, keys, values):
    span = own.shape[1] // rows
    for row in range(rows):
        for by, source in enumerate([own, *others]):
            start = (row * members + by) * span
            keys[start : start + span, :] = source[0, row * span : (row + 1) * span, :]
            values[start : start + span, :] = source[1, row * span : (row + 1) * span, :]


def fill_bias(member, members, span, bias):
    line = iota((span, members * span), 0)
    column = iota((span, members * span), 1)
    other = (member + column // span) % members < member
    seen = ((column < span) & (column <= line)) | ((column >= span) & other)
    bias[...] = jnp.where(seen, 0.0, masked_score)


def score(query, keys, bias, start, end):
    scores = dot_nt(query, keys[0:end, :])
    last = scores[:, start:] + bias[...]
    return jnp.concatenate([scores[:, :start], last], 1) if start else last


def attention_kernel(rows, members, me, queries, own, *refs):
    others = refs[: members - 1]
    mixed, logsum, keys, values, bias, total = refs[members - 1 :]
    span = queries.shape[0] // rows
    width = members * span
    fill_keys(rows, members, own, others, keys, values)
    fill_bias(me[0], members, span, bias)
    logsum[...] = jnp.zeros_like(logsum)

    def one_head(head, unused):
        lanes = iota((1, GROUP), 1) // DH == head
        mask = picks(lanes)
        for row in range(rows):
            block = slice(row * span, (row + 1) * span)
            start, end = row * width, (row + 1) * width
            scores = score(queries[block, :] * mask, keys, bias, start, end)
            highest = jnp.max(scores, -1, keepdims=True)
            expon = jnp.exp(scores - highest)
            totals = jnp.sum(expon, -1, keepdims=True)
            out = dot(expon.astype(BF16), values[0:end, :]) / totals
            total[block, :] = jnp.where(lanes, out, total[block, :])
            logsum[0, block, :] = jnp.where(
                iota((span, 128), 1) == head, highest + jnp.log(totals), logsum[0, block, :]
            )
        return unused

    lax.fori_loop(0, HEADS, one_head, 0)
    mixed[...] = total[...].astype(BF16)


def lane_group(ndim, block):
    return pl.BlockSpec(block, lambda group, *unused: (0,) * (ndim - 1) + (group,))


def attention_call(rows, members, me, queries, own, others, after=()):
    count = queries.shape[0]
    span = count // rows
    every = members * count
    pairs = rows * (rows + 1) // 2 * members * span * span
    return call(
        functools.partial(attention_kernel, rows, members),
        (shape((count, D), BF16), shape((D // GROUP, count, 128), F32)),
        grid=(D // GROUP,),
        scalars=1,
        in_specs=[lane_group(2, (count, GROUP))] + [lane_group(3, (2, count, GROUP))] * members,
        out_specs=(
            lane_group(2, (count, GROUP)),
            pl.BlockSpec((1, count, 128), lambda group, *unused: (group, 0, 0)),
        ),
        scratch=[
            pltpu.VMEM((every, GROUP), BF16),
            pltpu.VMEM((every, GROUP), BF16),
            pltpu.VMEM((span, members * span), F32),
            pltpu.VMEM((count, GROUP), F32),
        ],
        flops=16 * pairs * D,
        after=after,
    )(me, queries, own, *others)


def attention_back_kernel(rows, members, me, queries, own, *refs):
    others = refs[: members - 1]
    mixed, logsum, grad_mixed, grad_queries, *rest = refs[members - 1 :]
    pieces = rest[:members]
    keys, values, bias, turned, turned_grad, grad_keys, grad_values, total = rest[members:]
    span = queries.shape[0] // rows
    width = members * span
    fill_keys(rows, members, own, others, keys, values)
    fill_bias(me[0], members, span, bias)
    for row in range(rows):
        block = slice(row * span, (row + 1) * span)
        turned[row] = queries[block, :].T
        turned_grad[row] = grad_mixed[block, :].T

    def one_head(head, unused):
        lanes = iota((1, GROUP), 1) // DH == head
        mask = picks(lanes)
        mine = pl.ds(pl.multiple_of(head * DH, DH), DH)
        for row in reversed(range(rows)):
            block = slice(row * span, (row + 1) * span)
            start, end = row * width, (row + 1) * width
            grad = grad_mixed[block, :] * mask
            summed = jnp.sum(
                jnp.where(iota((span, 128), 1) == head, logsum[0, block, :], 0.0), -1, keepdims=True
            )
            probs = jnp.exp(score(queries[block, :] * mask, keys, bias, start, end) - summed)
            delta = jnp.sum(grad.astype(F32) * mixed[block, :].astype(F32), -1, keepdims=True)
            grad_scores = (probs * (dot_nt(grad, values[0:end, :]) - delta)).astype(BF16)
            out = dot(grad_scores, keys[0:end, :])
            total[block, :] = jnp.where(lanes, out, total[block, :])
            part_keys = dot(turned[row, mine, :], grad_scores)
            part_values = dot(turned_grad[row, mine, :], probs.astype(BF16))
            if row == rows - 1:
                grad_keys[mine, 0:end] = part_keys
                grad_values[mine, 0:end] = part_values
            else:
                grad_keys[mine, 0:end] += part_keys
                grad_values[mine, 0:end] += part_values
        return unused

    lax.fori_loop(0, HEADS, one_head, 0)
    grad_queries[...] = total[...].astype(BF16)
    for number, source in enumerate((grad_keys, grad_values)):
        made = source[...].astype(BF16).T
        for row in range(rows):
            for by, piece in enumerate(pieces):
                start = (row * members + by) * span
                piece[number, row * span : (row + 1) * span, :] = made[start : start + span, :]


def attention_back_call(rows, members, me, queries, own, others, mixed, logsum, grad_mixed, after=()):
    count = queries.shape[0]
    span = count // rows
    every = members * count
    pairs = rows * (rows + 1) // 2 * members * span * span
    made = call(
        functools.partial(attention_back_kernel, rows, members),
        (shape((count, D), BF16),) + (shape((2, count, D), BF16),) * members,
        grid=(D // GROUP,),
        scalars=1,
        in_specs=[lane_group(2, (count, GROUP))]
        + [lane_group(3, (2, count, GROUP))] * members
        + [
            lane_group(2, (count, GROUP)),
            pl.BlockSpec((1, count, 128), lambda group, *unused: (group, 0, 0)),
            lane_group(2, (count, GROUP)),
        ],
        out_specs=(lane_group(2, (count, GROUP)),) + (lane_group(3, (2, count, GROUP)),) * members,
        scratch=[
            pltpu.VMEM((every, GROUP), BF16),
            pltpu.VMEM((every, GROUP), BF16),
            pltpu.VMEM((span, members * span), F32),
            pltpu.VMEM((rows, GROUP, span), BF16),
            pltpu.VMEM((rows, GROUP, span), BF16),
            pltpu.VMEM((GROUP, every), F32),
            pltpu.VMEM((GROUP, every), F32),
            pltpu.VMEM((count, GROUP), F32),
        ],
        flops=40 * pairs * D,
        after=after,
    )(me, queries, own, *others, mixed, logsum, grad_mixed)
    return (made[0], made[1:])


CHUNK = 512


def ffn_kernel(layer, rows, inputs, mixed, w_out, gain, w_up, w_down, output, edges, middle, hidden, low, total):
    part = pl.program_id(0)

    @pl.when(part == 0)
    def first():
        value = inputs[...].astype(F32) + dot(mixed[...], w_out[0])
        middle[...] = value
        total[...] = value
        low[...] = normalize(value, gain_row(gain, layer))[0]

    made = dot(low[...], w_up[0])
    hidden[...] = made.astype(BF16)
    total[...] += dot(gelu_both(made)[0].astype(BF16), w_down[0])

    @pl.when(part == pl.num_programs(0) - 1)
    def last():
        made = total[...].astype(BF16)
        output[...] = made
        count = made.shape[0]
        span = count // rows
        line = iota((2 * rows, count), 0)
        pick = picks(iota((2 * rows, count), 1) == (line // 2 + 1) * span - 2 + line % 2)
        edges[...] = dot(pick, made).astype(BF16)


def ffn_call(layer, rows, inputs, mixed, w_out, gain, w_up, w_down, after=()):
    count = inputs.shape[0]
    units = w_up.shape[2]
    return call(
        functools.partial(ffn_kernel, layer, rows),
        (
            shape((count, D), BF16),
            shape((2 * rows, D), BF16),
            shape((count, D), F32),
            shape((count, units), BF16),
        ),
        grid=(units // CHUNK,),
        in_specs=[
            fixed((count, D)),
            fixed((count, D)),
            fixed((1, D, D), (layer, 0, 0)),
            fixed(gain.shape),
            pl.BlockSpec((1, D, CHUNK), lambda part: (layer, 0, part)),
            pl.BlockSpec((1, CHUNK, D), lambda part: (layer, part, 0)),
        ],
        out_specs=(
            fixed((count, D)),
            fixed((2 * rows, D)),
            fixed((count, D)),
            pl.BlockSpec((count, CHUNK), lambda part: (0, part)),
        ),
        scratch=[pltpu.VMEM((count, D), BF16), pltpu.VMEM((count, D), F32)],
        flops=2 * count * D * (D + 2 * units),
        after=after,
    )(inputs, mixed, w_out, gain, w_up, w_down)


def ffn_blocks(batches, seqs, units):
    return ((D // batches, units // seqs), (D // seqs, units // batches), (D // seqs, D // batches))


def ffn_back_kernel(
    layer, rows, members, batches, seqs, order, carries,
    me, grad_ref, carried, mixed, middle, hidden, w_out, gain, w_up, w_down,
    stays, leaves, grad_gain, grad_middle, grad_mixed,
    low, turned_low, grad, turned_grad, total, packed, sems,
):
    part = pl.program_id(0)
    blocks = ffn_blocks(batches, seqs, CHUNK * pl.num_programs(0))
    starts, unused = layout(blocks)

    @pl.when(part == 0)
    def first():
        value = grad_ref[...]
        if carries:
            count = value.shape[0]
            span = count // rows
            early = jnp.where(me[0] == members - 1, 1, 0)
            line = iota((count, 2 * rows), 1)
            place = iota((count, 2 * rows), 0) == (line // 2 + 1 - early) * span - 2 + line % 2
            value = (value.astype(F32) + dot(picks(place), carried[...])).astype(BF16)
        grad[...] = value
        turned_grad[...] = value.T
        made = normalize(middle[...], gain_row(gain, layer))[0]
        low[...] = made
        turned_low[...] = made.T

    active, slope = gelu_both(hidden[...].astype(F32))
    grad_hidden = (dot_nt(grad[...], w_down[0]) * slope).astype(BF16)
    made = dot(turned_grad[...], active.astype(BF16)).astype(BF16)
    deep, wide = blocks[1]
    for column in range(CHUNK // wide):
        batch = slot_of(order, "batch", (part * (CHUNK // wide) + column) ^ me[1])
        for seq in range(seqs):
            slot = batch + slot_of(order, "seq", seq ^ me[2])
            put(packed, slot, starts[1], made[seq * deep : (seq + 1) * deep, column * wide : (column + 1) * wide])
    made = dot(turned_low[...], grad_hidden).astype(BF16)
    deep, wide = blocks[0]
    for column in range(CHUNK // wide):
        seq = slot_of(order, "seq", (part * (CHUNK // wide) + column) ^ me[2])
        for batch in range(batches):
            slot = seq + slot_of(order, "batch", batch ^ me[1])
            put(packed, slot, starts[0], made[batch * deep : (batch + 1) * deep, column * wide : (column + 1) * wide])
    made = dot_nt(grad_hidden, w_up[0])

    @pl.when(part == 0)
    def begin():
        total[...] = made

    @pl.when(part > 0)
    def add():
        total[...] += made

    @pl.when(part == pl.num_programs(0) - 1)
    def last():
        row = gain_row(gain, layer)
        unused, normed, inverse = normalize(middle[...], row)
        back, gain_sum = normalize_back(total[...], normed, inverse, row)
        grad_gain[...] = gain_sum
        value = grad[...].astype(F32) + back
        grad_middle[...] = value
        branch = value.astype(BF16)
        grad_mixed[...] = dot_nt(branch, w_out[0]).astype(BF16)
        put_all(packed, order, me, starts[2], dot(branch.T, mixed[...]).astype(BF16), *blocks[2], True)
        hand_out(packed, stays, leaves, sems)


def ffn_back_call(
    layer, rows, members, batches, seqs, order, me,
    grad, carried, mixed, middle, hidden, w_out, gain, w_up, w_down, after=()):
    count = grad.shape[0]
    units = w_up.shape[2]
    carries = carried is not None
    if not carries:
        carried = jnp.zeros((2 * rows, D), BF16)
    packs = layout(ffn_blocks(batches, seqs, units))[1]
    return call(
        functools.partial(ffn_back_kernel, layer, rows, members, batches, seqs, order, carries),
        packed_shapes(batches, seqs, packs)
        + (shape((1, D), F32), shape((count, D), F32), shape((count, D), BF16)),
        grid=(units // CHUNK,),
        scalars=1,
        in_specs=[
            fixed((count, D)),
            fixed((2 * rows, D)),
            fixed((count, D)),
            fixed((count, D)),
            pl.BlockSpec((count, CHUNK), lambda part, me: (0, part)),
            fixed((1, D, D), (layer, 0, 0)),
            fixed(gain.shape),
            pl.BlockSpec((1, D, CHUNK), lambda part, me: (layer, 0, part)),
            pl.BlockSpec((1, CHUNK, D), lambda part, me: (layer, part, 0)),
        ],
        out_specs=(ANYWHERE, ANYWHERE, fixed((1, D)), fixed((count, D)), fixed((count, D))),
        scratch=[
            pltpu.VMEM((count, D), BF16),
            pltpu.VMEM((D, count), BF16),
            pltpu.VMEM((count, D), BF16),
            pltpu.VMEM((D, count), BF16),
            pltpu.VMEM((count, D), F32),
        ]
        + packed_scratch(batches, seqs, packs),
        flops=2 * count * D * (2 * D + 4 * units),
        after=after,
    )(me, grad, carried, mixed, middle, hidden, w_out, gain, w_up, w_down)


def joined_blocks(batches, seqs, other):
    return ((3 * D // seqs, D // batches), other)


def joined_back(layer, batches, seqs, order, me, inputs, grad_queries, sources, rest):
    grad_middle, cosine, sine, gain, w_qkv, grad_gain, turned, packed = rest
    row = gain_row(gain, layer)
    low, normed, inverse = normalize(inputs[...].astype(F32), row)
    back = 0.0
    for part in range(3):
        if part == 0:
            value = grad_queries[...].astype(F32) * DH ** (-0.5)
        else:
            value = sources[0][part - 1].astype(F32)
            for other in sources[1:]:
                value = value + other[part - 1].astype(F32)
        if part < 2:
            value = rotate(value, cosine[...], -sine[...])
        value = value.astype(BF16)
        turned[part * D : (part + 1) * D, :] = value.T
        back = back + dot_nt(value, w_qkv[0, :, part * D : (part + 1) * D])
    deep, wide = joined_blocks(batches, seqs, None)[0]

    def one_block(seq, unused):
        made = dot(turned[pl.ds(pl.multiple_of(seq * deep, deep), deep), :], low).astype(BF16)
        place = slot_of(order, "seq", seq ^ me[2])
        for batch in range(batches):
            slot = place + slot_of(order, "batch", batch ^ me[1])
            put(packed, slot, 0, made[:, batch * wide : (batch + 1) * wide])
        return unused

    lax.fori_loop(0, seqs, one_block, 0)
    value, gain_sum = normalize_back(back, normed, inverse, row)
    grad_gain[...] = gain_sum
    return grad_middle[...] + value


def embed_back_kernel(layer, members, batches, seqs, order, me, inputs, grad_queries, *refs):
    sources = refs[:members]
    (
        grad_middle, cosine, sine, gain, w_qkv, tokens,
        stays, leaves, grad_gain, grad_inputs, turned, packed, sems,
    ) = refs[members:]
    value = joined_back(
        layer, batches, seqs, order, me, inputs, grad_queries, sources,
        (grad_middle, cosine, sine, gain, w_qkv, grad_gain, turned, packed),
    ).astype(BF16)
    grad_inputs[...] = value
    blocks = joined_blocks(batches, seqs, (VOCAB // batches, D // seqs))
    onehot = picks(tokens[...] == iota((VOCAB, tokens.shape[1]), 0))
    put_all(packed, order, me, layout(blocks)[0][1], dot(onehot, value).astype(BF16), *blocks[1], False)
    hand_out(packed, stays, leaves, sems)


def embed_back_call(
    layer, batches, seqs, order, me, inputs, grad_queries, pieces, grad_middle, cosine, sine, gain, w_qkv, tokens, after=()):
    count = inputs.shape[0]
    members = len(pieces)
    packs = layout(joined_blocks(batches, seqs, (VOCAB // batches, D // seqs)))[1]
    return call(
        functools.partial(embed_back_kernel, layer, members, batches, seqs, order),
        packed_shapes(batches, seqs, packs) + (shape((1, D), F32), shape((count, D), BF16)),
        grid=(1,),
        scalars=1,
        in_specs=[fixed((count, D))] * 2
        + [fixed((2, count, D))] * members
        + [
            fixed((count, D)),
            fixed(cosine.shape),
            fixed(sine.shape),
            fixed(gain.shape),
            fixed((1, D, 3 * D), (layer, 0, 0)),
            fixed(tokens.shape),
        ],
        out_specs=(ANYWHERE, ANYWHERE, fixed((1, D)), fixed((count, D))),
        scratch=[pltpu.VMEM((3 * D, count), BF16)] + packed_scratch(batches, seqs, packs),
        flops=2 * count * D * (6 * D + VOCAB),
        after=after,
    )(me, inputs, grad_queries, *pieces, grad_middle, cosine, sine, gain, w_qkv, tokens)


def pool_back_kernel(layer, rows, members, batches, seqs, order, me, inputs, grad_queries, *refs):
    sources = refs[:members]
    (
        grad_middle, cosine, sine, gain, w_qkv, grouped, w_pool,
        stays, leaves, grad_gain, grad_first, edges, turned, packed, sems,
    ) = refs[members:]
    value = joined_back(
        layer, batches, seqs, order, me, inputs, grad_queries, sources,
        (grad_middle, cosine, sine, gain, w_qkv, grad_gain, turned, packed),
    ).astype(BF16)
    blocks = joined_blocks(batches, seqs, (D // seqs, 3 * D // batches))
    put_all(packed, order, me, layout(blocks)[0][1], dot(value.T, grouped[...]).astype(BF16), *blocks[1], True)
    count = value.shape[0]
    short = count // rows
    span = grad_first.shape[0] // rows
    parts = [dot_nt(value, w_pool[third * D : (third + 1) * D, :]).astype(BF16) for third in range(3)]
    line = iota((2 * rows, count), 0)
    found = 0.0
    for third in range(2):
        pick = (iota((2 * rows, count), 1) == (line // 2) * short) & (line % 2 == third)
        found = found + dot(picks(pick), parts[third])
    edges[...] = found.astype(BF16)
    for row in range(rows):
        total = 0.0
        for third in range(3):
            pick = picks(iota((span, short), 0) == 3 * iota((span, short), 1) + third - 2)
            total = total + dot(pick, parts[third][row * short : (row + 1) * short, :])
        grad_first[row * span : (row + 1) * span, :] = total.astype(BF16)
    hand_out(packed, stays, leaves, sems)


def pool_back_call(
    layer, rows, span, batches, seqs, order, me, inputs, grad_queries, pieces, grad_middle, cosine, sine,
    gain, w_qkv, grouped, w_pool, after=()):
    count = inputs.shape[0]
    members = len(pieces)
    packs = layout(joined_blocks(batches, seqs, (D // seqs, 3 * D // batches)))[1]
    return call(
        functools.partial(pool_back_kernel, layer, rows, members, batches, seqs, order),
        packed_shapes(batches, seqs, packs)
        + (shape((1, D), F32), shape((rows * span, D), BF16), shape((2 * rows, D), BF16)),
        grid=(1,),
        scalars=1,
        in_specs=[fixed((count, D))] * 2
        + [fixed((2, count, D))] * members
        + [
            fixed((count, D)),
            fixed(cosine.shape),
            fixed(sine.shape),
            fixed(gain.shape),
            fixed((1, D, 3 * D), (layer, 0, 0)),
            fixed(grouped.shape),
            fixed(w_pool.shape),
        ],
        out_specs=(ANYWHERE, ANYWHERE, fixed((1, D)), fixed((rows * span, D)), fixed((2 * rows, D))),
        scratch=[pltpu.VMEM((3 * D, count), BF16)] + packed_scratch(batches, seqs, packs),
        flops=2 * count * D * (12 * D),
        after=after,
    )(me, inputs, grad_queries, *pieces, grad_middle, cosine, sine, gain, w_qkv, grouped, w_pool)


def angles(positions):
    half_size = DH // 2
    freqs = 10000.0 ** (-jnp.arange(half_size).astype(jnp.float32) / half_size)
    phase = positions.astype(jnp.float32)[:, None] * freqs[None, :]
    cosine, sine = jnp.cos(phase), jnp.sin(phase)
    return (jnp.concatenate([cosine] * 4, 1), jnp.concatenate([-sine, sine] * 2, 1))


class Plan:
    def __init__(self, rows):
        self.S = lax.axis_size("seq")
        self.B = lax.axis_size("batch")
        self.R = rows
        self.P = self.S // rows
        self.s = lax.axis_index("seq")
        self.b = lax.axis_index("batch")
        self.z = self.s // self.P
        self.h = self.s % self.P // 2 * 2 + self.b % 2

    def device(self, pair, z, y, core):
        return (z * self.P + y) * self.B + 2 * pair + core

    def exchange(self, value):
        moves = []
        for apart in range(self.R):
            perm = []
            for pair in range(self.B // 2):
                for z in range(self.R):
                    for y in range(self.P):
                        for core in range(2):
                            other = self.device(pair, z ^ apart, y // 2 * 2 + core, y % 2)
                            perm.append((self.device(pair, z, y, core), other))
            piece = lax.dynamic_index_in_dim(value, self.z ^ apart, 0, keepdims=False)
            moves.append(lax.ppermute(piece, AXES, perm))
        got, bit = moves, 1
        while bit < self.R:
            flip = (self.z // bit) % 2 == 1
            got = [jnp.where(flip, got[n ^ bit], got[n]) for n in range(self.R)]
            bit *= 2
        return (jnp.stack(got), moves)

    def shift(self, value, by):
        perm = []
        for pair in range(self.B // 2):
            for z in range(self.R):
                for batch in range(2):
                    for member in range(self.P):
                        to = (member + by) % self.P
                        perm.append((
                            self.device(pair, z, member // 2 * 2 + batch, member % 2),
                            self.device(pair, z, to // 2 * 2 + batch, to % 2),
                        ))
        return lax.ppermute(value, AXES, perm)

    def others(self, value):
        return [self.shift(value, by) for by in range(1, self.P)]

    def swap(self, value, axis, bit):
        count = lax.axis_size(axis)
        return lax.ppermute(value, axis, [(n, n ^ bit) for n in range(count)])

    def bits(self, axis):
        count = lax.axis_size(axis)
        return [1 << n for n in range(count.bit_length() - 1)]

    def order(self, first):
        batch = [("batch", bit) for bit in self.bits("batch")]
        seq = [("seq", bit) for bit in self.bits("seq")]
        return batch + seq if first == "batch" else batch[:1] + seq[:1] + batch[1:] + seq[1:]

    def all_sum(self, value):
        for axis in ("batch", "seq"):
            for bit in self.bits(axis):
                value = value + self.swap(value, axis, bit)
        return value


class Halving:
    def __init__(self, plan, order, stays, leaves):
        self.plan, self.order = plan, order
        self.value, self.leaves = stays.astype(F32), leaves
        self.got = []

    def step(self, count=1):
        for axis, bit in self.order[len(self.got) : len(self.got) + count]:
            got = self.plan.swap(self.leaves, axis, bit)
            self.got.append(got)
            self.value = self.value + got.astype(F32)
            half = self.value.shape[0] // 2
            if half:
                self.leaves, self.value = self.value[half:].astype(BF16), self.value[:half]
        return self.got[-1]

    def end(self):
        self.step(len(self.order))
        return self.value[0]


def unpacked(total, blocks):
    starts, unused = layout(blocks)
    made = []
    for (deep, wide), start in zip(blocks, starts):
        tiles = [
            total[start + tile * deep : start + (tile + 1) * deep, : min(128, wide - tile * 128)]
            for tile in range(-(-wide // 128))
        ]
        made.append(jnp.concatenate(tiles, 1))
    return made


def body(
    tokens, loss_mask, cotangent, embed, gain_attn, w_qkv, w_out, gain_ffn, w_up, w_down, w_pool
):
    plan = Plan(tokens.shape[0])
    rows, span = tokens.shape
    short = loss_mask.shape[1]
    members, batches, seqs = plan.P, plan.B, plan.S
    units = w_up.shape[2]
    by_x, by_y = plan.order("batch"), plan.order("seq")
    me = jnp.stack([plan.h, plan.b, plan.s]).astype(jnp.int32)

    my_tokens = plan.exchange(tokens)[0]
    token_line, token_column = my_tokens.reshape(1, rows * span), my_tokens.reshape(rows * span, 1)

    def places(length):
        block = jnp.arange(rows, dtype=jnp.int32)[:, None] * members + plan.h
        return (block * length + jnp.arange(length, dtype=jnp.int32)[None]).reshape(-1)

    first_angles, second_angles = angles(places(span)), angles(places(short))

    inputs, low, own_0 = embed_call(0, token_column, embed, gain_attn, w_qkv, *first_angles)
    others_0 = plan.others(own_0)
    queries_0 = query_call(0, low, w_qkv, *first_angles)
    start_grad, start_moves = plan.exchange(cotangent * loss_mask.astype(BF16)[..., None])
    mixed_0, logsum_0 = attention_call(rows, members, me, queries_0, own_0, others_0)
    first_low, edges, middle_0, hidden_0 = ffn_call(
        0, rows, inputs, mixed_0, w_out, gain_ffn, w_up, w_down, after=start_moves
    )
    edge = plan.shift(edges, 1)
    full_out, full_moves = plan.exchange(first_low.reshape(rows, span, D))

    grouped, pooled, low, own_1 = pool_call(
        1, rows, members, me, first_low, edge, w_pool, gain_attn, w_qkv, *second_angles
    )
    others_1 = plan.others(own_1)
    queries_1 = query_call(1, low, w_qkv, *second_angles)
    mixed_1, logsum_1 = attention_call(rows, members, me, queries_1, own_1, others_1)
    second_low, unused, middle_1, hidden_1 = ffn_call(
        1, rows, pooled, mixed_1, w_out, gain_ffn, w_up, w_down, after=full_moves
    )
    short_out, short_moves = plan.exchange(second_low.reshape(rows, short, D))

    stays, leaves, gain_ffn_1, grad_middle, grad_mixed = ffn_back_call(
        1, rows, members, batches, seqs, by_x, me, start_grad.reshape(-1, D), None, mixed_1, middle_1, hidden_1,
        w_out, gain_ffn, w_up, w_down,
    )
    ffn_1 = Halving(plan, by_x, stays, leaves)
    after = [ffn_1.step()]
    grad_queries, pieces = attention_back_call(
        rows, members, me, queries_1, own_1, others_1, mixed_1, logsum_1, grad_mixed
    )
    pieces = [pieces[0]] + [plan.shift(pieces[by], -by) for by in range(1, members)]
    stays, leaves, gain_attn_1, grad_first, edges = pool_back_call(
        1, rows, span, batches, seqs, by_y, me, pooled, grad_queries, pieces, grad_middle, *second_angles,
        gain_attn, w_qkv, grouped, w_pool, after=after + short_moves,
    )
    pool_1 = Halving(plan, by_y, stays, leaves)
    carried = plan.shift(edges, -1)

    after = [ffn_1.step(), pool_1.step()]
    stays, leaves, gain_ffn_0, grad_middle, grad_mixed = ffn_back_call(
        0, rows, members, batches, seqs, by_x, me, grad_first, carried, mixed_0, middle_0, hidden_0,
        w_out, gain_ffn, w_up, w_down,
    )
    ffn_0 = Halving(plan, by_x, stays, leaves)
    grad_queries, pieces = attention_back_call(
        rows, members, me, queries_0, own_0, others_0, mixed_0, logsum_0, grad_mixed, after=after
    )
    pieces = [pieces[0]] + [plan.shift(pieces[by], -by) for by in range(1, members)]
    after = [ffn_1.step(), pool_1.step(), ffn_0.step()]
    stays, leaves, gain_attn_0, grad_inputs = embed_back_call(
        0, batches, seqs, by_y, me, inputs, grad_queries, pieces, grad_middle, *first_angles,
        gain_attn, w_qkv, token_line, after=after,
    )
    qkv_0 = Halving(plan, by_y, stays, leaves)
    input_grad = plan.exchange(grad_inputs.reshape(rows, span, D))[0]

    blocks = ffn_blocks(batches, seqs, units)
    up_1, down_1, out_1 = unpacked(ffn_1.end(), blocks)
    up_0, down_0, out_0 = unpacked(ffn_0.end(), blocks)
    blocks = joined_blocks(batches, seqs, (D // seqs, 3 * D // batches))
    qkv_1, pool = unpacked(pool_1.end(), blocks)
    blocks = joined_blocks(batches, seqs, (VOCAB // batches, D // seqs))
    qkv_0, embed_grad = unpacked(qkv_0.end(), blocks)
    gains = plan.all_sum(jnp.concatenate([gain_attn_0, gain_attn_1, gain_ffn_0, gain_ffn_1]))
    return (
        full_out,
        short_out,
        input_grad.astype(jnp.float32),
        embed_grad,
        gains[:2],
        jnp.stack([qkv_0.T, qkv_1.T]),
        jnp.stack([out_0.T, out_1.T]),
        gains[2:],
        jnp.stack([up_0, up_1]),
        jnp.stack([down_0.T, down_1.T]),
        pool.T,
    )


def solution(mesh):
    in_specs = (
        P("batch", "seq"),
        P("batch", "seq"),
        P("batch", "seq", None),
        P(),
        P(),
        P(),
        P(),
        P(),
        P(),
        P(),
        P(),
    )
    out_specs = (
        P("batch", "seq", None),
        P("batch", "seq", None),
        P("batch", "seq", None),
        P("batch", "seq"),
        P(),
        P(None, "batch", "seq"),
        P(None, "batch", "seq"),
        P(),
        P(None, "batch", "seq"),
        P(None, "batch", "seq"),
        P("batch", "seq"),
    )
    return jax.shard_map(body, mesh=mesh, in_specs=in_specs, out_specs=out_specs, check_vma=False)
```

time: 1760 us -> 356 us (0.20)
  waiting for transfers between devices: 1160 us -> 69.3 us
  local copies, waits for them, and re-layouts: 256 us -> 20.2 us
  matrix products: 192 us -> 0 us
  Pallas kernels: 0 us -> 165 us
  starting transfers between devices: 5.63 us -> 68.5 us
  other arithmetic: 68.9 us -> 25.6 us
  blocking collectives: 40.1 us -> 0 us
    unnamed x25 -> x0, waiting for transfers between devices: 484 us -> none
    all_gather x4 -> x0, waiting for transfers between devices: 460 us -> none  [the longest x2 231 us: block_forward(): lax.all_gather(keys, 'seq', axis=1, tiled=True)]
    reduce_scatter x7 -> x0, waiting for transfers between devices: 215 us -> none  [the longest x1 64.4 us: body(): lax.psum_scatter(partial_sums[2].astype(jnp.bfloat16), 'seq', scatter_dim...]
    dot_general x85 -> x0, matrix products: 192 us -> none  [the longest x8 28.3 us: query_pass(): jnp.einsum('hqk,khd->qhd', grad_scores, keys, preferred_element_type=jnp....]
    unnamed x199 -> x102, local copies, waits for them, and re-layouts: 189 us -> 13.6 us
    pallas_call x0 -> x14, Pallas kernels: none -> 165 us  [call(): return lambda *operands: made(*operands, *after)]
    ppermute x2 -> x51, waiting for transfers between devices: 4.06 us -> 69.3 us  [the longest x25 57.9 us: swap(): return lax.ppermute(value, axis, [(n, n ^ bit) for n in range(count)])]
    ppermute x2 -> x51, starting transfers between devices: 4.15 us -> 68.5 us  [the longest x25 32 us: swap(): return lax.ppermute(value, axis, [(n, n ^ bit) for n in range(count)])]
  transfers between devices with their start and end apart: 20 -> 51, of which waited for: 18 -> 21; matrix products, arithmetic and copies ran while one was open for 11% -> 7% of each run, Pallas kernels for 0% -> 36%
where the time goes in v2:
time: 356 us; the launch traced here: 350 us
  Pallas kernels  165 us (46%)
  waiting for transfers between devices  69.3 us (19%)
  starting transfers between devices  68.5 us (19%)
  other arithmetic  25.6 us (7%)
  local copies, waits for them, and re-layouts  20.2 us (6%)
    pallas_call x14, Pallas kernels, call(): return lambda *operands: made(*operands, *after)  165 us
    ppermute x25, waiting for transfers between devices, swap(): return lax.ppermute(value, axis, [(n, n ^ bit) for n in range(count)])  57.9 us
    ppermute x25, starting transfers between devices, swap(): return lax.ppermute(value, axis, [(n, n ^ bit) for n in range(count)])  32 us
    ppermute x20, starting transfers between devices, exchange(): moves.append(lax.ppermute(piece, AXES, perm))  30.1 us
    unnamed x102, local copies, waits for them, and re-layouts  13.6 us
    ppermute x20, waiting for transfers between devices, exchange(): moves.append(lax.ppermute(piece, AXES, perm))  11.2 us
  transfers between devices with their start and end apart: 51, of which 21 were waited for; matrix products, arithmetic and copies ran while one was open for 7% of the time, Pallas kernels for 36%

profile of v2, /device:TPU:0, one launch (start us, length us, event | category | flops | bytes accessed | tf_op | source)
XLA Modules:
  0.0 350.3 jit_solution(14113616903130485505)
XLA Ops:
  1.5 4.1 %collective-permute-start.1 = (s32[192]{0:T(256)S(1)}, s32[192]{0:T(256)S(1)}, u32[]{:S(2)}, u32[]{:S(2)}) collective-permute-start(s32[192]{0:T(256)S(1)} %bitcast.162), channel_id=1, source_target_pairs={{0,16},{1,20},{4,17},{5,21},{8,24},{9,28},{12,25},{13,29},{16,0},{... | collective-permute-start | bytes 2312 | tf_op jit(solution)/shard_map/ppermute | solution.py:797
  13.6 6.1 %shard_map.194 = (bf16[768,512]{1,0:T(8,128)(2,1)}, bf16[768,512]{1,0:T(8,128)(2,1)}, bf16[2,768,512]{2,1,0:T(8,128)(2,1)}) custom-call(s32[768,1]{1,0:T(8,128)} %reshape.115.refs_0_, bf16[256,512]{1,0:T(8,128)(2,1)} %refs_1_.3, bf16[2,512]{1,0:T(2,128)(2,1)} %refs_8_.7, bf16[2,512,1536]{2,1,0:T(8,128)(2,1)} %refs_9_.7, ...), custom_call_target="tpu_custom_call" | custom-call | flops 1006632960 | bytes 3355443 | tf_op jit(solution)/shard_map/pallas_call | solution.py:61
  30.6 3.9 %shard_map.195.refs_1_ = bf16[768,512]{1,0:T(8,128)(2,1)} custom-call(bf16[768,512]{1,0:T(8,128)(2,1)} %get-tuple-element.55.refs_0_, bf16[2,512,1536]{2,1,0:T(8,128)(2,1)} %refs_9_.7, f32[768,128]{1,0:T(8,128)} %pad_maximum_fusion.1.refs_4_.refs_2_.refs_6_, f32[768,128]{1,0:T(8,128)} %pad_maximum_fusion.2.refs_5_.refs_3_.refs_7_), custom_call_target="tpu_custom_call" | custom-call | flops 402653184 | bytes 1342177 | tf_op jit(solution)/shard_map/pallas_call | solution.py:61
  35.6 21.3 %shard_map.196 = (bf16[768,512]{1,0:T(8,128)(2,1)}, f32[2,768,128]{2,1,0:T(8,128)}) custom-call(s32[3]{0:T(128)} %pad_add_fusion.1.refs_0_, bf16[768,512]{1,0:T(8,128)(2,1)} %shard_map.195.refs_1_, bf16[2,768,512]{2,1,0:T(8,128)(2,1)} %get-tuple-element.56.refs_2_, bf16[2,768,512]{2,1,0:T(8,128)(2,1)} %copy-done.45), custom_call_target="tpu_custom_call" | custom-call | flops 6039797760 | bytes 20132660 | tf_op jit(solution)/shard_map/pallas_call | solution.py:61
  57.7 10.0 %shard_map.197 = (bf16[768,512]{1,0:T(8,128)(2,1)}, bf16[8,512]{1,0:T(8,128)(2,1)}, f32[768,512]{1,0:T(8,128)}, bf16[768,2048]{1,0:T(8,128)(2,1)}) custom-call(bf16[768,512]{1,0:T(8,128)(2,1)} %get-tuple-element.54.refs_0_.refs_1_, bf16[768,512]{1,0:T(8,128)(2,1)} %get-tuple-element.57.refs_1_.refs_3_.refs_4_, bf16[2,512,512]{2,1,0:T(8,128)(2,1)} %refs_6_.3, ...), custom_call_target="tpu_custom_call" | custom-call | flops 3623878656 | bytes 12079595 | tf_op jit(solution)/shard_map/pallas_call | solution.py:61
  72.4 5.7 %shard_map.198 = (bf16[256,1536]{1,0:T(8,128)(2,1)}, f32[256,512]{1,0:T(8,128)}, bf16[256,512]{1,0:T(8,128)(2,1)}, bf16[2,256,512]{2,1,0:T(8,128)(2,1)}) custom-call(s32[3]{0:T(128)} %pad_add_fusion.1.refs_0_, bf16[768,512]{1,0:T(8,128)(2,1)} %get-tuple-element.58.refs_1_, bf16[8,512]{1,0:T(8,128)(2,1)} %copy-done.43, bf16[1536,512]{1,0:T(8,128)(2,1)} %refs_11_.1, ...), custom_call_target="tpu_custom_call" | custom-call | flops 671088640 | bytes 2236962 | tf_op jit(solution)/shard_map/pallas_call | solution.py:61
  87.9 12.6 %shard_map.200 = (bf16[256,512]{1,0:T(8,128)(2,1)}, f32[2,256,128]{2,1,0:T(8,128)}) custom-call(s32[3]{0:T(128)} %pad_add_fusion.1.refs_0_, bf16[256,512]{1,0:T(8,128)(2,1)} %shard_map.199.refs_1_, bf16[2,256,512]{2,1,0:T(8,128)(2,1)} %get-tuple-element.62.refs_2_, bf16[2,256,512]{2,1,0:T(8,128)(2,1)} %copy-done.47), custom_call_target="tpu_custom_call" | custom-call | flops 671088640 | bytes 2236962 | tf_op jit(solution)/shard_map/pallas_call | solution.py:61
  101.4 6.5 %shard_map.201 = (bf16[256,512]{1,0:T(8,128)(2,1)}, bf16[8,512]{1,0:T(8,128)(2,1)}, f32[256,512]{1,0:T(8,128)}, bf16[256,2048]{1,0:T(8,128)(2,1)}) custom-call(f32[256,512]{1,0:T(8,128)} %get-tuple-element.60.refs_0_.refs_1_, bf16[256,512]{1,0:T(8,128)(2,1)} %get-tuple-element.63.refs_1_.refs_3_.refs_4_, bf16[2,512,512]{2,1,0:T(8,128)(2,1)} %refs_6_.3, ...), custom_call_target="tpu_custom_call" | custom-call | flops 1207959552 | bytes 4026531 | tf_op jit(solution)/shard_map/pallas_call | solution.py:61
  108.5 11.6 %shard_map.202 = (bf16[16,576,128]{2,1,0:T(8,128)(2,1)}, bf16[16,576,128]{2,1,0:T(8,128)(2,1)}, f32[1,512]{1,0:T(1,128)}, f32[256,512]{1,0:T(8,128)}, bf16[256,512]{1,0:T(8,128)(2,1)}) custom-call(s32[3]{0:T(128)} %pad_add_fusion.1.refs_0_, bf16[256,512]{1,0:T(8,128)(2,1)} %bitcast.151, bf16[8,512]{1,0:T(8,128)(2,1)} %broadcast_in_dim.2.refs_2_, ...), custom_call_target="tpu_custom_call" | custom-call | flops 2415919104 | bytes 8053063 | tf_op jit(solution)/shard_map/pallas_call | solution.py:61
  123.4 4.4 %collective-permute-done.20.refs_12_ = bf16[16,576,128]{2,1,0:T(8,128)(2,1)S(1)} collective-permute-done((bf16[16,576,128]{2,1,0:T(8,128)(2,1)}, bf16[16,576,128]{2,1,0:T(8,128)(2,1)S(1)}, u32[]{:S(2)}, u32[]{:S(2)}) %collective-permute-start.20) | collective-permute-done | bytes 2359328 | tf_op jit(solution)/shard_map/ppermute | solution.py:823
  134.8 13.2 %shard_map.203 = (bf16[256,512]{1,0:T(8,128)(2,1)}, bf16[2,256,512]{2,1,0:T(8,128)(2,1)}, bf16[2,256,512]{2,1,0:T(8,128)(2,1)}) custom-call(s32[3]{0:T(128)} %pad_add_fusion.1.refs_0_, bf16[256,512]{1,0:T(8,128)(2,1)} %shard_map.199.refs_1_, bf16[2,256,512]{2,1,0:T(8,128)(2,1)} %get-tuple-element.62.refs_2_, bf16[2,256,512]{2,1,0:T(8,128)(2,1)} %copy-done.47, ...), custom_call_target="tpu_custom_call" | custom-call | flops 1677721600 | bytes 5592405 | tf_op jit(solution)/shard_map/pallas_call | solution.py:61
  159.8 10.8 %shard_map.204 = (bf16[16,384,128]{2,1,0:T(8,128)(2,1)}, bf16[16,384,128]{2,1,0:T(8,128)(2,1)}, f32[1,512]{1,0:T(1,128)}, bf16[768,512]{1,0:T(8,128)(2,1)}, bf16[8,512]{1,0:T(8,128)(2,1)}) custom-call(s32[3]{0:T(128)} %pad_add_fusion.1.refs_0_, f32[256,512]{1,0:T(8,128)} %get-tuple-element.60.refs_0_.refs_1_, bf16[256,512]{1,0:T(8,128)(2,1)} %get-tuple-element.70.refs_2_, ...), custom_call_target="tpu_custom_call" | custom-call | flops 1610612736 | bytes 5368709 | tf_op jit(solution)/shard_map/pallas_call | solution.py:61
  170.6 4.0 %collective-permute-start.23 = (bf16[16,384,128]{2,1,0:T(8,128)(2,1)}, bf16[16,384,128]{2,1,0:T(8,128)(2,1)}, u32[]{:S(2)}, u32[]{:S(2)}) collective-permute-start(bf16[16,384,128]{2,1,0:T(8,128)(2,1)} %get-tuple-element.82), channel_id=1, source_target_pairs={{0,1},{1,0},{2,3},{3,2},{4,5},{5,4},{6,7},{7,6},{8,9},{9,8},{10,11... | collective-permute-start | bytes 4718600 | tf_op jit(solution)/shard_map/ppermute | solution.py:823
  180.0 20.5 %shard_map.205 = (bf16[16,576,128]{2,1,0:T(8,128)(2,1)}, bf16[16,576,128]{2,1,0:T(8,128)(2,1)}, f32[1,512]{1,0:T(1,128)}, f32[768,512]{1,0:T(8,128)}, bf16[768,512]{1,0:T(8,128)(2,1)}) custom-call(s32[3]{0:T(128)} %pad_add_fusion.1.refs_0_, bf16[768,512]{1,0:T(8,128)(2,1)} %get-tuple-element.76.refs_1_, bf16[8,512]{1,0:T(8,128)(2,1)} %copy-done.48, ...), custom_call_target="tpu_custom_call" | custom-call | flops 7247757312 | bytes 24159192 | tf_op jit(solution)/shard_map/pallas_call | solution.py:61
  206.5 3.8 %collective-permute-done.49 = bf16[2,576,128]{2,1,0:T(8,128)(2,1)S(1)} collective-permute-done((bf16[2,576,128]{2,1,0:T(8,128)(2,1)S(1)}, bf16[2,576,128]{2,1,0:T(8,128)(2,1)S(1)}, u32[]{:S(2)}, u32[]{:S(2)}) %collective-permute-start.49) | collective-permute-done | bytes 294944 | tf_op jit(solution)/shard_map/ppermute | solution.py:823
  212.1 25.5 %shard_map.206 = (bf16[768,512]{1,0:T(8,128)(2,1)}, bf16[2,768,512]{2,1,0:T(8,128)(2,1)}, bf16[2,768,512]{2,1,0:T(8,128)(2,1)}) custom-call(s32[3]{0:T(128)} %pad_add_fusion.1.refs_0_, bf16[768,512]{1,0:T(8,128)(2,1)} %shard_map.195.refs_1_, bf16[2,768,512]{2,1,0:T(8,128)(2,1)} %get-tuple-element.56.refs_2_, bf16[2,768,512]{2,1,0:T(8,128)(2,1)} %copy-done.45, ...), custom_call_target="tpu_custom_call" | custom-call | flops 15099494400 | bytes 50331648 | tf_op jit(solution)/shard_map/pallas_call | solution.py:61
  240.6 9.6 %collective-permute-done.42 = bf16[4,384,128]{2,1,0:T(8,128)(2,1)S(1)} collective-permute-done((bf16[4,384,128]{2,1,0:T(8,128)(2,1)S(1)}, bf16[4,384,128]{2,1,0:T(8,128)(2,1)S(1)}, u32[]{:S(2)}, u32[]{:S(2)}) %collective-permute-start.42) | collective-permute-done | bytes 393248 | tf_op jit(solution)/shard_map/ppermute | solution.py:823
  259.1 14.4 %shard_map.207 = (bf16[16,256,128]{2,1,0:T(8,128)(2,1)}, bf16[16,256,128]{2,1,0:T(8,128)(2,1)}, f32[1,512]{1,0:T(1,128)}, bf16[768,512]{1,0:T(8,128)(2,1)}) custom-call(s32[3]{0:T(128)} %pad_add_fusion.1.refs_0_, bf16[768,512]{1,0:T(8,128)(2,1)} %get-tuple-element.54.refs_0_.refs_1_, bf16[768,512]{1,0:T(8,128)(2,1)} %get-tuple-element.83.refs_2_, ...), custom_call_target="tpu_custom_call" | custom-call | flops 2617245696 | bytes 8724152 | tf_op jit(solution)/shard_map/pallas_call | solution.py:61
  276.8 4.2 %collective-permute-done.38 = f32[4,512]{1,0:T(4,128)S(1)} collective-permute-done((f32[4,512]{1,0:T(4,128)S(1)}, f32[4,512]{1,0:T(4,128)S(1)}, u32[]{:S(2)}, u32[]{:S(2)}) %collective-permute-start.38) | collective-permute-done | bytes 8224 | tf_op jit(solution)/shard_map/ppermute | solution.py:823
  300.3 7.5 %collective-permute-done.29 = bf16[192,512]{1,0:T(8,128)(2,1)S(1)} collective-permute-done((bf16[192,512]{1,0:T(8,128)(2,1)S(1)}, bf16[192,512]{1,0:T(8,128)(2,1)S(1)}, u32[]{:S(2)}, u32[]{:S(2)}) %collective-permute-start.29) | collective-permute-done | bytes 196640 | tf_op jit(solution)/shard_map/ppermute | solution.py:797
  310.3 5.4 %collective-permute-done.47 = bf16[2,576,128]{2,1,0:T(8,128)(2,1)S(1)} collective-permute-done((bf16[2,576,128]{2,1,0:T(8,128)(2,1)S(1)}, bf16[2,576,128]{2,1,0:T(8,128)(2,1)S(1)}, u32[]{:S(2)}, u32[]{:S(2)}) %collective-permute-start.47) | collective-permute-done | bytes 294944 | tf_op jit(solution)/shard_map/ppermute | solution.py:823
  319.6 5.5 %collective-permute-done.48 = bf16[1,576,128]{2,1,0:T(8,128)(2,1)S(1)} collective-permute-done((bf16[1,576,128]{2,1,0:T(8,128)(2,1)S(1)}, bf16[1,576,128]{2,1,0:T(8,128)(2,1)S(1)}, u32[]{:S(2)}, u32[]{:S(2)}) %collective-permute-start.48) | collective-permute-done | bytes 147488 | tf_op jit(solution)/shard_map/ppermute | solution.py:823
  325.2 5.2 %collective-permute-done.33 = bf16[8,256,128]{2,1,0:T(8,128)(2,1)S(1)} collective-permute-done((bf16[8,256,128]{2,1,0:T(8,128)(2,1)S(1)}, bf16[8,256,128]{2,1,0:T(8,128)(2,1)S(1)}, u32[]{:S(2)}, u32[]{:S(2)}) %collective-permute-start.33) | collective-permute-done | bytes 524320 | tf_op jit(solution)/shard_map/ppermute | solution.py:823
  332.0 5.1 %collective-permute-done.34 = bf16[4,256,128]{2,1,0:T(8,128)(2,1)S(1)} collective-permute-done((bf16[4,256,128]{2,1,0:T(8,128)(2,1)S(1)}, bf16[4,256,128]{2,1,0:T(8,128)(2,1)S(1)}, u32[]{:S(2)}, u32[]{:S(2)}) %collective-permute-start.34) | collective-permute-done | bytes 262176 | tf_op jit(solution)/shard_map/ppermute | solution.py:823
  (288 shorter events, 127.5 us)
Async XLA Ops:
  19.7 14.7 %collective-permute-start.4 = (bf16[2,768,512]{2,1,0:T(8,128)(2,1)}, bf16[2,768,512]{2,1,0:T(8,128)(2,1)S(1)}, u32[]{:S(2)}, u32[]{:S(2)}) collective-permute-start(bf16[2,768,512]{2,1,0:T(8,128)(2,1)} %get-tuple-element.56.refs_2_), channel_id=1, source_target_pairs={{0,1},{1,0},{4,5},{5,4},{8,9},{9,8},{12,13},{13,12},{16,17},{17,16... | collective-permute-start | bytes 4718600 | tf_op jit(solution)/shard_map/ppermute | solution.py:816
  22.7 34.3 %collective-permute-start.8 = (bf16[64,512]{1,0:T(8,128)(2,1)S(1)}, bf16[64,512]{1,0:T(8,128)(2,1)S(1)}, u32[]{:S(2)}, u32[]{:S(2)}) collective-permute-start(bf16[64,512]{1,0:T(8,128)(2,1)S(1)} %get-tuple-element.139), channel_id=1, source_target_pairs={{0,24},{1,28},{4,25},{5,29},{8,16},{9,20},{12,17},{13,21},{16,8},{... | collective-permute-start | bytes 196616 | tf_op jit(solution)/shard_map/ppermute | solution.py:797
  26.0 31.0 %collective-permute-start.7 = (bf16[64,512]{1,0:T(8,128)(2,1)S(1)}, bf16[64,512]{1,0:T(8,128)(2,1)S(1)}, u32[]{:S(2)}, u32[]{:S(2)}) collective-permute-start(bf16[64,512]{1,0:T(8,128)(2,1)S(1)} %get-tuple-element.140), channel_id=1, source_target_pairs={{0,16},{1,20},{4,17},{5,21},{8,24},{9,28},{12,25},{13,29},{16,0},{... | collective-permute-start | bytes 196616 | tf_op jit(solution)/shard_map/ppermute | solution.py:797
  26.0 31.0 %collective-permute-start.6 = (bf16[64,512]{1,0:T(8,128)(2,1)S(1)}, bf16[64,512]{1,0:T(8,128)(2,1)S(1)}, u32[]{:S(2)}, u32[]{:S(2)}) collective-permute-start(bf16[64,512]{1,0:T(8,128)(2,1)S(1)} %get-tuple-element.141), channel_id=1, source_target_pairs={{0,8},{1,12},{4,9},{5,13},{8,0},{9,4},{12,1},{13,5},{16,24},{17,28... | collective-permute-start | bytes 196616 | tf_op jit(solution)/shard_map/ppermute | solution.py:797
  27.2 29.9 %collective-permute-start.5 = (bf16[64,512]{1,0:T(8,128)(2,1)S(1)}, bf16[64,512]{1,0:T(8,128)(2,1)S(1)}, u32[]{:S(2)}, u32[]{:S(2)}) collective-permute-start(bf16[64,512]{1,0:T(8,128)(2,1)S(1)} %get-tuple-element.142), channel_id=1, source_target_pairs={{0,0},{1,4},{4,1},{5,5},{8,8},{9,12},{12,9},{13,13},{16,16},{17,20... | collective-permute-start | bytes 196616 | tf_op jit(solution)/shard_map/ppermute | solution.py:797
  78.5 22.0 %collective-permute-start.11 = (bf16[192,512]{1,0:T(8,128)(2,1)S(1)}, bf16[192,512]{1,0:T(8,128)(2,1)S(1)}, u32[]{:S(2)}, u32[]{:S(2)}) collective-permute-start(bf16[192,512]{1,0:T(8,128)(2,1)S(1)} %get-tuple-element.109), channel_id=1, source_target_pairs={{0,8},{1,12},{4,9},{5,13},{8,0},{9,4},{12,1},{13,5},{16,24},{17,28... | collective-permute-start | bytes 589832 | tf_op jit(solution)/shard_map/ppermute | solution.py:797
  80.0 20.6 %collective-permute-start.12 = (bf16[192,512]{1,0:T(8,128)(2,1)S(1)}, bf16[192,512]{1,0:T(8,128)(2,1)S(1)}, u32[]{:S(2)}, u32[]{:S(2)}) collective-permute-start(bf16[192,512]{1,0:T(8,128)(2,1)S(1)} %get-tuple-element.110), channel_id=1, source_target_pairs={{0,0},{1,4},{4,1},{5,5},{8,8},{9,12},{12,9},{13,13},{16,16},{17,20... | collective-permute-start | bytes 589832 | tf_op jit(solution)/shard_map/ppermute | solution.py:797
  80.8 19.8 %collective-permute-start.10 = (bf16[192,512]{1,0:T(8,128)(2,1)S(1)}, bf16[192,512]{1,0:T(8,128)(2,1)S(1)}, u32[]{:S(2)}, u32[]{:S(2)}) collective-permute-start(bf16[192,512]{1,0:T(8,128)(2,1)S(1)} %get-tuple-element.111), channel_id=1, source_target_pairs={{0,16},{1,20},{4,17},{5,21},{8,24},{9,28},{12,25},{13,29},{16,0},{... | collective-permute-start | bytes 589832 | tf_op jit(solution)/shard_map/ppermute | solution.py:797
  83.3 17.4 %collective-permute-start.9 = (bf16[192,512]{1,0:T(8,128)(2,1)S(1)}, bf16[192,512]{1,0:T(8,128)(2,1)S(1)}, u32[]{:S(2)}, u32[]{:S(2)}) collective-permute-start(bf16[192,512]{1,0:T(8,128)(2,1)S(1)} %get-tuple-element.112), channel_id=1, source_target_pairs={{0,24},{1,28},{4,25},{5,29},{8,16},{9,20},{12,17},{13,21},{16,8},{... | collective-permute-start | bytes 589832 | tf_op jit(solution)/shard_map/ppermute | solution.py:797
  133.2 43.2 %collective-permute-start.22 = (bf16[8,576,128]{2,1,0:T(8,128)(2,1)S(1)}, bf16[8,576,128]{2,1,0:T(8,128)(2,1)S(1)}, u32[]{:S(2)}, u32[]{:S(2)}) collective-permute-start(bf16[8,576,128]{2,1,0:T(8,128)(2,1)S(1)} %slice.414), channel_id=1, source_target_pairs={{0,2},{1,3},{2,0},{3,1},{4,6},{5,7},{6,4},{7,5},{8,10},{9,11},{10,... | collective-permute-start | bytes 3538952 | tf_op jit(solution)/shard_map/ppermute | solution.py:823
  170.6 30.2 %collective-permute-start.23 = (bf16[16,384,128]{2,1,0:T(8,128)(2,1)}, bf16[16,384,128]{2,1,0:T(8,128)(2,1)}, u32[]{:S(2)}, u32[]{:S(2)}) collective-permute-start(bf16[16,384,128]{2,1,0:T(8,128)(2,1)} %get-tuple-element.82), channel_id=1, source_target_pairs={{0,1},{1,0},{2,3},{3,2},{4,5},{5,4},{6,7},{7,6},{8,9},{9,8},{10,11... | collective-permute-start | bytes 4718600 | tf_op jit(solution)/shard_map/ppermute | solution.py:823
  178.9 21.8 %collective-permute-start.25 = (bf16[4,576,128]{2,1,0:T(8,128)(2,1)S(1)}, bf16[4,576,128]{2,1,0:T(8,128)(2,1)S(1)}, u32[]{:S(2)}, u32[]{:S(2)}) collective-permute-start(bf16[4,576,128]{2,1,0:T(8,128)(2,1)S(1)} %slice.417), channel_id=1, source_target_pairs={{0,4},{4,0},{8,12},{12,8},{16,20},{20,16},{24,28},{28,24},{1,5},{5... | collective-permute-start | bytes 1769480 | tf_op jit(solution)/shard_map/ppermute | solution.py:823
  200.5 51.3 %collective-permute-start.27 = (bf16[16,576,128]{2,1,0:T(8,128)(2,1)}, bf16[16,576,128]{2,1,0:T(8,128)(2,1)S(1)}, u32[]{:S(2)}, u32[]{:S(2)}) collective-permute-start(bf16[16,576,128]{2,1,0:T(8,128)(2,1)} %get-tuple-element.88), channel_id=1, source_target_pairs={{0,1},{1,0},{2,3},{3,2},{4,5},{5,4},{6,7},{7,6},{8,9},{9,8},{10,11... | collective-permute-start | bytes 7077896 | tf_op jit(solution)/shard_map/ppermute | solution.py:823
  204.9 32.8 %collective-permute-start.26 = (bf16[8,384,128]{2,1,0:T(8,128)(2,1)}, bf16[8,384,128]{2,1,0:T(8,128)(2,1)S(1)}, u32[]{:S(2)}, u32[]{:S(2)}) collective-permute-start(bf16[8,384,128]{2,1,0:T(8,128)(2,1)} %slice.415), channel_id=1, source_target_pairs={{0,4},{4,0},{8,12},{12,8},{16,20},{20,16},{24,28},{28,24},{1,5},{5... | collective-permute-start | bytes 2359304 | tf_op jit(solution)/shard_map/ppermute | solution.py:823
  211.2 26.5 %collective-permute-start.50 = (bf16[1,576,128]{2,1,0:T(8,128)(2,1)S(1)}, bf16[1,576,128]{2,1,0:T(8,128)(2,1)S(1)}, u32[]{:S(2)}, u32[]{:S(2)}) collective-permute-start(bf16[1,576,128]{2,1,0:T(8,128)(2,1)S(1)} %slice.424), channel_id=1, source_target_pairs={{0,16},{4,20},{8,24},{12,28},{16,0},{20,4},{24,8},{28,12},{1,17},{... | collective-permute-start | bytes 442376 | tf_op jit(solution)/shard_map/ppermute | solution.py:823
  237.6 21.5 %collective-permute-start.24 = (bf16[2,768,512]{2,1,0:T(8,128)(2,1)}, bf16[2,768,512]{2,1,0:T(8,128)(2,1)}, u32[]{:S(2)}, u32[]{:S(2)}) collective-permute-start(bf16[2,768,512]{2,1,0:T(8,128)(2,1)} %get-tuple-element.85), channel_id=1, source_target_pairs={{0,1},{1,0},{4,5},{5,4},{8,9},{9,8},{12,13},{13,12},{16,17},{17,16... | collective-permute-start | bytes 4718600 | tf_op jit(solution)/shard_map/ppermute | solution.py:816
  253.5 28.9 %collective-permute-start.45 = (bf16[8,576,128]{2,1,0:T(8,128)(2,1)S(1)}, bf16[8,576,128]{2,1,0:T(8,128)(2,1)S(1)}, u32[]{:S(2)}, u32[]{:S(2)}) collective-permute-start(bf16[8,576,128]{2,1,0:T(8,128)(2,1)S(1)} %slice.413), channel_id=1, source_target_pairs={{0,2},{1,3},{2,0},{3,1},{4,6},{5,7},{6,4},{7,5},{8,10},{9,11},{10,... | collective-permute-start | bytes 3538952 | tf_op jit(solution)/shard_map/ppermute | solution.py:823
  257.0 17.4 %collective-permute-start.44 = (bf16[1,384,128]{2,1,0:T(8,128)(2,1)S(1)}, bf16[1,384,128]{2,1,0:T(8,128)(2,1)S(1)}, u32[]{:S(2)}, u32[]{:S(2)}) collective-permute-start(bf16[1,384,128]{2,1,0:T(8,128)(2,1)S(1)} %slice.427), channel_id=1, source_target_pairs={{0,16},{4,20},{8,24},{12,28},{16,0},{20,4},{24,8},{28,12},{1,17},{... | collective-permute-start | bytes 294920 | tf_op jit(solution)/shard_map/ppermute | solution.py:823
  282.7 15.3 %collective-permute-start.46 = (bf16[4,576,128]{2,1,0:T(8,128)(2,1)S(1)}, bf16[4,576,128]{2,1,0:T(8,128)(2,1)S(1)}, u32[]{:S(2)}, u32[]{:S(2)}) collective-permute-start(bf16[4,576,128]{2,1,0:T(8,128)(2,1)S(1)} %slice.416), channel_id=1, source_target_pairs={{0,4},{4,0},{8,12},{12,8},{16,20},{20,16},{24,28},{28,24},{1,5},{5... | collective-permute-start | bytes 1769480 | tf_op jit(solution)/shard_map/ppermute | solution.py:823
  292.7 15.1 %collective-permute-start.29 = (bf16[192,512]{1,0:T(8,128)(2,1)S(1)}, bf16[192,512]{1,0:T(8,128)(2,1)S(1)}, u32[]{:S(2)}, u32[]{:S(2)}) collective-permute-start(bf16[192,512]{1,0:T(8,128)(2,1)S(1)} %get-tuple-element.103), channel_id=1, source_target_pairs={{0,16},{1,20},{4,17},{5,21},{8,24},{9,28},{12,25},{13,29},{16,0},{... | collective-permute-start | bytes 589832 | tf_op jit(solution)/shard_map/ppermute | solution.py:797
  293.8 14.0 %collective-permute-start.28 = (bf16[192,512]{1,0:T(8,128)(2,1)S(1)}, bf16[192,512]{1,0:T(8,128)(2,1)S(1)}, u32[]{:S(2)}, u32[]{:S(2)}) collective-permute-start(bf16[192,512]{1,0:T(8,128)(2,1)S(1)} %get-tuple-element.104), channel_id=1, source_target_pairs={{0,24},{1,28},{4,25},{5,29},{8,16},{9,20},{12,17},{13,21},{16,8},{... | collective-permute-start | bytes 589832 | tf_op jit(solution)/shard_map/ppermute | solution.py:797
  298.1 17.8 %collective-permute-start.32 = (bf16[16,256,128]{2,1,0:T(8,128)(2,1)S(1)}, bf16[16,256,128]{2,1,0:T(8,128)(2,1)S(1)}, u32[]{:S(2)}, u32[]{:S(2)}) collective-permute-start(bf16[16,256,128]{2,1,0:T(8,128)(2,1)S(1)} %copy-done.46), channel_id=1, source_target_pairs={{0,1},{1,0},{2,3},{3,2},{4,5},{5,4},{6,7},{7,6},{8,9},{9,8},{10,11... | collective-permute-start | bytes 3145736 | tf_op jit(solution)/shard_map/ppermute | solution.py:823
  299.8 15.9 %collective-permute-start.47 = (bf16[2,576,128]{2,1,0:T(8,128)(2,1)S(1)}, bf16[2,576,128]{2,1,0:T(8,128)(2,1)S(1)}, u32[]{:S(2)}, u32[]{:S(2)}) collective-permute-start(bf16[2,576,128]{2,1,0:T(8,128)(2,1)S(1)} %slice.421), channel_id=1, source_target_pairs={{0,8},{4,12},{8,0},{12,4},{16,24},{20,28},{24,16},{28,20},{1,9},{5... | collective-permute-start | bytes 884744 | tf_op jit(solution)/shard_map/ppermute | solution.py:823
  316.2 14.2 %collective-permute-start.33 = (bf16[8,256,128]{2,1,0:T(8,128)(2,1)S(1)}, bf16[8,256,128]{2,1,0:T(8,128)(2,1)S(1)}, u32[]{:S(2)}, u32[]{:S(2)}) collective-permute-start(bf16[8,256,128]{2,1,0:T(8,128)(2,1)S(1)} %slice.418), channel_id=1, source_target_pairs={{0,4},{4,0},{8,12},{12,8},{16,20},{20,16},{24,28},{28,24},{1,5},{5... | collective-permute-start | bytes 1572872 | tf_op jit(solution)/shard_map/ppermute | solution.py:823
  (78 other events, 557.4 us)

commit v3 on v2

v3 whole, which is shorter than its diff:
```python
import functools

import jax
import jax.numpy as jnp
from jax import lax
from jax.experimental import pallas as pl
from jax.experimental.pallas import tpu as pltpu
from jax.sharding import PartitionSpec as P

D = 512
H = 8
DH = 64

epsilon = 1e-05
masked_score = -1e30
AXES = ("seq", "batch")


VOCAB = 256
BF16 = jnp.bfloat16
F32 = jnp.float32
ANYWHERE = pl.BlockSpec(memory_space=pl.ANY)
ROOM = 56 * 1024 * 1024


def dot(left, right):
    return jnp.dot(left, right, preferred_element_type=F32)


def dot_nt(left, right):
    return lax.dot_general(left, right, (((1,), (1,)), ((), ())), preferred_element_type=F32)


def iota(shape, dim):
    return lax.broadcasted_iota(jnp.int32, shape, dim)


def picks(condition):
    return jnp.where(condition, 1.0, 0.0).astype(BF16)


def call(kernel, out_shape, grid, in_specs, out_specs, scratch=(), scalars=0):
    return pl.pallas_call(
        kernel,
        out_shape=out_shape,
        grid_spec=pltpu.PrefetchScalarGridSpec(
            num_scalar_prefetch=scalars,
            grid=grid,
            in_specs=in_specs,
            out_specs=out_specs,
            scratch_shapes=scratch,
        ),
        compiler_params=pltpu.CompilerParams(vmem_limit_bytes=ROOM),
    )


def shape(dims, dtype):
    return jax.ShapeDtypeStruct(dims, dtype)


def fixed(block, index=None, buffers=1):
    place = index or (0,) * len(block)
    return pl.BlockSpec(block, lambda *unused: place, pipeline_mode=pl.Buffered(buffers))


def gain_row(ref, layer):
    return ref[...].astype(F32)[layer : layer + 1]


def normalize(inputs, gain):
    centred = inputs - jnp.mean(inputs, -1, keepdims=True)
    inverse = lax.rsqrt(jnp.mean(centred * centred, -1, keepdims=True) + epsilon)
    normed = centred * inverse
    return ((normed * gain).astype(BF16), normed, inverse)


def normalize_back(grad, normed, inverse, gain):
    scaled = grad * gain
    result = inverse * (
        scaled
        - jnp.mean(scaled, -1, keepdims=True)
        - normed * jnp.mean(scaled * normed, -1, keepdims=True)
    )
    return (result, jnp.sum(grad * normed, axis=0, keepdims=True))


def rotate(inputs, table, back=False):
    width = inputs.shape[1]
    turned = pltpu.roll(table, DH, 1)
    early = iota(table.shape, 1) < DH
    cosine, sine = jnp.where(early, table, turned), jnp.where(early, turned, table)
    if back:
        sine = -sine
    count = width // 128
    first = iota(inputs.shape, 1) % DH < DH // 2
    other = jnp.where(
        first, pltpu.roll(inputs, width - DH // 2, 1), pltpu.roll(inputs, DH // 2, 1)
    )
    return inputs * jnp.concatenate([cosine] * count, 1) + other * jnp.concatenate([sine] * count, 1)


def gelu_both(hidden):
    scale = 0.7978845608028654
    square = hidden * hidden
    tanh = jnp.tanh(scale * hidden * (1.0 + 0.044715 * square))
    half = 0.5 + 0.5 * tanh
    slope = half + (0.5 * scale) * hidden * (1.0 - tanh * tanh) * (1.0 + 0.134145 * square)
    return (hidden * half, slope)


def layout(blocks):
    starts, at = [], 0
    for deep, wide in blocks:
        starts.append(at)
        at += deep * -(-wide // 128)
    return starts, at


def unpacked(slot, blocks):
    made = []
    for (deep, wide), start in zip(blocks, layout(blocks)[0]):
        tiles = [
            slot[start + tile * deep : start + (tile + 1) * deep, : min(128, wide - tile * 128)]
            for tile in range(-(-wide // 128))
        ]
        made.append(tiles[0] if len(tiles) == 1 else jnp.concatenate(tiles, 1))
    return made


def slot_of(order, axis, place, own):
    if all(name != axis for name, bit in order):
        return place << len(order)
    slot, apart = 0, place ^ own
    for number, (name, bit) in enumerate(order):
        if name == axis:
            slot = slot + ((apart // bit) % 2) * (1 << (len(order) - 1 - number))
    return slot


class Packs:
    def __init__(self, batches, seqs, order, blocks):
        self.batches, self.seqs, self.order, self.blocks = batches, seqs, order, blocks
        self.starts, self.rows = layout(blocks)
        self.slots = batches * seqs
        self.whole = len(order) < 2 or batches * seqs != 1 << len(order)

    def put(self, packed, slot, start, block):
        deep, wide = block.shape
        for tile in range(-(-wide // 128)):
            piece = block[:, tile * 128 : min(wide, (tile + 1) * 128)]
            first = pl.multiple_of(slot * self.rows + (start + tile * deep), 16)
            packed[pl.ds(first, deep), : piece.shape[1]] = piece

    def put_block(self, packed, me, number, batch, seq, block):
        if self.order:
            slot = slot_of(self.order, "batch", batch, me[1]) + slot_of(self.order, "seq", seq, me[2])
        else:
            slot = batch * self.seqs + seq
        self.put(packed, slot, self.starts[number], block)

    def put_all(self, packed, me, number, made, swapped):
        deep, wide = self.blocks[number]
        for line in range(made.shape[0] // deep):
            for column in range(made.shape[1] // wide):
                batch, seq = (column, line) if swapped else (line, column)
                block = made[line * deep : (line + 1) * deep, column * wide : (column + 1) * wide]
                self.put_block(packed, me, number, batch, seq, block)

    def hand_out(self, packed, outs, sems):
        copies, at = [], 0
        for number, out in enumerate(outs):
            copies.append(pltpu.make_async_copy(packed.at[pl.ds(at, out.shape[0])], out, sems.at[number]))
            at += out.shape[0]
        for copy in copies:
            copy.start()
        for copy in copies:
            copy.wait()

    def send(self, packed, outs, moves, first, last):
        for slot in range(self.slots):
            at, out = slot * self.rows, outs[0]
            to = at
            if len(outs) == 2 and slot >= self.slots // 2:
                to, out = at - self.slots // 2 * self.rows, outs[1]
            rows = last - first
            moves.start(packed.at[pl.ds(at + first, rows)], out.at[pl.ds(to + first, rows)])

    def shapes(self, extra=0):
        if self.whole:
            return (shape((self.slots * self.rows, 128), BF16),)
        half = self.slots * self.rows // 2
        return (shape((half, 128), BF16), shape((half + extra, 128), BF16))

    def specs(self):
        return (ANYWHERE,) * len(self.shapes())

    def scratch(self, extra=0):
        return [pltpu.VMEM((self.slots * self.rows + extra, 128), BF16), pltpu.SemaphoreType.DMA((2,))]


def in_two(value):
    high = value.astype(BF16)
    return high, (value - high.astype(F32)).astype(BF16)


def halve_kernel(kept, got, sums, stays, leaves, made):
    size = kept.shape[0]
    half = size // 2
    stays[...] = (kept[:half, :].astype(F32) + got[:half, :].astype(F32)).astype(BF16)
    leaves[:half, :] = (kept[half:, :].astype(F32) + got[half:size, :].astype(F32)).astype(BF16)
    made[...] = add_sums(sums[...], got, size)
    high, low = in_two(made[...])
    leaves[half : half + high.shape[0], :] = high
    leaves[half + high.shape[0] :, :] = low


def add_sums(own, got, at):
    count = own.shape[0]
    high, low = in_two(own)
    own = high.astype(F32) + low.astype(F32)
    return own + (got[at : at + count, :].astype(F32) + got[at + count : at + 2 * count, :].astype(F32))


def halve_call(kept, got, sums):
    half = kept.shape[0] // 2
    operands = (kept, got, sums)
    outs = (
        shape((half, 128), BF16),
        shape((half + 2 * sums.shape[0], 128), BF16),
        shape(sums.shape, F32),
    )
    return call(
        halve_kernel,
        outs,
        grid=(1,),
        in_specs=[fixed(each.shape) for each in operands],
        out_specs=tuple(fixed(each.shape) for each in outs),
    )(*operands)


def spread_kernel(kept, got, sums, own, made, *leaves):
    size, rows = kept.shape[0], own.shape[0]
    made[...] = add_sums(sums[...], got, size)
    high, low = in_two(made[...])
    for slot in range(size // rows):
        lines = slice(slot * rows, (slot + 1) * rows)
        value = (kept[lines, :].astype(F32) + got[lines, :].astype(F32)).astype(BF16)
        if slot == 0:
            own[...] = value
        else:
            out = leaves[slot - 1]
            out[:rows, :] = value
            out[rows : rows + high.shape[0], :] = high
            out[rows + high.shape[0] :, :] = low


def spread_call(rows, kept, got, sums):
    operands = (kept, got, sums)
    outs = (shape((rows, 128), BF16), shape(sums.shape, F32))
    outs += (shape((rows + 2 * sums.shape[0], 128), BF16),) * (kept.shape[0] // rows - 1)
    made = call(
        spread_kernel,
        outs,
        grid=(1,),
        in_specs=[fixed(each.shape) for each in operands],
        out_specs=tuple(fixed(each.shape) for each in outs),
    )(*operands)
    return made[0], made[1], made[2:]


def pairwise(values):
    while len(values) > 1:
        values = [values[n] + values[n + 1] for n in range(0, len(values), 2)]
    return values[0]


def finish_kernel(layouts, counts, *refs):
    terms = []
    for count in counts:
        terms.append(sum([ref[...].astype(F32) for ref in refs[:count]]))
        refs = refs[count:]
    qkv_0, sums, *came = refs[:-8]
    qkv_out, out_out, up_out, down_out, pool_out, embed_out, gain_attn, gain_ffn = refs[-8:]
    for number in range(2):
        up_out[number], down_out[number], out_out[number] = unpacked(terms[number], layouts[0])
    qkv_out[1], pool_out[...] = unpacked(terms[2], layouts[1])
    at, count = qkv_0.shape[0], sums.shape[0]
    slot = pairwise([each[:at, :].astype(F32) for each in (qkv_0, *came)])
    qkv_out[0], embed_out[...] = unpacked(slot, layouts[2])
    high, low = in_two(sums[...])
    made = [high.astype(F32) + low.astype(F32)]
    for each in came:
        made.append(each[at : at + count, :].astype(F32) + each[at + count :, :].astype(F32))
    made = pairwise(made)
    tiles = D // 128
    for number, ref in enumerate((gain_attn, gain_attn, gain_ffn, gain_ffn)):
        for tile in range(tiles):
            place = number * tiles + tile
            ref[number % 2 : number % 2 + 1, tile * 128 : (tile + 1) * 128] = made[place : place + 1, :]


def finish_call(layouts, terms, *rest):
    (up, down, out), (qkv, pool), (unused, embed) = layouts
    dims = [(2,) + qkv, (2,) + out, (2,) + up, (2,) + down, pool, embed, (2, D), (2, D)]
    specs = []
    for number, group in enumerate(terms):
        specs += [fixed((layout(layouts[number // 2])[1], 128))] * len(group)
    return call(
        functools.partial(finish_kernel, layouts, [len(group) for group in terms]),
        tuple(shape(each, F32) for each in dims),
        grid=(1,),
        in_specs=specs + [fixed(each.shape) for each in rest],
        out_specs=tuple(fixed(each) for each in dims),
    )(*sum(terms, []), *rest)


def embed_kernel(layer, tokens, embed, gain, w_qkv, table, inputs, low, both):
    part = pl.program_id(0)

    @pl.when(part == 0)
    def first():
        onehot = picks(tokens[...] == iota((tokens.shape[0], embed.shape[0]), 1))
        value = dot(onehot, embed[...])
        inputs[...] = value.astype(BF16)
        low[...] = normalize(value, gain_row(gain, layer))[0]

    joined = dot(low[...], w_qkv[0])

    @pl.when(part == 0)
    def keys():
        both[0] = rotate(joined, table[...]).astype(BF16)

    @pl.when(part == 1)
    def values():
        both[0] = joined.astype(BF16)


def embed_call(layer, tokens, embed, gain, w_qkv, table):
    count = tokens.shape[0]
    return call(
        functools.partial(embed_kernel, layer),
        (shape((count, D), BF16), shape((count, D), BF16), shape((2, count, D), BF16)),
        grid=(2,),
        in_specs=[
            fixed(tokens.shape),
            fixed(embed.shape),
            fixed(gain.shape),
            pl.BlockSpec((1, D, D), lambda part: (layer, 0, part + 1)),
            fixed(table.shape),
        ],
        out_specs=(
            fixed((count, D)),
            fixed((count, D)),
            pl.BlockSpec((1, count, D), lambda part: (part, 0, 0)),
        ),
    )(tokens, embed, gain, w_qkv, table)


def pool_kernel(layer, rows, members, me, first, edge, w_pool, gain, w_qkv, table, grouped, pooled, low, both):
    span = first.shape[0] // rows
    count = pooled.shape[0]
    short = count // rows
    late = jnp.where(me[0] == 0, 1, 0)
    total = jnp.zeros((count, D), F32)
    for third in range(3):
        pick = picks(iota((short, span), 1) == 3 * iota((short, span), 0) + third - 2)
        piece = jnp.concatenate(
            [dot(pick, first[row * span : (row + 1) * span, :]) for row in range(rows)], 0
        )
        if third < 2:
            place = iota((count, 2 * rows), 0) == (iota((count, 2 * rows), 1) // 2 + late) * short
            place = picks(place & (iota((count, 2 * rows), 1) % 2 == third))
            piece = piece + dot(place, edge[...])
        piece = piece.astype(BF16)
        grouped[:, third * D : (third + 1) * D] = piece
        total = total + dot(piece, w_pool[third * D : (third + 1) * D, :])
    pooled[...] = total
    low[...] = normalize(total, gain_row(gain, layer))[0]
    both[0] = rotate(dot(low[...], w_qkv[0, :, D : 2 * D]), table[...]).astype(BF16)
    both[1] = dot(low[...], w_qkv[0, :, 2 * D :]).astype(BF16)


def pool_call(layer, rows, members, me, first, edge, w_pool, gain, w_qkv, table):
    count = table.shape[0]
    return call(
        functools.partial(pool_kernel, layer, rows, members),
        (
            shape((count, 3 * D), BF16),
            shape((count, D), F32),
            shape((count, D), BF16),
            shape((2, count, D), BF16),
        ),
        grid=(1,),
        scalars=1,
        in_specs=[
            fixed(first.shape),
            fixed(edge.shape),
            fixed(w_pool.shape),
            fixed(gain.shape),
            fixed((1, D, 3 * D), (layer, 0, 0)),
            fixed(table.shape),
        ],
        out_specs=(fixed((count, 3 * D)), fixed((count, D)), fixed((count, D)), fixed((2, count, D))),
    )(me, first, edge, w_pool, gain, w_qkv, table)


GROUP = 256
HEADS = GROUP // DH


def fill_keys(rows, members, own, others, keys, values):
    span = own.shape[1] // rows
    for row in range(rows):
        for by, source in enumerate([own, *others]):
            start = (row * members + by) * span
            keys[start : start + span, :] = source[0, row * span : (row + 1) * span, :]
            values[start : start + span, :] = source[1, row * span : (row + 1) * span, :]


def tiles_of(rows, members, span):
    step = min(rows, max(1, 256 // span))
    return [(first, min(rows, first + step)) for first in range(0, rows, step)]


def heads_at_once(rows, members, span):
    size = sum((last - first) * span * last * members * span * 4 for first, last in tiles_of(rows, members, span))
    return max(count for count in (1, 2, HEADS) if count == 1 or count * size <= 12 << 20)


def bias_shape(rows, members, span):
    first, last = tiles_of(rows, members, span)[0]
    return ((last - first) * span, (last - first) * members * span)


def turned_shape(rows, members, span):
    tiles = tiles_of(rows, members, span)
    return (len(tiles), GROUP, rows * span)


def fill_bias(member, members, span, bias):
    line, column = iota(bias.shape, 0), iota(bias.shape, 1)
    width = members * span
    by = column % width // span
    own = (by == 0) & (column % span <= line % span)
    same = own | ((by > 0) & ((member + by) % members < member))
    seen = (column // width < line // span) | ((column // width == line // span) & same)
    bias[...] = jnp.where(seen, 0.0, masked_score)


def score(query, keys, bias, start, end):
    scores = dot_nt(query, keys[0:end, :])
    last = scores[:, start:] + bias[...]
    return jnp.concatenate([scores[:, :start], last], 1) if start else last


def attention_part(rows, members, queries, own, *refs):
    others = refs[: members - 1]
    mixed, logsum, keys, values, bias, total = refs[members - 1 :]
    span = queries.shape[0] // rows
    width = members * span
    tiles = tiles_of(rows, members, span)
    fill_keys(rows, members, own, others, keys, values)
    logsum[...] = jnp.zeros_like(logsum)

    at_once = heads_at_once(rows, members, span)

    def some_heads(turn, unused):
        todo = []
        for number in range(at_once):
            head = turn * at_once + number
            lanes = iota((1, GROUP), 1) // DH == head
            mask = picks(lanes)
            for first, last in tiles:
                block = slice(first * span, last * span)
                todo.append((head, lanes, mask, block, first * width, last * width))
        scores = [
            score(queries[block, :] * mask, keys, bias, start, end)
            for head, lanes, mask, block, start, end in todo
        ]
        highest = [jnp.max(value, -1, keepdims=True) for value in scores]
        expon = [jnp.exp(value - most) for value, most in zip(scores, highest)]
        totals = [jnp.sum(value, -1, keepdims=True) for value in expon]
        outs = [
            dot(value.astype(BF16), values[0:end, :]) * (1.0 / whole)
            for value, whole, (head, lanes, mask, block, start, end) in zip(expon, totals, todo)
        ]
        for (head, lanes, mask, block, start, end), out, most, whole in zip(todo, outs, highest, totals):
            total[block, :] = jnp.where(lanes, out, total[block, :])
            here = iota((out.shape[0], 128), 1) == head
            logsum[0, block, :] = jnp.where(here, most + jnp.log(whole), logsum[0, block, :])
        return unused

    lax.fori_loop(0, HEADS // at_once, some_heads, 0)
    mixed[...] = total[...].astype(BF16)


def lane_group(ndim, block, base=0):
    return pl.BlockSpec(block, lambda group, *unused: (0,) * (ndim - 1) + (group + base,))


def lane_part(ref, group):
    lanes = pl.ds(group * GROUP, GROUP)
    return ref.at[:, lanes] if len(ref.shape) == 2 else ref.at[:, :, lanes]


def attention_scratch(rows, members, count):
    span = count // rows
    return [
        pltpu.VMEM((members * count, GROUP), BF16),
        pltpu.VMEM((members * count, GROUP), BF16),
        pltpu.VMEM(bias_shape(rows, members, span), F32),
        pltpu.VMEM((count, GROUP), F32),
    ]


def attention_back_scratch(rows, members, count):
    span = count // rows
    return [
        pltpu.VMEM(turned_shape(rows, members, span), BF16),
        pltpu.VMEM(turned_shape(rows, members, span), BF16),
        pltpu.VMEM((GROUP, members * count), F32),
        pltpu.VMEM((GROUP, members * count), F32),
    ]


def attention_back_kernel(rows, members, me, queries, own, *refs):
    fill_bias(me[0], members, queries.shape[0] // rows, refs[-6])
    attention_back_part(rows, members, queries, own, *refs)


def attention_back_part(rows, members, queries, own, *refs):
    others = refs[: members - 1]
    mixed, logsum, grad_mixed, grad_queries, *rest = refs[members - 1 :]
    pieces = rest[:members]
    keys, values, bias, total, turned, turned_grad, grad_keys, grad_values = rest[members:]
    span = queries.shape[0] // rows
    width = members * span
    fill_keys(rows, members, own, others, keys, values)
    tiles = tiles_of(rows, members, span)
    for tile, (first, last) in enumerate(tiles):
        lines = (rows - first) * span
        turned[tile, :, 0:lines] = queries[first * span :, :].T
        turned_grad[tile, :, 0:lines] = grad_mixed[first * span :, :].T

    at_once = heads_at_once(rows, members, span)

    def some_heads(turn, unused):
        todo = []
        for number in range(at_once):
            head = turn * at_once + number
            lanes = iota((1, GROUP), 1) // DH == head
            for tile, (first, last) in enumerate(tiles):
                block = slice(first * span, last * span)
                todo.append((head, lanes, picks(lanes), tile, block, first * width, last * width))
        grads = [grad_mixed[block, :] * mask for head, lanes, mask, tile, block, start, end in todo]
        scores = [
            score(queries[block, :] * mask, keys, bias, start, end)
            for head, lanes, mask, tile, block, start, end in todo
        ]
        grad_probs = [dot_nt(grad, values[0 : each[-1], :]) for grad, each in zip(grads, todo)]
        sums = [
            jnp.sum(
                jnp.where(iota((block.stop - block.start, 128), 1) == head, logsum[0, block, :], 0.0),
                -1,
                keepdims=True,
            )
            for head, lanes, mask, tile, block, start, end in todo
        ]
        deltas = [
            jnp.sum(grad.astype(F32) * mixed[each[4], :].astype(F32), -1, keepdims=True)
            for grad, each in zip(grads, todo)
        ]
        probs = [jnp.exp(value - whole) for value, whole in zip(scores, sums)]
        grad_scores = [
            (prob * (grad - delta)).astype(BF16) for prob, grad, delta in zip(probs, grad_probs, deltas)
        ]
        for each, grad in zip(todo, grad_scores):
            head, lanes, mask, tile, block, start, end = each
            total[block, :] = jnp.where(lanes, dot(grad, keys[0:end, :]), total[block, :])
        count = len(tiles)
        for number in range(at_once):
            mine = pl.ds(pl.multiple_of((turn * at_once + number) * DH, DH), DH)
            for tile, (first, last) in enumerate(tiles):
                columns = slice(first * width, last * width)
                lines = (rows - first) * span
                for source, made, into in (
                    (turned, grad_scores, grad_keys),
                    (turned_grad, probs, grad_values),
                ):
                    later = made[number * count + tile : (number + 1) * count]
                    stack = jnp.concatenate([value[:, columns].astype(BF16) for value in later], 0)
                    into[mine, columns] = dot(source[tile, mine, 0:lines], stack)
        return unused

    lax.fori_loop(0, HEADS // at_once, some_heads, 0)
    grad_queries[...] = total[...].astype(BF16)
    for number, source in enumerate((grad_keys, grad_values)):
        made = source[...].astype(BF16).T
        for row in range(rows):
            for by, piece in enumerate(pieces):
                start = (row * members + by) * span
                piece[number, row * span : (row + 1) * span, :] = made[start : start + span, :]


def attention_back_call(rows, members, me, queries, own, others, mixed, logsum, grad_mixed, groups):
    count = queries.shape[0]
    base, wide = groups[0], len(groups) * GROUP
    made = call(
        functools.partial(attention_back_kernel, rows, members),
        (shape((count, wide), BF16),) + (shape((2, count, wide), BF16),) * members,
        grid=(len(groups),),
        scalars=1,
        in_specs=[lane_group(2, (count, GROUP), base)]
        + [lane_group(3, (2, count, GROUP), base)] * members
        + [
            lane_group(2, (count, GROUP), base),
            pl.BlockSpec((1, count, 128), lambda group, *unused: (group + base, 0, 0)),
            lane_group(2, (count, GROUP), base),
        ],
        out_specs=(lane_group(2, (count, GROUP)),) + (lane_group(3, (2, count, GROUP)),) * members,
        scratch=attention_scratch(rows, members, count) + attention_back_scratch(rows, members, count),
    )(me, queries, own, *others, mixed, logsum, grad_mixed)
    return (made[0], made[1:])


CHUNK = 512


class Moves:
    def __init__(self, sems, first=0):
        self.sems, self.taken, self.open = sems, first, []

    def start(self, source, target):
        copy = pltpu.make_async_copy(source, target, self.sems.at[self.taken])
        copy.start()
        self.open.append(copy)
        self.taken += 1
        return copy

    def end(self):
        for copy in self.open:
            copy.wait()
        self.open = []


class Weights:
    def __init__(self, sems, layer, sources, held):
        self.sems, self.layer, self.sources, self.held = sems, layer, sources, held
        self.chunks = held[1].shape[1] // CHUNK
        self.copies = 1 + 2 * self.chunks

    def pair(self, name, part=0):
        (w_out, w_up, w_down), (out, up, down) = self.sources, self.held
        if name == "out":
            return w_out.at[self.layer], out
        lines = pl.ds(pl.multiple_of(part * CHUNK, CHUNK), CHUNK)
        if name == "up":
            return w_up.at[self.layer, :, lines], up.at[:, lines]
        return w_down.at[self.layer, lines, :], down.at[lines, :]

    def copy(self, name, part=0):
        place = {"out": 0, "up": 1, "down": 2}[name] + 2 * part
        return pltpu.make_async_copy(*self.pair(name, part), self.sems.at[place])

    def start(self):
        self.copy("out").start()
        for part in range(self.chunks):
            self.copy("up", part).start()
            self.copy("down", part).start()

    def wait(self, name, part=0):
        self.copy(name, part).wait()

    def get(self, name, part=0):
        return self.pair(name, part)[1][...]


def weight_scratch(units):
    return [pltpu.VMEM((D, D), BF16), pltpu.VMEM((D, units), BF16), pltpu.VMEM((units, D), BF16)]


def edge_rows(made, rows):
    count = made.shape[0]
    span = count // rows
    line = iota((2 * rows, count), 0)
    pick = picks(iota((2 * rows, count), 1) == (line // 2 + 1) * span - 2 + line % 2)
    return dot(pick, made).astype(BF16)


def make_queries(low, w_qkv, table):
    joined = dot(low[...], w_qkv[0])
    return (rotate(joined, table[...]) * DH ** (-0.5)).astype(BF16)


def attend(rows, members, me, queries, own, others, mixed, logsum, scratch):
    fill_bias(me[0], members, queries.shape[0] // rows, scratch[2])
    for group in range(D // GROUP):
        sources = [lane_part(each, group) for each in (queries, own, *others, mixed)]
        attention_part(rows, members, *sources, logsum.at[pl.ds(group, 1)], *scratch)


def forward_kernel(layer, rows, members, me, inputs, low, own, *refs):
    others = refs[: members - 1]
    (
        table, gain, w_qkv, w_out, w_up, w_down,
        output, edges, queries_out, mixed_out, logsum_out, middle_out, hidden_out,
        queries, mixed, logsum, middle, hidden, low_now, sum_now, *scratch,
    ) = refs[members - 1 :]
    held, attention, sems = scratch[:3], scratch[3:7], scratch[7]
    weights = Weights(sems, layer, (w_out, w_up, w_down), held)
    moves = Moves(sems, weights.copies)
    weights.start()
    queries[...] = make_queries(low, w_qkv, table)
    moves.start(queries, queries_out)
    attend(rows, members, me, queries, own, others, mixed, logsum, attention)
    moves.start(mixed, mixed_out)
    moves.start(logsum, logsum_out)
    weights.wait("out")
    total = inputs[...].astype(F32) + dot(mixed[...], weights.get("out"))
    middle[...] = total
    moves.start(middle, middle_out)
    normed = normalize(total, gain_row(gain, layer))[0]
    low_now[...] = normed
    sum_now[...] = total

    def one_part(part, unused):
        weights.wait("up", part)
        made = dot(low_now[...], weights.get("up", part))
        lanes = pl.ds(pl.multiple_of(part * CHUNK, CHUNK), CHUNK)
        hidden[:, lanes] = made.astype(BF16)
        weights.wait("down", part)
        sum_now[...] += dot(gelu_both(made)[0].astype(BF16), weights.get("down", part))
        return unused

    lax.fori_loop(0, weights.chunks, one_part, 0)
    moves.start(hidden, hidden_out)
    made = sum_now[...].astype(BF16)
    output[...] = made
    edges[...] = edge_rows(made, rows)
    moves.end()


def forward_call(layer, rows, members, me, inputs, low, own, others, table, gain, w_qkv, w_out, w_up, w_down):
    count = inputs.shape[0]
    units = w_up.shape[2]
    handed = [
        ((count, D), BF16), ((count, D), BF16), ((D // GROUP, count, 128), F32),
        ((count, D), F32), ((count, units), BF16),
    ]
    return call(
        functools.partial(forward_kernel, layer, rows, members),
        (shape((count, D), BF16), shape((2 * rows, D), BF16)) + tuple(shape(*each) for each in handed),
        grid=(1,),
        scalars=1,
        in_specs=[fixed((count, D))] * 2
        + [fixed((2, count, D))] * members
        + [fixed(table.shape), fixed(gain.shape), fixed((1, D, D), (layer, 0, 0))]
        + [ANYWHERE] * 3,
        out_specs=(fixed((count, D)), fixed((2 * rows, D))) + (ANYWHERE,) * len(handed),
        scratch=[pltpu.VMEM(*each) for each in handed]
        + [pltpu.VMEM((count, D), BF16), pltpu.VMEM((count, D), F32)]
        + weight_scratch(units)
        + attention_scratch(rows, members, count)
        + [pltpu.SemaphoreType.DMA((6 + 2 * (units // CHUNK),))],
    )(me, inputs, low, own, *others, table, gain, w_qkv, w_out, w_up, w_down)


def ffn_blocks(batches, seqs, units):
    return ((D // batches, units // seqs), (D // seqs, units // batches), (D // seqs, D // batches))


def ffn_back(layer, packs, me, middle, mixed, parts, weights, gain, packed, outs, moves, scratch, unroll):
    grad, turned_low, turned_grad, total = scratch
    row = gain_row(gain, layer)
    turned_low[...] = normalize(middle[...], row)[0].T
    turned_grad[...] = grad[...].T
    total[...] = jnp.zeros_like(total)

    def one_part(part, unused):
        active, slope = parts(part)
        grad_hidden = (dot_nt(grad[...], weights.get("down", part)) * slope).astype(BF16)
        made = dot(turned_grad[...], active.astype(BF16)).astype(BF16)
        deep, wide = packs.blocks[1]
        for column in range(CHUNK // wide):
            for seq in range(packs.seqs):
                block = made[seq * deep : (seq + 1) * deep, column * wide : (column + 1) * wide]
                packs.put_block(packed, me, 1, part * (CHUNK // wide) + column, seq, block)
        made = dot(turned_low[...], grad_hidden).astype(BF16)
        deep, wide = packs.blocks[0]
        for column in range(CHUNK // wide):
            for batch in range(packs.batches):
                block = made[batch * deep : (batch + 1) * deep, column * wide : (column + 1) * wide]
                packs.put_block(packed, me, 0, batch, part * (CHUNK // wide) + column, block)
        total[...] += dot_nt(grad_hidden, weights.get("up", part))
        return unused

    lax.fori_loop(0, weights.chunks, one_part, 0, unroll=unroll)
    packs.send(packed, outs, moves, 0, packs.starts[2])
    unused, normed, inverse = normalize(middle[...], row)
    back, gain_sum = normalize_back(total[...], normed, inverse, row)
    grad_middle = grad[...].astype(F32) + back
    branch = grad_middle.astype(BF16)
    packs.put_all(packed, me, 2, dot(branch.T, mixed[...]).astype(BF16), True)
    packs.send(packed, outs, moves, packs.starts[2], packs.rows)
    return grad_middle, dot_nt(branch, weights.get("out")).astype(BF16), gain_sum


def ffn_back_scratch(count):
    return [
        pltpu.VMEM((count, D), BF16),
        pltpu.VMEM((D, count), BF16),
        pltpu.VMEM((D, count), BF16),
        pltpu.VMEM((count, D), F32),
    ]


def ffn_back_kernel(
    layer, rows, members, packs, me, grad_ref, carried, middle_ref, mixed_ref, hidden_ref, gain,
    w_out, w_up, w_down, *refs,
):
    outs = refs[: len(packs.shapes())]
    (
        grad_gain, grad_middle, grad_mixed,
        middle, mixed, hidden, out, up, down, grad, turned_low, turned_grad, total, packed, sems,
    ) = refs[len(outs) :]
    weights = Weights(sems, layer, (w_out, w_up, w_down), (out, up, down))
    moves = Moves(sems, weights.copies + weights.chunks)
    came = moves.start(middle_ref, middle)

    def hidden_copy(part):
        lanes = pl.ds(pl.multiple_of(part * CHUNK, CHUNK), CHUNK)
        return pltpu.make_async_copy(
            hidden_ref.at[:, lanes], hidden.at[:, lanes], sems.at[weights.copies + part]
        )

    for part in range(weights.chunks):
        weights.copy("down", part).start()
        hidden_copy(part).start()
        weights.copy("up", part).start()
    weights.copy("out").start()
    late = moves.start(mixed_ref, mixed)
    moves.open = []
    value = grad_ref[...]
    count = value.shape[0]
    span = count // rows
    early = jnp.where(me[0] == members - 1, 1, 0)
    line = iota((count, 2 * rows), 1)
    place = iota((count, 2 * rows), 0) == (line // 2 + 1 - early) * span - 2 + line % 2
    grad[...] = (value.astype(F32) + dot(picks(place), carried[...])).astype(BF16)

    def parts(part):
        hidden_copy(part).wait()
        weights.wait("down", part)
        weights.wait("up", part)
        lanes = pl.ds(pl.multiple_of(part * CHUNK, CHUNK), CHUNK)
        return gelu_both(hidden[:, lanes].astype(F32))

    came.wait()
    late.wait()
    weights.wait("out")
    made = ffn_back(
        layer, packs, me, middle, mixed, parts, weights, gain, packed, outs, moves,
        (grad, turned_low, turned_grad, total), 1,
    )
    grad_middle[...], grad_mixed[...], grad_gain[...] = made
    moves.end()


def ffn_back_call(
    layer, rows, members, batches, seqs, order, me, grad, carried, middle, mixed, hidden, gain, w_out, w_up, w_down
):
    count = grad.shape[0]
    units = w_up.shape[2]
    packs = Packs(batches, seqs, order, ffn_blocks(batches, seqs, units))
    return call(
        functools.partial(ffn_back_kernel, layer, rows, members, packs),
        packs.shapes() + (shape((1, D), F32), shape((count, D), F32), shape((count, D), BF16)),
        grid=(1,),
        scalars=1,
        in_specs=[fixed((count, D)), fixed((2 * rows, D)), ANYWHERE, ANYWHERE, ANYWHERE, fixed(gain.shape)]
        + [ANYWHERE] * 3,
        out_specs=packs.specs() + (fixed((1, D)), fixed((count, D)), fixed((count, D))),
        scratch=[pltpu.VMEM((count, D), F32), pltpu.VMEM((count, D), BF16), pltpu.VMEM((count, units), BF16)]
        + weight_scratch(units)
        + ffn_back_scratch(count)
        + [packs.scratch()[0], pltpu.SemaphoreType.DMA((3 + 3 * (units // CHUNK) + 2 * packs.slots,))],
    )(me, grad, carried, middle, mixed, hidden, gain, w_out, w_up, w_down)


def middle_kernel(layer, rows, members, packs, me, inputs, low, own, *refs):
    others = refs[: members - 1]
    (
        grad_ref, table, gain, w_qkv, w_out, w_up, w_down,
        output, *refs,
    ) = refs[members - 1 :]
    outs = refs[: len(packs.shapes())]
    grad_gain, grad_middle, grad_queries, *refs = refs[len(outs) :]
    pieces = refs[:members]
    queries, mixed, logsum, middle, active, slope, grad_mixed, packed, *scratch = refs[members:]
    held, attention, back, ffn, sems = scratch[:3], scratch[3:7], scratch[7:11], scratch[11:15], scratch[15]
    parts = range(w_up.shape[2] // CHUNK)
    weights = Weights(sems, layer, (w_out, w_up, w_down), held)
    moves = Moves(sems, weights.copies)
    weights.start()
    queries[...] = make_queries(low, w_qkv, table)
    attend(rows, members, me, queries, own, others, mixed, logsum, attention)
    weights.wait("out")
    total = inputs[...].astype(F32) + dot(mixed[...], weights.get("out"))
    middle[...] = total
    normed = normalize(total, gain_row(gain, layer))[0]
    for part in parts:
        lanes = pl.ds(part * CHUNK, CHUNK)
        weights.wait("up", part)
        one, other = gelu_both(dot(normed, weights.get("up", part)))
        active[:, lanes], slope[:, lanes] = one.astype(BF16), other
        weights.wait("down", part)
        total = total + dot(active[:, lanes], weights.get("down", part))
    output[...] = total.astype(BF16)
    ffn[0][...] = grad_ref[...]

    def part_of(part):
        lanes = pl.ds(pl.multiple_of(part * CHUNK, CHUNK), CHUNK)
        return active[:, lanes], slope[:, lanes]

    made = ffn_back(
        layer, packs, me, middle, mixed, part_of, weights, gain, packed, outs, moves, ffn, True
    )
    grad_middle[...], grad_mixed[...], grad_gain[...] = made
    for group in range(D // GROUP):
        sources = [lane_part(each, group) for each in (queries, own, *others, mixed)]
        targets = [lane_part(each, group) for each in (grad_mixed, grad_queries, *pieces)]
        attention_back_part(
            rows, members, *sources, logsum.at[pl.ds(group, 1)], *targets, *attention, *back
        )
    moves.end()


def middle_call(
    layer, rows, members, batches, seqs, order, me, inputs, low, own, others, grad, table, gain,
    w_qkv, w_out, w_up, w_down,
):
    count = inputs.shape[0]
    units = w_up.shape[2]
    packs = Packs(batches, seqs, order, ffn_blocks(batches, seqs, units))
    made = call(
        functools.partial(middle_kernel, layer, rows, members, packs),
        (shape((count, D), BF16),)
        + packs.shapes()
        + (shape((1, D), F32), shape((count, D), F32), shape((count, D), BF16))
        + (shape((2, count, D), BF16),) * members,
        grid=(1,),
        scalars=1,
        in_specs=[fixed((count, D))] * 2
        + [fixed((2, count, D))] * members
        + [fixed((count, D)), fixed(table.shape), fixed(gain.shape)]
        + [fixed((1, D, D), (layer, 0, 0))]
        + [ANYWHERE] * 3,
        out_specs=(fixed((count, D)),)
        + packs.specs()
        + (fixed((1, D)), fixed((count, D)), fixed((count, D)))
        + (fixed((2, count, D)),) * members,
        scratch=[
            pltpu.VMEM((count, D), BF16),
            pltpu.VMEM((count, D), BF16),
            pltpu.VMEM((D // GROUP, count, 128), F32),
            pltpu.VMEM((count, D), F32),
            pltpu.VMEM((count, units), BF16),
            pltpu.VMEM((count, units), F32),
            pltpu.VMEM((count, D), BF16),
            packs.scratch()[0],
        ]
        + weight_scratch(units)
        + attention_scratch(rows, members, count)
        + attention_back_scratch(rows, members, count)
        + ffn_back_scratch(count)
        + [pltpu.SemaphoreType.DMA((1 + 2 * (units // CHUNK) + 2 * packs.slots,))],
    )(me, inputs, low, own, *others, grad, table, gain, w_qkv, w_out, w_up, w_down)
    cut = 4 + len(packs.shapes())
    return (*made[:cut], made[cut:])


def joined_blocks(batches, seqs, other):
    return ((3 * D // seqs, D // batches), other)


def joined_back(layer, packs, me, inputs, grad_queries, sources, rest):
    grad_middle, table, gain, w_qkv, grad_gain, turned, packed = rest
    row = gain_row(gain, layer)
    low, normed, inverse = normalize(inputs[...].astype(F32), row)
    back = 0.0
    for part in range(3):
        if part == 0:
            value = [lanes[...].astype(F32) * DH ** (-0.5) for lanes in grad_queries]
        else:
            value = [sum([source[part - 1].astype(F32) for source in lanes]) for lanes in sources]
        value = jnp.concatenate(value, 1)
        if part < 2:
            value = rotate(value, table[...], True)
        value = value.astype(BF16)
        turned[part * D : (part + 1) * D, :] = value.T
        back = back + dot_nt(value, w_qkv[0, :, part * D : (part + 1) * D])
    deep, wide = packs.blocks[0]

    def one_block(seq, unused):
        made = dot(turned[pl.ds(pl.multiple_of(seq * deep, deep), deep), :], low).astype(BF16)
        for batch in range(packs.batches):
            packs.put_block(packed, me, 0, batch, seq, made[:, batch * wide : (batch + 1) * wide])
        return unused

    lax.fori_loop(0, packs.seqs, one_block, 0)
    value, gain_sum = normalize_back(back, normed, inverse, row)
    grad_gain[...] = gain_sum
    return grad_middle[...] + value


def split_sources(refs, members, cuts):
    rest = refs[cuts:]
    sources = [rest[cut * members : (cut + 1) * members] for cut in range(cuts)]
    return (refs[:cuts], sources, rest[cuts * members :])


def source_specs(count, members, cuts):
    wide = D // cuts
    return [fixed((count, wide))] * cuts + [fixed((2, count, wide))] * (members * cuts)


def embed_back_kernel(layer, members, cuts, packs, me, inputs, *refs):
    grad_queries, sources, refs = split_sources(refs, members, cuts)
    (
        grad_middle, table, gain, w_qkv, tokens, gain_attn_1, gain_ffn_0, gain_ffn_1,
        stays, leaves, sums, grad_inputs, gain_attn_0, turned, packed, sems,
    ) = refs
    value = joined_back(
        layer, packs, me, inputs, grad_queries, sources,
        (grad_middle, table, gain, w_qkv, gain_attn_0, turned, packed),
    ).astype(BF16)
    grad_inputs[...] = value
    onehot = picks(tokens[...] == iota((VOCAB, tokens.shape[1]), 0))
    packs.put_all(packed, me, 1, dot(onehot, value).astype(BF16), False)
    tiles = D // 128
    for number, ref in enumerate((gain_attn_0, gain_attn_1, gain_ffn_0, gain_ffn_1)):
        for tile in range(tiles):
            place = number * tiles + tile
            sums[place : place + 1, :] = ref[:, tile * 128 : (tile + 1) * 128]
    at = packs.slots * packs.rows
    for number, piece in enumerate(in_two(sums[...])):
        packed[at + number * 4 * tiles : at + (number + 1) * 4 * tiles, :] = piece
    packs.hand_out(packed, (stays, leaves), sems)


def embed_back_call(
    layer, batches, seqs, order, me, inputs, grad_queries, sources, grad_middle, table, gain, w_qkv,
    tokens, *gains,
):
    count = inputs.shape[0]
    cuts, members = len(sources), len(sources[0])
    packs = Packs(batches, seqs, order, joined_blocks(batches, seqs, (VOCAB // batches, D // seqs)))
    summed = 4 * D // 128
    return call(
        functools.partial(embed_back_kernel, layer, members, cuts, packs),
        packs.shapes(2 * summed) + (shape((summed, 128), F32), shape((count, D), BF16)),
        grid=(1,),
        scalars=1,
        in_specs=[fixed((count, D))]
        + source_specs(count, members, cuts)
        + [
            fixed((count, D)),
            fixed(table.shape),
            fixed(gain.shape),
            fixed((1, D, 3 * D), (layer, 0, 0)),
            fixed(tokens.shape),
        ]
        + [fixed((1, D))] * 3,
        out_specs=packs.specs() + (fixed((summed, 128)), fixed((count, D))),
        scratch=[pltpu.VMEM((1, D), F32), pltpu.VMEM((3 * D, count), BF16)] + packs.scratch(2 * summed),
    )(me, inputs, *grad_queries, *sum(sources, []), grad_middle, table, gain, w_qkv, tokens, *gains)


def pool_back_kernel(layer, rows, members, cuts, packs, me, inputs, *refs):
    grad_queries, sources, refs = split_sources(refs, members, cuts)
    grad_middle, table, gain, w_qkv, grouped, w_pool, *refs = refs
    outs = refs[: len(packs.shapes())]
    grad_gain, grad_first, edges, turned, packed, sems = refs[len(outs) :]
    value = joined_back(
        layer, packs, me, inputs, grad_queries, sources,
        (grad_middle, table, gain, w_qkv, grad_gain, turned, packed),
    ).astype(BF16)
    packs.put_all(packed, me, 1, dot(value.T, grouped[...]).astype(BF16), True)
    count = value.shape[0]
    short = count // rows
    span = grad_first.shape[0] // rows
    parts = [dot_nt(value, w_pool[third * D : (third + 1) * D, :]).astype(BF16) for third in range(3)]
    line = iota((2 * rows, count), 0)
    found = 0.0
    for third in range(2):
        pick = (iota((2 * rows, count), 1) == (line // 2) * short) & (line % 2 == third)
        found = found + dot(picks(pick), parts[third])
    edges[...] = found.astype(BF16)
    for row in range(rows):
        total = 0.0
        for third in range(3):
            pick = picks(iota((span, short), 0) == 3 * iota((span, short), 1) + third - 2)
            total = total + dot(pick, parts[third][row * short : (row + 1) * short, :])
        grad_first[row * span : (row + 1) * span, :] = total.astype(BF16)
    packs.hand_out(packed, outs, sems)


def pool_back_call(
    layer, rows, span, batches, seqs, order, me, inputs, grad_queries, sources, grad_middle, table,
    gain, w_qkv, grouped, w_pool,
):
    count = inputs.shape[0]
    cuts, members = len(sources), len(sources[0])
    packs = Packs(batches, seqs, order, joined_blocks(batches, seqs, (D // seqs, 3 * D // batches)))
    return call(
        functools.partial(pool_back_kernel, layer, rows, members, cuts, packs),
        packs.shapes() + (shape((1, D), F32), shape((rows * span, D), BF16), shape((2 * rows, D), BF16)),
        grid=(1,),
        scalars=1,
        in_specs=[fixed((count, D))]
        + source_specs(count, members, cuts)
        + [
            fixed((count, D)),
            fixed(table.shape),
            fixed(gain.shape),
            fixed((1, D, 3 * D), (layer, 0, 0)),
            fixed(grouped.shape),
            fixed(w_pool.shape),
        ],
        out_specs=packs.specs() + (fixed((1, D)), fixed((rows * span, D)), fixed((2 * rows, D))),
        scratch=[pltpu.VMEM((3 * D, count), BF16)] + packs.scratch(),
    )(me, inputs, *grad_queries, *sum(sources, []), grad_middle, table, gain, w_qkv, grouped, w_pool)


def angles(positions):
    half_size = DH // 2
    freqs = 10000.0 ** (-jnp.arange(half_size).astype(jnp.float32) / half_size)
    phase = positions.astype(jnp.float32)[:, None] * jnp.tile(freqs, 4)[None, :]
    lane = jnp.arange(4 * half_size)[None, :]
    sine = jnp.sin(phase) * jnp.where(lane < 3 * half_size, -1.0, 1.0)
    return jnp.where(lane < 2 * half_size, jnp.cos(phase), sine)


class Plan:
    def __init__(self, rows):
        self.S = lax.axis_size("seq")
        self.B = lax.axis_size("batch")
        self.R = rows
        self.P = self.S // rows
        self.s = lax.axis_index("seq")
        self.b = lax.axis_index("batch")
        self.z = self.s // self.P
        self.h = self.s % self.P // 2 * 2 + self.b % 2

    def device(self, pair, z, y, core):
        return (z * self.P + y) * self.B + 2 * pair + core

    def exchange(self, value):
        moves = []
        for apart in range(self.R):
            perm = []
            for pair in range(self.B // 2):
                for z in range(self.R):
                    for y in range(self.P):
                        for core in range(2):
                            other = self.device(pair, z ^ apart, y // 2 * 2 + core, y % 2)
                            perm.append((self.device(pair, z, y, core), other))
            piece = lax.dynamic_index_in_dim(value, self.z ^ apart, 0, keepdims=False)
            moves.append(lax.ppermute(piece, AXES, perm))
        got, bit = moves, 1
        while bit < self.R:
            flip = (self.z // bit) % 2 == 1
            got = [jnp.where(flip, got[n ^ bit], got[n]) for n in range(self.R)]
            bit *= 2
        return (jnp.stack(got), moves)

    def shift(self, value, by):
        perm = []
        for pair in range(self.B // 2):
            for z in range(self.R):
                for batch in range(2):
                    for member in range(self.P):
                        to = (member + by) % self.P
                        perm.append((
                            self.device(pair, z, member // 2 * 2 + batch, member % 2),
                            self.device(pair, z, to // 2 * 2 + batch, to % 2),
                        ))
        return lax.ppermute(value, AXES, perm)

    def others(self, value):
        return [self.shift(value, by) for by in range(1, self.P)]

    def swap(self, value, axis, bit):
        count = lax.axis_size(axis)
        return lax.ppermute(value, axis, [(n, n ^ bit) for n in range(count)])

    def bits(self, axis):
        count = lax.axis_size(axis)
        return [1 << n for n in range(count.bit_length() - 1)]

    def order(self, *axes):
        return [(axis, bit) for axis in axes for bit in self.bits(axis)]


def behind(value, *others):
    return lax.optimization_barrier((value, others))[0]


class Halving:
    def __init__(self, plan, order, stays, leaves=None):
        self.plan, self.order = plan, order
        self.terms, self.count, self.leaves = [(stays, 0, stays.shape[0])], stays.shape[0], []
        if leaves is not None:
            self.leaves = [(leaves, 0, leaves.shape[0])]

    def sum(self, start, stop):
        made = 0.0
        for array, first, last in self.terms:
            if first <= start and stop <= last:
                made = made + array[start - first : stop - first].astype(F32)
        return made

    def add(self, cuts=1):
        self.count //= 2
        size = self.count // cuts
        self.leaves = []
        for cut in reversed(range(cuts)):
            made = self.sum(self.count + cut * size, self.count + (cut + 1) * size).astype(BF16)
            self.leaves.append((made, cut * size, (cut + 1) * size))
        return [made for made, start, stop in self.leaves]

    def send(self):
        (axis, bit), self.order = self.order[0], self.order[1:]
        got = [self.plan.swap(made, axis, bit) for made, start, stop in self.leaves]
        self.terms += [(each, start, stop) for each, (made, start, stop) in zip(got, self.leaves)]
        return got

    def wait(self, *others):
        array, start, stop = self.terms[0]
        self.terms[0] = (behind(array, *others), start, stop)

    def rest(self):
        return [array for array, start, stop in self.terms if start == 0]


def body(
    tokens, loss_mask, cotangent, embed, gain_attn, w_qkv, w_out, gain_ffn, w_up, w_down, w_pool
):
    plan = Plan(tokens.shape[0])
    rows, span = tokens.shape
    short = loss_mask.shape[1]
    members, batches, seqs = plan.P, plan.B, plan.S
    units = w_up.shape[2]
    groups = D // GROUP
    every, along = plan.order("batch", "seq"), plan.order("seq")
    me = jnp.stack([plan.h, plan.b, plan.s]).astype(jnp.int32)

    token_line = plan.exchange(tokens)[0].reshape(1, rows * span)
    token_column = token_line.reshape(rows * span, 1)

    def places(length):
        block = jnp.arange(rows, dtype=jnp.int32)[:, None] * members + plan.h
        return (block * length + jnp.arange(length, dtype=jnp.int32)[None]).reshape(-1)

    first_angles, second_angles = angles(places(span)), angles(places(short))

    ffn_layout = ffn_blocks(batches, seqs, units)
    pool_layout = joined_blocks(batches, seqs, (D // seqs, 3 * D // batches))
    embed_layout = joined_blocks(batches, seqs, (VOCAB // batches, D // seqs))

    def scatter(value, axis):
        return lax.psum_scatter(value, axis, scatter_dimension=0, tiled=True)

    inputs, low, own_0 = embed_call(0, token_column, embed, gain_attn, w_qkv, first_angles)
    others_0 = plan.others(own_0)
    start_grad, start_moves = plan.exchange(cotangent * loss_mask.astype(BF16)[..., None])
    first_low, edges, queries_0, mixed_0, logsum_0, middle_0, hidden_0 = forward_call(
        0, rows, members, me, inputs, low, own_0, others_0, first_angles, gain_ffn, w_qkv, w_out, w_up, w_down
    )
    edge = plan.shift(edges, 1)

    grouped, pooled, low, own_1 = pool_call(
        1, rows, members, me, behind(first_low, *start_moves), edge, w_pool, gain_attn, w_qkv, second_angles
    )
    others_1 = plan.others(own_1)
    second_low, packed, gain_ffn_1, grad_middle, grad_queries, pieces = middle_call(
        1, rows, members, batches, seqs, along, me, pooled, low, own_1, others_1, start_grad.reshape(-1, D),
        second_angles, gain_ffn, w_qkv, w_out, w_up, w_down,
    )
    ffn_1 = Halving(plan, along, scatter(packed, "batch"))
    others = [plan.shift(pieces[by], -by) for by in range(1, members)]
    outs, out_moves = plan.exchange(
        jnp.concatenate([first_low.reshape(rows, span, D), second_low.reshape(rows, short, D)], 1)
    )
    near, far = out_moves[: rows // 2], out_moves[rows // 2 :]
    packed, gain_attn_1, grad_first, edges = pool_back_call(
        1, rows, span, batches, seqs, along, me, pooled, [grad_queries], [[pieces[0]] + others],
        grad_middle, second_angles, gain_attn, w_qkv, grouped, w_pool,
    )
    pool_1 = Halving(plan, along, scatter(packed, "batch"))
    carried = plan.shift(edges, -1)

    stays, leaves, gain_ffn_0, grad_middle, grad_mixed = ffn_back_call(
        0, rows, members, batches, seqs, every, me, behind(grad_first, *near), carried, middle_0, mixed_0,
        hidden_0, gain_ffn, w_out, w_up, w_down,
    )
    ffn_0 = Halving(plan, every, stays, leaves)
    got = ffn_0.send()
    leaving = ffn_1.add()
    got += ffn_1.send()
    got += far[::2]
    grad_mixed = behind(grad_mixed, *leaving)
    grad_queries, sources = [], []
    for group in range(groups):
        grad, pieces = attention_back_call(
            rows, members, me, queries_0, own_0, others_0, mixed_0, logsum_0, grad_mixed, [group]
        )
        grad_queries.append(grad)
        sources.append([pieces[0]] + [plan.shift(pieces[by], -by) for by in range(1, members)])
        ffn_0.wait(grad, *got)
        ffn_1.wait(grad, *got)
        if group == 0:
            leaving = ffn_0.add(2) + ffn_1.add()
            late = ffn_0.send()
            got = [late.pop(0)] + ffn_1.send() + far[1::2]
            grad_mixed = behind(grad_mixed, *leaving)
        else:
            leaving = ffn_1.add()
            got = late + ffn_1.send()
            leaving += ffn_0.add(2)
            got.append(ffn_0.send()[0])
    stays, leaves, sums, grad_inputs = embed_back_call(
        0, batches, seqs, every, me, inputs, [behind(grad, *leaving) for grad in grad_queries], sources,
        grad_middle, first_angles, gain_attn, w_qkv, token_line, gain_attn_1, gain_ffn_0, gain_ffn_1,
    )

    leaves = behind(leaves, *got)
    for step, (axis, bit) in enumerate(every):
        came = plan.swap(leaves, axis, bit)
        if step == 1:
            input_grad = plan.exchange(behind(grad_inputs, leaves).reshape(rows, span, D))[0]
        for chain in (pool_1, ffn_1, ffn_0) if step else (pool_1,):
            if chain.order:
                chain.wait(leaves)
                chain.add()
                chain.send()
        if step < len(every) - 1:
            stays, leaves, sums = halve_call(stays, came, sums)
    made = finish_call(
        (ffn_layout, pool_layout, embed_layout),
        [ffn_0.rest(), ffn_1.rest(), pool_1.rest()],
        stays, sums, came,
    )
    qkv_grad, out_grad, up_grad, down_grad, pool_grad, embed_grad, gain_attn_grad, gain_ffn_grad = made
    return (
        outs[:, :span],
        outs[:, span:],
        input_grad.astype(F32),
        embed_grad,
        gain_attn_grad,
        jnp.swapaxes(qkv_grad, 1, 2),
        jnp.swapaxes(out_grad, 1, 2),
        gain_ffn_grad,
        up_grad,
        jnp.swapaxes(down_grad, 1, 2),
        pool_grad.T,
    )


def solution(mesh):
    in_specs = (
        P("batch", "seq"),
        P("batch", "seq"),
        P("batch", "seq", None),
        P(),
        P(),
        P(),
        P(),
        P(),
        P(),
        P(),
        P(),
    )
    out_specs = (
        P("batch", "seq", None),
        P("batch", "seq", None),
        P("batch", "seq", None),
        P("batch", "seq"),
        P(),
        P(None, "batch", "seq"),
        P(None, "batch", "seq"),
        P(),
        P(None, "batch", "seq"),
        P(None, "batch", "seq"),
        P("batch", "seq"),
    )
    return jax.shard_map(body, mesh=mesh, in_specs=in_specs, out_specs=out_specs, check_vma=False)
```

time: 356 us -> 280 us (0.79)
  waiting for transfers between devices: 69.3 us -> 36.7 us
  Pallas kernels: 165 us -> 134 us
  starting transfers between devices: 68.5 us -> 55 us
  between operations: 2.02 us -> 14.9 us
  local copies, waits for them, and re-layouts: 20.2 us -> 14.6 us
  other arithmetic: 25.6 us -> 20.1 us
    ppermute x25 -> x18, waiting for transfers between devices: 57.9 us -> 26.6 us  [swap(): return lax.ppermute(value, axis, [(n, n ^ bit) for n in range(count)])]
    pallas_call x14, Pallas kernels: 165 us -> 134 us  [the longest x2 26 us: attention_back_call(): call(functools.partial(attention_back_kernel, rows, members), (shape((cou...]
    convert_element_type x3 -> x11, other arithmetic: 1.42 us -> 13.2 us  [the longest x8 11.8 us: add(): self.sum(self.count + cut * size, self.count + (cut + 1) * size)]
    ppermute x20 -> x16, starting transfers between devices: 30.1 us -> 21.2 us  [exchange(): moves.append(lax.ppermute(piece, AXES, perm))]
    add x25 -> x0, other arithmetic: 8.39 us -> none  [the longest x20 6.98 us: step(): self.value = self.value + got.astype(F32)]
    ppermute x25 -> x18, starting transfers between devices: 32 us -> 25.8 us  [swap(): return lax.ppermute(value, axis, [(n, n ^ bit) for n in range(count)])]
    unnamed x102 -> x70, local copies, waits for them, and re-layouts: 13.6 us -> 8.59 us
    concatenate x5 -> x0, other arithmetic: 4.62 us -> none  [the longest x2 1.96 us: angles(): jnp.concatenate([-sine, sine] * 2, 1)]
  transfers between devices with their start and end apart: 51 -> 43, of which waited for: 21 -> 14; matrix products, arithmetic and copies ran while one was open for 7% -> 9% of each run, Pallas kernels for 36% -> 38%
where the time goes in v3:
time: 280 us; the launch traced here: 276 us
  Pallas kernels  134 us (48%)
  starting transfers between devices  55 us (20%)
  waiting for transfers between devices  36.7 us (13%)
  other arithmetic  20.1 us (7%)
  between operations  14.9 us (5%)
  local copies, waits for them, and re-layouts  14.6 us (5%)
    ppermute x18, waiting for transfers between devices, swap(): return lax.ppermute(value, axis, [(n, n ^ bit) for n in range(count)])  26.6 us
    pallas_call x2, Pallas kernels, attention_back_call(): call(functools.partial(attention_back_kernel, rows, members), (shape((cou...  26 us
    ppermute x18, starting transfers between devices, swap(): return lax.ppermute(value, axis, [(n, n ^ bit) for n in range(count)])  25.8 us
    pallas_call x1, Pallas kernels, forward_call(): call(functools.partial(forward_kernel, layer, rows, members), (shape((cou...  22.8 us
    ppermute x16, starting transfers between devices, exchange(): moves.append(lax.ppermute(piece, AXES, perm))  21.2 us
    pallas_call x1, Pallas kernels, ffn_back_call(): call(functools.partial(ffn_back_kernel, layer, rows, members, packs), pac...  20.9 us
    pallas_call x1, Pallas kernels, middle_call(): call(functools.partial(middle_kernel, layer, rows, members, packs), (shap...  16.5 us
    pallas_call x1, Pallas kernels, embed_back_call(): call(functools.partial(embed_back_kernel, layer, members, cuts, packs), p...  14.5 us
  transfers between devices with their start and end apart: 43, of which 14 were waited for; matrix products, arithmetic and copies ran while one was open for 9% of the time, Pallas kernels for 38%

profile of v3, /device:TPU:0, one launch (start us, length us, event | category | flops | bytes accessed | tf_op | source)
XLA Modules:
  0.0 275.5 jit_solution(17226116419485481448)
XLA Ops:
  8.1 4.1 %collective-permute-start.1 = (s32[192]{0:T(256)S(1)}, s32[192]{0:T(256)S(1)}, u32[]{:S(2)}, u32[]{:S(2)}) collective-permute-start(s32[192]{0:T(256)S(1)} %bitcast.78), channel_id=1, source_target_pairs={{0,16},{1,20},{4,17},{5,21},{8,24},{9,28},{12,25},{13,29},{16,0},{... | collective-permute-start | bytes 2312 | tf_op jit(solution)/shard_map/ppermute | solution.py:1169
  20.2 6.1 %shard_map.194 = (bf16[768,512]{1,0:T(8,128)(2,1)}, bf16[768,512]{1,0:T(8,128)(2,1)}, bf16[2,768,512]{2,1,0:T(8,128)(2,1)}) custom-call(s32[768,1]{1,0:T(8,128)} %reshape_reshape.4.tokens, bf16[256,512]{1,0:T(8,128)(2,1)} %embed.1, bf16[2,512]{1,0:T(2,128)(2,1)} %refs_8_.3, bf16[2,512,1536]{2,1,0:T(8,128)(2,1)} %refs_9_.1, f32[768,128]{1,0:T(8,128)} %fusion.table.refs_1_.refs_7_), custom_call_target="tpu_custom_call" | custom-call | tf_op jit(solution)/shard_map/pallas_call | solution.py:340
  28.1 3.5 %collective-permute-start.8 = (bf16[64,512]{1,0:T(8,128)(2,1)S(1)}, bf16[64,512]{1,0:T(8,128)(2,1)S(1)}, u32[]{:S(2)}, u32[]{:S(2)}) collective-permute-start(bf16[64,512]{1,0:T(8,128)(2,1)S(1)} %get-tuple-element.189), channel_id=1, source_target_pairs={{0,24},{1,28},{4,25},{5,29},{8,16},{9,20},{12,17},{13,21},{16,8},{... | collective-permute-start | bytes 196616 | tf_op jit(solution)/shard_map/ppermute | solution.py:1169
  35.4 22.8 %shard_map.195 = (bf16[768,512]{1,0:T(8,128)(2,1)}, bf16[8,512]{1,0:T(8,128)(2,1)}, bf16[768,512]{1,0:T(8,128)(2,1)}, bf16[768,512]{1,0:T(8,128)(2,1)}, f32[2,76...) custom-call(s32[3]{0:T(128)} %pad_add_fusion.1.me, bf16[768,512]{1,0:T(8,128)(2,1)} %get-tuple-element.88.inputs, ...), custom_call_target="tpu_custom_call" | custom-call | tf_op jit(solution)/shard_map/pallas_call | solution.py:750
  58.2 3.2 %collective-permute-start.9 = (bf16[8,512]{1,0:T(8,128)(2,1)}, bf16[8,512]{1,0:T(8,128)(2,1)S(1)}, u32[]{:S(2)}, u32[]{:S(2)}) collective-permute-start(bf16[8,512]{1,0:T(8,128)(2,1)} %get-tuple-element.93), channel_id=1, source_target_pairs={{0,1},{1,0},{4,5},{5,4},{8,9},{9,8},{12,13},{13,12},{16,17},{17,16... | collective-permute-start | bytes 24584 | tf_op jit(solution)/shard_map/ppermute | solution.py:1188
  63.3 5.5 %shard_map.196 = (bf16[256,1536]{1,0:T(8,128)(2,1)}, f32[256,512]{1,0:T(8,128)}, bf16[256,512]{1,0:T(8,128)(2,1)}, bf16[2,256,512]{2,1,0:T(8,128)(2,1)}) custom-call(s32[3]{0:T(128)} %pad_add_fusion.1.me, bf16[768,512]{1,0:T(8,128)(2,1)} %get-tuple-element.92.first, bf16[8,512]{1,0:T(8,128)(2,1)} %copy-done.30, bf16[1536,512]{1,0:T(8,128)(2,1)} %refs_8_.2, ...), custom_call_target="tpu_custom_call" | custom-call | tf_op jit(solution)/shard_map/pallas_call | solution.py:385
  71.7 16.5 %shard_map.197 = (bf16[256,512]{1,0:T(8,128)(2,1)}, bf16[18432,128]{1,0:T(8,128)(2,1)}, f32[1,512]{1,0:T(1,128)}, f32[256,512]{1,0:T(8,128)}, bf16[256,512]{1,0:...) custom-call(s32[3]{0:T(128)} %pad_add_fusion.1.me, f32[256,512]{1,0:T(8,128)} %get-tuple-element.94.inputs, ...), custom_call_target="tpu_custom_call" | custom-call | tf_op jit(solution)/shard_map/pallas_call | solution.py:945
  92.0 10.8 %shard_map.198 = (bf16[12288,128]{1,0:T(8,128)(2,1)}, f32[1,512]{1,0:T(1,128)}, bf16[768,512]{1,0:T(8,128)(2,1)}, bf16[8,512]{1,0:T(8,128)(2,1)}) custom-call(s32[3]{0:T(128)} %pad_add_fusion.1.me, f32[256,512]{1,0:T(8,128)} %get-tuple-element.94.inputs, bf16[256,512]{1,0:T(8,128)(2,1)} %get-tuple-element.101.refs_0_, ...), custom_call_target="tpu_custom_call" | custom-call | tf_op jit(solution)/shard_map/pallas_call | solution.py:1115
  109.0 4.7 %collective-permute-done.13 = bf16[256,512]{1,0:T(8,128)(2,1)S(1)} collective-permute-done((bf16[256,512]{1,0:T(8,128)(2,1)S(1)}, bf16[256,512]{1,0:T(8,128)(2,1)S(1)}, u32[]{:S(2)}, u32[]{:S(2)}) %collective-permute-start.13) | collective-permute-done | bytes 262176 | tf_op jit(solution)/shard_map/ppermute | solution.py:1169
  114.4 20.9 %shard_map.199 = (bf16[9216,128]{1,0:T(8,128)(2,1)}, bf16[9216,128]{1,0:T(8,128)(2,1)}, f32[1,512]{1,0:T(1,128)}, f32[768,512]{1,0:T(8,128)}, bf16[768,512]{1,0:T(8,128)(2,1)}) custom-call(s32[3]{0:T(128)} %pad_add_fusion.1.me, bf16[768,512]{1,0:T(8,128)(2,1)} %get-tuple-element.107.grad_ref, bf16[8,512]{1,0:T(8,128)(2,1)} %copy-done.31, ...), custom_call_target="tpu_custom_call" | custom-call | tf_op jit(solution)/shard_map/pallas_call | solution.py:875
  142.4 12.8 %shard_map.200 = (bf16[768,256]{1,0:T(8,128)(2,1)}, bf16[2,768,256]{2,1,0:T(8,128)(2,1)}, bf16[2,768,256]{2,1,0:T(8,128)(2,1)}) custom-call(s32[3]{0:T(128)} %pad_add_fusion.1.me, bf16[768,512]{1,0:T(8,128)(2,1)} %get-tuple-element.98.queries, bf16[2,768,512]{2,1,0:T(8,128)(2,1)} %get-tuple-element.90.own, bf16[2,768,512]{2,1,0:T(8,128)(2,1)} %copy-done, ...), custom_call_target="tpu_custom_call" | custom-call | tf_op jit(solution)/shard_map/pallas_call | solution.py:608
  156.4 2.7 add_convert_fusion
  163.1 3.5 %collective-permute-start.11 = (bf16[256,512]{1,0:T(8,128)(2,1)}, bf16[256,512]{1,0:T(8,128)(2,1)S(1)}, u32[]{:S(2)}, u32[]{:S(2)}) collective-permute-start(bf16[256,512]{1,0:T(8,128)(2,1)} %get-tuple-element.174), channel_id=1, source_target_pairs={{0,24},{1,28},{4,25},{5,29},{8,16},{9,20},{12,17},{13,21},{16,8},{... | collective-permute-start | bytes 786440 | tf_op jit(solution)/shard_map/ppermute | solution.py:1169
  167.1 13.2 %shard_map.201 = (bf16[768,256]{1,0:T(8,128)(2,1)}, bf16[2,768,256]{2,1,0:T(8,128)(2,1)}, bf16[2,768,256]{2,1,0:T(8,128)(2,1)}) custom-call(s32[3]{0:T(128)} %pad_add_fusion.1.me, bf16[768,512]{1,0:T(8,128)(2,1)} %get-tuple-element.98.queries, bf16[2,768,512]{2,1,0:T(8,128)(2,1)} %get-tuple-element.90.own, bf16[2,768,512]{2,1,0:T(8,128)(2,1)} %copy-done, ...), custom_call_target="tpu_custom_call" | custom-call | tf_op jit(solution)/shard_map/pallas_call | solution.py:608
  180.5 7.3 %collective-permute-done.19 = bf16[2304,128]{1,0:T(8,128)(2,1)S(1)} collective-permute-done((bf16[2304,128]{1,0:T(8,128)(2,1)S(1)}, bf16[2304,128]{1,0:T(8,128)(2,1)S(1)}, u32[]{:S(2)}, u32[]{:S(2)}) %collective-permute-start.19) | collective-permute-done | bytes 589856 | tf_op jit(solution)/shard_map/ppermute | solution.py:1195
  196.1 14.5 %shard_map.202 = (bf16[4096,128]{1,0:T(8,128)(2,1)}, bf16[4128,128]{1,0:T(8,128)(2,1)}, f32[16,128]{1,0:T(8,128)}, bf16[768,512]{1,0:T(8,128)(2,1)}) custom-call(s32[3]{0:T(128)} %pad_add_fusion.1.me, bf16[768,512]{1,0:T(8,128)(2,1)} %get-tuple-element.88.inputs, bf16[768,256]{1,0:T(8,128)(2,1)} %get-tuple-element.123.refs_0_, ...), custom_call_target="tpu_custom_call" | custom-call | tf_op jit(solution)/shard_map/pallas_call | solution.py:1059
  215.5 2.8 %shard_map.203 = (bf16[2048,128]{1,0:T(8,128)(2,1)}, bf16[2080,128]{1,0:T(8,128)(2,1)}, f32[16,128]{1,0:T(8,128)}) custom-call(bf16[4096,128]{1,0:T(8,128)(2,1)} %get-tuple-element.134.kept, bf16[4128,128]{1,0:T(8,128)(2,1)} %collective-permute-done.26.got, f32[16,128]{1,0:T(8,128)} %get-tuple-element.137.sums), custom_call_target="tpu_custom_call" | custom-call | tf_op jit(solution)/shard_map/pallas_call | solution.py:232
  222.8 4.2 %collective-permute-done.35.refs_11_ = bf16[1536,128]{1,0:T(8,128)(2,1)S(1)} collective-permute-done((bf16[1536,128]{1,0:T(8,128)(2,1)S(1)}, bf16[1536,128]{1,0:T(8,128)(2,1)S(1)}, u32[]{:S(2)}, u32[]{:S(2)}) %collective-permute-start.35) | collective-permute-done | bytes 393248 | tf_op jit(solution)/shard_map/ppermute | solution.py:1195
  228.3 4.4 %collective-permute-done.31.got = bf16[2080,128]{1,0:T(8,128)(2,1)S(1)} collective-permute-done((bf16[2080,128]{1,0:T(8,128)(2,1)}, bf16[2080,128]{1,0:T(8,128)(2,1)S(1)}, u32[]{:S(2)}, u32[]{:S(2)}) %collective-permute-start.31) | collective-permute-done | bytes 532512 | tf_op jit(solution)/shard_map/ppermute | solution.py:1195
  237.7 3.3 %collective-permute-start.38 = (bf16[1056,128]{1,0:T(8,128)(2,1)}, bf16[1056,128]{1,0:T(8,128)(2,1)S(1)}, u32[]{:S(2)}, u32[]{:S(2)}) collective-permute-start(bf16[1056,128]{1,0:T(8,128)(2,1)} %get-tuple-element.143), channel_id=1, source_target_pairs={{0,4},{4,0},{8,12},{12,8},{16,20},{20,16},{24,28},{28,24},{1,5},{5... | collective-permute-start | bytes 811016 | tf_op jit(solution)/shard_map/ppermute | solution.py:1195
  244.7 4.0 %collective-permute-done.38.got = bf16[1056,128]{1,0:T(8,128)(2,1)S(1)} collective-permute-done((bf16[1056,128]{1,0:T(8,128)(2,1)}, bf16[1056,128]{1,0:T(8,128)(2,1)S(1)}, u32[]{:S(2)}, u32[]{:S(2)}) %collective-permute-start.38) | collective-permute-done | bytes 270368 | tf_op jit(solution)/shard_map/ppermute | solution.py:1195
  253.0 2.9 %collective-permute-start.34 = (bf16[576,128]{1,0:T(8,128)(2,1)S(1)}, bf16[576,128]{1,0:T(8,128)(2,1)S(1)}, u32[]{:S(2)}, u32[]{:S(2)}) collective-permute-start(bf16[576,128]{1,0:T(8,128)(2,1)S(1)} %add_convert_fusion.7), channel_id=1, source_target_pairs={{0,16},{4,20},{8,24},{12,28},{16,0},{20,4},{24,8},{28,12},{1,17},{... | collective-permute-start | bytes 442376 | tf_op jit(solution)/shard_map/ppermute | solution.py:1195
  258.8 2.8 %collective-permute-start.40 = (bf16[288,128]{1,0:T(8,128)(2,1)}, bf16[288,128]{1,0:T(8,128)(2,1)S(1)}, u32[]{:S(2)}, u32[]{:S(2)}) collective-permute-start(bf16[288,128]{1,0:T(8,128)(2,1)} %get-tuple-element.156), channel_id=1, source_target_pairs={{0,16},{4,20},{8,24},{12,28},{16,0},{20,4},{24,8},{28,12},{1,17},{... | collective-permute-start | bytes 221192 | tf_op jit(solution)/shard_map/ppermute | solution.py:1195
  265.9 2.6 shard_map.207
  (189 shorter events, 81.6 us)
Async XLA Ops:
  7.2 130.2 %reduce-scatter.3.cloned.1.call-start = ((), (), s32[]{:S(2)}) async-start(), calls=%async_computation.2 | async-start | bytes 5898240 | tf_op jit(solution)/shard_map/reduce_scatter | solution.py:1272
  28.1 34.6 %collective-permute-start.8 = (bf16[64,512]{1,0:T(8,128)(2,1)S(1)}, bf16[64,512]{1,0:T(8,128)(2,1)S(1)}, u32[]{:S(2)}, u32[]{:S(2)}) collective-permute-start(bf16[64,512]{1,0:T(8,128)(2,1)S(1)} %get-tuple-element.189), channel_id=1, source_target_pairs={{0,24},{1,28},{4,25},{5,29},{8,16},{9,20},{12,17},{13,21},{16,8},{... | collective-permute-start | bytes 196616 | tf_op jit(solution)/shard_map/ppermute | solution.py:1169
  31.5 31.1 %collective-permute-start.7 = (bf16[64,512]{1,0:T(8,128)(2,1)S(1)}, bf16[64,512]{1,0:T(8,128)(2,1)S(1)}, u32[]{:S(2)}, u32[]{:S(2)}) collective-permute-start(bf16[64,512]{1,0:T(8,128)(2,1)S(1)} %get-tuple-element.190), channel_id=1, source_target_pairs={{0,16},{1,20},{4,17},{5,21},{8,24},{9,28},{12,25},{13,29},{16,0},{... | collective-permute-start | bytes 196616 | tf_op jit(solution)/shard_map/ppermute | solution.py:1169
  31.5 31.1 %collective-permute-start.6 = (bf16[64,512]{1,0:T(8,128)(2,1)S(1)}, bf16[64,512]{1,0:T(8,128)(2,1)S(1)}, u32[]{:S(2)}, u32[]{:S(2)}) collective-permute-start(bf16[64,512]{1,0:T(8,128)(2,1)S(1)} %get-tuple-element.191), channel_id=1, source_target_pairs={{0,8},{1,12},{4,9},{5,13},{8,0},{9,4},{12,1},{13,5},{16,24},{17,28... | collective-permute-start | bytes 196616 | tf_op jit(solution)/shard_map/ppermute | solution.py:1169
  32.5 30.1 %collective-permute-start.5 = (bf16[64,512]{1,0:T(8,128)(2,1)S(1)}, bf16[64,512]{1,0:T(8,128)(2,1)S(1)}, u32[]{:S(2)}, u32[]{:S(2)}) collective-permute-start(bf16[64,512]{1,0:T(8,128)(2,1)S(1)} %get-tuple-element.192), channel_id=1, source_target_pairs={{0,0},{1,4},{4,1},{5,5},{8,8},{9,12},{12,9},{13,13},{16,16},{17,20... | collective-permute-start | bytes 196616 | tf_op jit(solution)/shard_map/ppermute | solution.py:1169
  88.2 124.4 %reduce-scatter.5.cloned.1.call-start = ((), (), s32[]{:S(2)}) async-start(), calls=%async_computation.3 | async-start | bytes 3932160 | tf_op jit(solution)/shard_map/reduce_scatter | solution.py:1272
  135.3 19.8 %collective-permute-start.17 = (bf16[9216,128]{1,0:T(8,128)(2,1)}, bf16[9216,128]{1,0:T(8,128)(2,1)}, u32[]{:S(2)}, u32[]{:S(2)}) collective-permute-start(bf16[9216,128]{1,0:T(8,128)(2,1)} %get-tuple-element.115), channel_id=1, source_target_pairs={{0,1},{1,0},{2,3},{3,2},{4,5},{5,4},{6,7},{7,6},{8,9},{9,8},{10,11... | collective-permute-start | bytes 7077896 | tf_op jit(solution)/shard_map/ppermute | solution.py:1195
  138.5 17.9 %collective-permute-start.18 = (bf16[2304,128]{1,0:T(8,128)(2,1)S(1)}, bf16[2304,128]{1,0:T(8,128)(2,1)S(1)}, u32[]{:S(2)}, u32[]{:S(2)}) collective-permute-start(bf16[2304,128]{1,0:T(8,128)(2,1)S(1)} %slice.129), channel_id=1, source_target_pairs={{0,4},{4,0},{8,12},{12,8},{16,20},{20,16},{24,28},{28,24},{1,5},{5... | collective-permute-start | bytes 1769480 | tf_op jit(solution)/shard_map/ppermute | solution.py:1195
  140.0 15.2 %collective-permute-start.12 = (bf16[256,512]{1,0:T(8,128)(2,1)S(1)}, bf16[256,512]{1,0:T(8,128)(2,1)S(1)}, u32[]{:S(2)}, u32[]{:S(2)}) collective-permute-start(bf16[256,512]{1,0:T(8,128)(2,1)S(1)} %get-tuple-element.175), channel_id=1, source_target_pairs={{0,16},{1,20},{4,17},{5,21},{8,24},{9,28},{12,25},{13,29},{16,0},{... | collective-permute-start | bytes 786440 | tf_op jit(solution)/shard_map/ppermute | solution.py:1169
  159.1 28.8 %collective-permute-start.19 = (bf16[2304,128]{1,0:T(8,128)(2,1)S(1)}, bf16[2304,128]{1,0:T(8,128)(2,1)S(1)}, u32[]{:S(2)}, u32[]{:S(2)}) collective-permute-start(bf16[2304,128]{1,0:T(8,128)(2,1)S(1)} %get-tuple-element.168), channel_id=1, source_target_pairs={{0,2},{1,3},{2,0},{3,1},{4,6},{5,7},{6,4},{7,5},{8,10},{9,11},{10,... | collective-permute-start | bytes 1769480 | tf_op jit(solution)/shard_map/ppermute | solution.py:1195
  161.3 19.2 %collective-permute-start.20 = (bf16[1152,128]{1,0:T(8,128)(2,1)S(1)}, bf16[1152,128]{1,0:T(8,128)(2,1)S(1)}, u32[]{:S(2)}, u32[]{:S(2)}) collective-permute-start(bf16[1152,128]{1,0:T(8,128)(2,1)S(1)} %add_convert_fusion.5), channel_id=1, source_target_pairs={{0,8},{4,12},{8,0},{12,4},{16,24},{20,28},{24,16},{28,20},{1,9},{5... | collective-permute-start | bytes 884744 | tf_op jit(solution)/shard_map/ppermute | solution.py:1195
  163.1 17.2 %collective-permute-start.11 = (bf16[256,512]{1,0:T(8,128)(2,1)}, bf16[256,512]{1,0:T(8,128)(2,1)S(1)}, u32[]{:S(2)}, u32[]{:S(2)}) collective-permute-start(bf16[256,512]{1,0:T(8,128)(2,1)} %get-tuple-element.174), channel_id=1, source_target_pairs={{0,24},{1,28},{4,25},{5,29},{8,16},{9,20},{12,17},{13,21},{16,8},{... | collective-permute-start | bytes 786440 | tf_op jit(solution)/shard_map/ppermute | solution.py:1169
  166.5 29.6 %collective-permute-start.21 = (bf16[2,768,256]{2,1,0:T(8,128)(2,1)}, bf16[2,768,256]{2,1,0:T(8,128)(2,1)}, u32[]{:S(2)}, u32[]{:S(2)}) collective-permute-start(bf16[2,768,256]{2,1,0:T(8,128)(2,1)} %get-tuple-element.126), channel_id=1, source_target_pairs={{0,1},{1,0},{4,5},{5,4},{8,9},{9,8},{12,13},{13,12},{16,17},{17,16... | collective-permute-start | bytes 2359304 | tf_op jit(solution)/shard_map/ppermute | solution.py:1188
  166.5 44.1 %collective-permute-start.23 = (bf16[2304,128]{1,0:T(8,128)(2,1)}, bf16[2304,128]{1,0:T(8,128)(2,1)S(1)}, u32[]{:S(2)}, u32[]{:S(2)}) collective-permute-start(bf16[2304,128]{1,0:T(8,128)(2,1)} %get-tuple-element.167), channel_id=1, source_target_pairs={{0,2},{1,3},{2,0},{3,1},{4,6},{5,7},{6,4},{7,5},{8,10},{9,11},{10,... | collective-permute-start | bytes 1769480 | tf_op jit(solution)/shard_map/ppermute | solution.py:1195
  180.3 15.8 %collective-permute-start.22 = (bf16[2,768,256]{2,1,0:T(8,128)(2,1)}, bf16[2,768,256]{2,1,0:T(8,128)(2,1)}, u32[]{:S(2)}, u32[]{:S(2)}) collective-permute-start(bf16[2,768,256]{2,1,0:T(8,128)(2,1)} %get-tuple-element.128), channel_id=1, source_target_pairs={{0,1},{1,0},{4,5},{5,4},{8,9},{9,8},{12,13},{13,12},{16,17},{17,16... | collective-permute-start | bytes 2359304 | tf_op jit(solution)/shard_map/ppermute | solution.py:1188
  190.0 20.7 %collective-permute-start.25 = (bf16[1152,128]{1,0:T(8,128)(2,1)}, bf16[1152,128]{1,0:T(8,128)(2,1)}, u32[]{:S(2)}, u32[]{:S(2)}) collective-permute-start(bf16[1152,128]{1,0:T(8,128)(2,1)} %get-tuple-element.166), channel_id=1, source_target_pairs={{0,4},{4,0},{8,12},{12,8},{16,20},{20,16},{24,28},{28,24},{1,5},{5... | collective-permute-start | bytes 884744 | tf_op jit(solution)/shard_map/ppermute | solution.py:1195
  193.0 17.6 %collective-permute-start.24 = (bf16[576,128]{1,0:T(8,128)(2,1)}, bf16[576,128]{1,0:T(8,128)(2,1)}, u32[]{:S(2)}, u32[]{:S(2)}) collective-permute-start(bf16[576,128]{1,0:T(8,128)(2,1)} %add_convert_fusion.8), channel_id=1, source_target_pairs={{0,16},{4,20},{8,24},{12,28},{16,0},{20,4},{24,8},{28,12},{1,17},{... | collective-permute-start | bytes 442376 | tf_op jit(solution)/shard_map/ppermute | solution.py:1195
  218.3 14.4 %collective-permute-start.31 = (bf16[2080,128]{1,0:T(8,128)(2,1)}, bf16[2080,128]{1,0:T(8,128)(2,1)S(1)}, u32[]{:S(2)}, u32[]{:S(2)}) collective-permute-start(bf16[2080,128]{1,0:T(8,128)(2,1)} %get-tuple-element.138), channel_id=1, source_target_pairs={{0,2},{1,3},{2,0},{3,1},{4,6},{5,7},{6,4},{7,5},{8,10},{9,11},{10,... | collective-permute-start | bytes 1597448 | tf_op jit(solution)/shard_map/ppermute | solution.py:1195
  219.9 15.8 %collective-permute-start.29 = (bf16[192,512]{1,0:T(8,128)(2,1)S(1)}, bf16[192,512]{1,0:T(8,128)(2,1)S(1)}, u32[]{:S(2)}, u32[]{:S(2)}) collective-permute-start(bf16[192,512]{1,0:T(8,128)(2,1)S(1)} %get-tuple-element.181), channel_id=1, source_target_pairs={{0,8},{1,12},{4,9},{5,13},{8,0},{9,4},{12,1},{13,5},{16,24},{17,28... | collective-permute-start | bytes 589832 | tf_op jit(solution)/shard_map/ppermute | solution.py:1169
  219.9 16.8 %collective-permute-start.30 = (bf16[192,512]{1,0:T(8,128)(2,1)S(1)}, bf16[192,512]{1,0:T(8,128)(2,1)S(1)}, u32[]{:S(2)}, u32[]{:S(2)}) collective-permute-start(bf16[192,512]{1,0:T(8,128)(2,1)S(1)} %get-tuple-element.182), channel_id=1, source_target_pairs={{0,0},{1,4},{4,1},{5,5},{8,8},{9,12},{12,9},{13,13},{16,16},{17,20... | collective-permute-start | bytes 589832 | tf_op jit(solution)/shard_map/ppermute | solution.py:1169
  220.6 17.1 %collective-permute-start.28 = (bf16[192,512]{1,0:T(8,128)(2,1)S(1)}, bf16[192,512]{1,0:T(8,128)(2,1)S(1)}, u32[]{:S(2)}, u32[]{:S(2)}) collective-permute-start(bf16[192,512]{1,0:T(8,128)(2,1)S(1)} %get-tuple-element.183), channel_id=1, source_target_pairs={{0,16},{1,20},{4,17},{5,21},{8,24},{9,28},{12,25},{13,29},{16,0},{... | collective-permute-start | bytes 589832 | tf_op jit(solution)/shard_map/ppermute | solution.py:1169
  232.7 19.1 %collective-permute-start.32 = (bf16[1152,128]{1,0:T(8,128)(2,1)S(1)}, bf16[1152,128]{1,0:T(8,128)(2,1)S(1)}, u32[]{:S(2)}, u32[]{:S(2)}) collective-permute-start(bf16[1152,128]{1,0:T(8,128)(2,1)S(1)} %copy-done.14), channel_id=1, source_target_pairs={{0,4},{4,0},{8,12},{12,8},{16,20},{20,16},{24,28},{28,24},{1,5},{5... | collective-permute-start | bytes 884744 | tf_op jit(solution)/shard_map/ppermute | solution.py:1195
  236.8 15.1 %collective-permute-start.33 = (bf16[1152,128]{1,0:T(8,128)(2,1)S(1)}, bf16[1152,128]{1,0:T(8,128)(2,1)S(1)}, u32[]{:S(2)}, u32[]{:S(2)}) collective-permute-start(bf16[1152,128]{1,0:T(8,128)(2,1)S(1)} %add_convert_fusion.2), channel_id=1, source_target_pairs={{0,8},{4,12},{8,0},{12,4},{16,24},{20,28},{24,16},{28,20},{1,9},{5... | collective-permute-start | bytes 884744 | tf_op jit(solution)/shard_map/ppermute | solution.py:1195
  244.7 18.2 %collective-permute-start.37 = (bf16[384,128]{1,0:T(8,128)(2,1)S(1)}, bf16[384,128]{1,0:T(8,128)(2,1)S(1)}, u32[]{:S(2)}, u32[]{:S(2)}) collective-permute-start(bf16[384,128]{1,0:T(8,128)(2,1)S(1)} %add_convert_fusion.9), channel_id=1, source_target_pairs={{0,16},{4,20},{8,24},{12,28},{16,0},{20,4},{24,8},{28,12},{1,17},{... | collective-permute-start | bytes 294920 | tf_op jit(solution)/shard_map/ppermute | solution.py:1195
  (54 other events, 468.4 us)
Sparse Core Ops, SparseCore 0:
  88.4 48.9 reduce-scatter.2
  140.0 53.0 reduce-scatter.4

commit v4 on v3

--- a/solution.py
+++ b/solution.py
@@ -165,16 +165,6 @@
                 batch, seq = (column, line) if swapped else (line, column)
                 block = made[line * deep : (line + 1) * deep, column * wide : (column + 1) * wide]
                 self.put_block(packed, me, number, batch, seq, block)
-
-    def hand_out(self, packed, outs, sems):
-        copies, at = [], 0
-        for number, out in enumerate(outs):
-            copies.append(pltpu.make_async_copy(packed.at[pl.ds(at, out.shape[0])], out, sems.at[number]))
-            at += out.shape[0]
-        for copy in copies:
-            copy.start()
-        for copy in copies:
-            copy.wait()
 
     def send(self, packed, outs, moves, first, last):
         for slot in range(self.slots):
@@ -319,8 +309,8 @@
 
     @pl.when(part == 0)
     def first():
-        onehot = picks(tokens[...] == iota((tokens.shape[0], embed.shape[0]), 1))
-        value = dot(onehot, embed[...])
+        onehot = picks(tokens[...] == iota((embed.shape[0], tokens.shape[1]), 0))
+        value = lax.dot_general(onehot, embed[...], (((0,), (0,)), ((), ())), preferred_element_type=F32)
         inputs[...] = value.astype(BF16)
         low[...] = normalize(value, gain_row(gain, layer))[0]
 
@@ -336,7 +326,7 @@
 
 
 def embed_call(layer, tokens, embed, gain, w_qkv, table):
-    count = tokens.shape[0]
+    count = tokens.shape[1]
     return call(
         functools.partial(embed_kernel, layer),
         (shape((count, D), BF16), shape((count, D), BF16), shape((2, count, D), BF16)),
@@ -447,10 +437,21 @@
     bias[...] = jnp.where(seen, 0.0, masked_score)
 
 
-def score(query, keys, bias, start, end):
-    scores = dot_nt(query, keys[0:end, :])
-    last = scores[:, start:] + bias[...]
+def stacked(block, masks):
+    return jnp.concatenate([block * mask for mask in masks], 0)
+
+
+def score(stack, keys, bias, start, end):
+    scores = dot_nt(stack, keys[0:end, :])
+    last = scores[:, start:] + jnp.concatenate([bias[...]] * (stack.shape[0] // bias.shape[0]), 0)
     return jnp.concatenate([scores[:, :start], last], 1) if start else last
+
+
+def unstacked(stack, lanes, held):
+    count = held.shape[0]
+    for number, mine in enumerate(lanes):
+        held = jnp.where(mine, stack[number * count : (number + 1) * count, :], held)
+    return held
 
 
 def attention_part(rows, members, queries, own, *refs):
@@ -465,29 +466,26 @@
     at_once = heads_at_once(rows, members, span)
 
     def some_heads(turn, unused):
-        todo = []
-        for number in range(at_once):
-            head = turn * at_once + number
-            lanes = iota((1, GROUP), 1) // DH == head
-            mask = picks(lanes)
-            for first, last in tiles:
-                block = slice(first * span, last * span)
-                todo.append((head, lanes, mask, block, first * width, last * width))
+        heads = [turn * at_once + number for number in range(at_once)]
+        lanes = [iota((1, GROUP), 1) // DH == head for head in heads]
+        masks = [picks(mine) for mine in lanes]
+        blocks = [slice(first * span, last * span) for first, last in tiles]
         scores = [
-            score(queries[block, :] * mask, keys, bias, start, end)
-            for head, lanes, mask, block, start, end in todo
+            score(stacked(queries[block, :], masks), keys, bias, first * width, last * width)
+            for block, (first, last) in zip(blocks, tiles)
         ]
         highest = [jnp.max(value, -1, keepdims=True) for value in scores]
         expon = [jnp.exp(value - most) for value, most in zip(scores, highest)]
         totals = [jnp.sum(value, -1, keepdims=True) for value in expon]
         outs = [
-            dot(value.astype(BF16), values[0:end, :]) * (1.0 / whole)
-            for value, whole, (head, lanes, mask, block, start, end) in zip(expon, totals, todo)
+            dot(value.astype(BF16), values[0 : last * width, :]) * (1.0 / whole)
+            for value, whole, (first, last) in zip(expon, totals, tiles)
         ]
-        for (head, lanes, mask, block, start, end), out, most, whole in zip(todo, outs, highest, totals):
-            total[block, :] = jnp.where(lanes, out, total[block, :])
-            here = iota((out.shape[0], 128), 1) == head
-            logsum[0, block, :] = jnp.where(here, most + jnp.log(whole), logsum[0, block, :])
+        for block, out, most, whole in zip(blocks, outs, highest, totals):
+            total[block, :] = unstacked(out, lanes, total[block, :])
+            logs = jnp.broadcast_to(most + jnp.log(whole), (out.shape[0], 128))
+            places = [iota((1, 128), 1) == head for head in heads]
+            logsum[0, block, :] = unstacked(logs, places, logsum[0, block, :])
         return unused
 
     lax.fori_loop(0, HEADS // at_once, some_heads, 0)
@@ -545,39 +543,37 @@
     at_once = heads_at_once(rows, members, span)
 
     def some_heads(turn, unused):
-        todo = []
-        for number in range(at_once):
-            head = turn * at_once + number
-            lanes = iota((1, GROUP), 1) // DH == head
-            for tile, (first, last) in enumerate(tiles):
-                block = slice(first * span, last * span)
-                todo.append((head, lanes, picks(lanes), tile, block, first * width, last * width))
-        grads = [grad_mixed[block, :] * mask for head, lanes, mask, tile, block, start, end in todo]
+        heads = [turn * at_once + number for number in range(at_once)]
+        lanes = [iota((1, GROUP), 1) // DH == head for head in heads]
+        masks = [picks(mine) for mine in lanes]
+        blocks = [slice(first * span, last * span) for first, last in tiles]
+        grads = [stacked(grad_mixed[block, :], masks) for block in blocks]
         scores = [
-            score(queries[block, :] * mask, keys, bias, start, end)
-            for head, lanes, mask, tile, block, start, end in todo
+            score(stacked(queries[block, :], masks), keys, bias, first * width, last * width)
+            for block, (first, last) in zip(blocks, tiles)
         ]
-        grad_probs = [dot_nt(grad, values[0 : each[-1], :]) for grad, each in zip(grads, todo)]
-        sums = [
-            jnp.sum(
-                jnp.where(iota((block.stop - block.start, 128), 1) == head, logsum[0, block, :], 0.0),
-                -1,
-                keepdims=True,
+        grad_probs = [dot_nt(grad, values[0 : last * width, :]) for grad, (first, last) in zip(grads, tiles)]
+        sums, deltas = [], []
+        for block, grad in zip(blocks, grads):
+            logs = logsum[0, block, :]
+            sums.append(
+                jnp.concatenate(
+                    [
+                        jnp.sum(jnp.where(iota(logs.shape, 1) == head, logs, 0.0), -1, keepdims=True)
+                        for head in heads
+                    ],
+                    0,
+                )
             )
-            for head, lanes, mask, tile, block, start, end in todo
-        ]
-        deltas = [
-            jnp.sum(grad.astype(F32) * mixed[each[4], :].astype(F32), -1, keepdims=True)
-            for grad, each in zip(grads, todo)
-        ]
+            product = grad.astype(F32) * jnp.concatenate([mixed[block, :].astype(F32)] * at_once, 0)
+            deltas.append(jnp.sum(product, -1, keepdims=True))
         probs = [jnp.exp(value - whole) for value, whole in zip(scores, sums)]
         grad_scores = [
             (prob * (grad - delta)).astype(BF16) for prob, grad, delta in zip(probs, grad_probs, deltas)
         ]
-        for each, grad in zip(todo, grad_scores):
-            head, lanes, mask, tile, block, start, end = each
-            total[block, :] = jnp.where(lanes, dot(grad, keys[0:end, :]), total[block, :])
-        count = len(tiles)
+        for block, grad, (first, last) in zip(blocks, grad_scores, tiles):
+            total[block, :] = unstacked(dot(grad, keys[0 : last * width, :]), lanes, total[block, :])
+        probs = [prob.astype(BF16) for prob in probs]
         for number in range(at_once):
             mine = pl.ds(pl.multiple_of((turn * at_once + number) * DH, DH), DH)
             for tile, (first, last) in enumerate(tiles):
@@ -587,9 +583,11 @@
                     (turned, grad_scores, grad_keys),
                     (turned_grad, probs, grad_values),
                 ):
-                    later = made[number * count + tile : (number + 1) * count]
-                    stack = jnp.concatenate([value[:, columns].astype(BF16) for value in later], 0)
-                    into[mine, columns] = dot(source[tile, mine, 0:lines], stack)
+                    later = []
+                    for each in made[tile:]:
+                        size = each.shape[0] // at_once
+                        later.append(each[number * size : (number + 1) * size, columns])
+                    into[mine, columns] = dot(source[tile, mine, 0:lines], jnp.concatenate(later, 0))
         return unused
 
     lax.fori_loop(0, HEADS // at_once, some_heads, 0)
@@ -772,7 +770,9 @@
 def ffn_back(layer, packs, me, middle, mixed, parts, weights, gain, packed, outs, moves, scratch, unroll):
     grad, turned_low, turned_grad, total = scratch
     row = gain_row(gain, layer)
-    turned_low[...] = normalize(middle[...], row)[0].T
+    low, normed, inverse = normalize(middle[...], row)
+    turned_low[...] = low.T
+    middle[...] = normed
     turned_grad[...] = grad[...].T
     total[...] = jnp.zeros_like(total)
 
@@ -796,8 +796,7 @@
 
     lax.fori_loop(0, weights.chunks, one_part, 0, unroll=unroll)
     packs.send(packed, outs, moves, 0, packs.starts[2])
-    unused, normed, inverse = normalize(middle[...], row)
-    back, gain_sum = normalize_back(total[...], normed, inverse, row)
+    back, gain_sum = normalize_back(total[...], middle[...], inverse, row)
     grad_middle = grad[...].astype(F32) + back
     branch = grad_middle.astype(BF16)
     packs.put_all(packed, me, 2, dot(branch.T, mixed[...]).astype(BF16), True)
@@ -984,10 +983,10 @@
 
 
 def joined_back(layer, packs, me, inputs, grad_queries, sources, rest):
-    grad_middle, table, gain, w_qkv, grad_gain, turned, packed = rest
+    grad_middle, came, table, gain, w_qkv, grad_gain, turned, packed, outs, moves = rest
     row = gain_row(gain, layer)
     low, normed, inverse = normalize(inputs[...].astype(F32), row)
-    back = 0.0
+    joined = []
     for part in range(3):
         if part == 0:
             value = [lanes[...].astype(F32) * DH ** (-0.5) for lanes in grad_queries]
@@ -996,9 +995,8 @@
         value = jnp.concatenate(value, 1)
         if part < 2:
             value = rotate(value, table[...], True)
-        value = value.astype(BF16)
-        turned[part * D : (part + 1) * D, :] = value.T
-        back = back + dot_nt(value, w_qkv[0, :, part * D : (part + 1) * D])
+        joined.append(value.astype(BF16))
+        turned[part * D : (part + 1) * D, :] = joined[part].T
     deep, wide = packs.blocks[0]
 
     def one_block(seq, unused):
@@ -1008,6 +1006,12 @@
         return unused
 
     lax.fori_loop(0, packs.seqs, one_block, 0)
+    packs.send(packed, outs, moves, 0, packs.starts[1])
+    back = 0.0
+    for copy in came:
+        copy.wait()
+    for part in range(3):
+        back = back + dot_nt(joined[part], w_qkv[:, part * D : (part + 1) * D])
     value, gain_sum = normalize_back(back, normed, inverse, row)
     grad_gain[...] = gain_sum
     return grad_middle[...] + value
@@ -1027,25 +1031,30 @@
 def embed_back_kernel(layer, members, cuts, packs, me, inputs, *refs):
     grad_queries, sources, refs = split_sources(refs, members, cuts)
     (
-        grad_middle, table, gain, w_qkv, tokens, gain_attn_1, gain_ffn_0, gain_ffn_1,
-        stays, leaves, sums, grad_inputs, gain_attn_0, turned, packed, sems,
+        middle_in, table, gain, w_in, tokens, gain_attn_1, gain_ffn_0, gain_ffn_1,
+        stays, leaves, sums, grad_inputs, gain_attn_0, turned, grad_middle, w_qkv, packed, sems,
     ) = refs
+    moves = Moves(sems)
+    came = [moves.start(w_in.at[layer], w_qkv), moves.start(middle_in, grad_middle)]
+    moves.open = []
     value = joined_back(
         layer, packs, me, inputs, grad_queries, sources,
-        (grad_middle, table, gain, w_qkv, gain_attn_0, turned, packed),
+        (grad_middle, came, table, gain, w_qkv, gain_attn_0, turned, packed, (stays, leaves), moves),
     ).astype(BF16)
     grad_inputs[...] = value
     onehot = picks(tokens[...] == iota((VOCAB, tokens.shape[1]), 0))
     packs.put_all(packed, me, 1, dot(onehot, value).astype(BF16), False)
+    packs.send(packed, (stays, leaves), moves, packs.starts[1], packs.rows)
     tiles = D // 128
     for number, ref in enumerate((gain_attn_0, gain_attn_1, gain_ffn_0, gain_ffn_1)):
         for tile in range(tiles):
             place = number * tiles + tile
             sums[place : place + 1, :] = ref[:, tile * 128 : (tile + 1) * 128]
-    at = packs.slots * packs.rows
+    at, extra = packs.slots * packs.rows, 8 * tiles
     for number, piece in enumerate(in_two(sums[...])):
         packed[at + number * 4 * tiles : at + (number + 1) * 4 * tiles, :] = piece
-    packs.hand_out(packed, (stays, leaves), sems)
+    moves.start(packed.at[pl.ds(at, extra)], leaves.at[pl.ds(at // 2, extra)])
+    moves.end()
 
 
 def embed_back_call(
@@ -1063,29 +1072,37 @@
         scalars=1,
         in_specs=[fixed((count, D))]
         + source_specs(count, members, cuts)
-        + [
-            fixed((count, D)),
-            fixed(table.shape),
-            fixed(gain.shape),
-            fixed((1, D, 3 * D), (layer, 0, 0)),
-            fixed(tokens.shape),
-        ]
+        + [ANYWHERE, fixed(table.shape), fixed(gain.shape), ANYWHERE, fixed(tokens.shape)]
         + [fixed((1, D))] * 3,
         out_specs=packs.specs() + (fixed((summed, 128)), fixed((count, D))),
-        scratch=[pltpu.VMEM((1, D), F32), pltpu.VMEM((3 * D, count), BF16)] + packs.scratch(2 * summed),
+        scratch=[
+            pltpu.VMEM((1, D), F32),
+            pltpu.VMEM((3 * D, count), BF16),
+            pltpu.VMEM((count, D), F32),
+            pltpu.VMEM((D, 3 * D), BF16),
+            packs.scratch(2 * summed)[0],
+            pltpu.SemaphoreType.DMA((3 + 2 * packs.slots,)),
+        ],
     )(me, inputs, *grad_queries, *sum(sources, []), grad_middle, table, gain, w_qkv, tokens, *gains)
 
 
 def pool_back_kernel(layer, rows, members, cuts, packs, me, inputs, *refs):
     grad_queries, sources, refs = split_sources(refs, members, cuts)
-    grad_middle, table, gain, w_qkv, grouped, w_pool, *refs = refs
+    middle_in, table, gain, w_in, grouped_in, pool_in, *refs = refs
     outs = refs[: len(packs.shapes())]
-    grad_gain, grad_first, edges, turned, packed, sems = refs[len(outs) :]
+    grad_gain, grad_first, edges, turned, grad_middle, w_qkv, grouped, w_pool, packed, sems = refs[len(outs) :]
+    moves = Moves(sems)
+    came = [moves.start(w_in.at[layer], w_qkv), moves.start(middle_in, grad_middle)]
+    late = [moves.start(grouped_in, grouped), moves.start(pool_in, w_pool)]
+    moves.open = []
     value = joined_back(
         layer, packs, me, inputs, grad_queries, sources,
-        (grad_middle, table, gain, w_qkv, grad_gain, turned, packed),
+        (grad_middle, came, table, gain, w_qkv, grad_gain, turned, packed, outs, moves),
     ).astype(BF16)
+    for copy in late:
+        copy.wait()
     packs.put_all(packed, me, 1, dot(value.T, grouped[...]).astype(BF16), True)
+    packs.send(packed, outs, moves, packs.starts[1], packs.rows)
     count = value.shape[0]
     short = count // rows
     span = grad_first.shape[0] // rows
@@ -1102,7 +1119,7 @@
             pick = picks(iota((span, short), 0) == 3 * iota((span, short), 1) + third - 2)
             total = total + dot(pick, parts[third][row * short : (row + 1) * short, :])
         grad_first[row * span : (row + 1) * span, :] = total.astype(BF16)
-    packs.hand_out(packed, outs, sems)
+    moves.end()
 
 
 def pool_back_call(
@@ -1119,16 +1136,17 @@
         scalars=1,
         in_specs=[fixed((count, D))]
         + source_specs(count, members, cuts)
-        + [
-            fixed((count, D)),
-            fixed(table.shape),
-            fixed(gain.shape),
-            fixed((1, D, 3 * D), (layer, 0, 0)),
-            fixed(grouped.shape),
-            fixed(w_pool.shape),
+        + [ANYWHERE, fixed(table.shape), fixed(gain.shape), ANYWHERE, ANYWHERE, ANYWHERE],
+        out_specs=packs.specs() + (fixed((1, D)), fixed((rows * span, D)), fixed((2 * rows, D))),
+        scratch=[
+            pltpu.VMEM((3 * D, count), BF16),
+            pltpu.VMEM((count, D), F32),
+            pltpu.VMEM((D, 3 * D), BF16),
+            pltpu.VMEM(grouped.shape, BF16),
+            pltpu.VMEM(w_pool.shape, BF16),
+            packs.scratch()[0],
+            pltpu.SemaphoreType.DMA((4 + 2 * packs.slots,)),
         ],
-        out_specs=packs.specs() + (fixed((1, D)), fixed((rows * span, D)), fixed((2 * rows, D))),
-        scratch=[pltpu.VMEM((3 * D, count), BF16)] + packs.scratch(),
     )(me, inputs, *grad_queries, *sum(sources, []), grad_middle, table, gain, w_qkv, grouped, w_pool)
 
 
@@ -1253,10 +1271,10 @@
     units = w_up.shape[2]
     groups = D // GROUP
     every, along = plan.order("batch", "seq"), plan.order("seq")
+    crossed = every[:1] + along[:1] + every[1:-len(along)] + along[1:]
     me = jnp.stack([plan.h, plan.b, plan.s]).astype(jnp.int32)
 
     token_line = plan.exchange(tokens)[0].reshape(1, rows * span)
-    token_column = token_line.reshape(rows * span, 1)
 
     def places(length):
         block = jnp.arange(rows, dtype=jnp.int32)[:, None] * members + plan.h
@@ -1271,7 +1289,7 @@
     def scatter(value, axis):
         return lax.psum_scatter(value, axis, scatter_dimension=0, tiled=True)
 
-    inputs, low, own_0 = embed_call(0, token_column, embed, gain_attn, w_qkv, first_angles)
+    inputs, low, own_0 = embed_call(0, token_line, embed, gain_attn, w_qkv, first_angles)
     others_0 = plan.others(own_0)
     start_grad, start_moves = plan.exchange(cotangent * loss_mask.astype(BF16)[..., None])
     first_low, edges, queries_0, mixed_0, logsum_0, middle_0, hidden_0 = forward_call(
@@ -1301,10 +1319,10 @@
     carried = plan.shift(edges, -1)
 
     stays, leaves, gain_ffn_0, grad_middle, grad_mixed = ffn_back_call(
-        0, rows, members, batches, seqs, every, me, behind(grad_first, *near), carried, middle_0, mixed_0,
+        0, rows, members, batches, seqs, crossed, me, behind(grad_first, *near), carried, middle_0, mixed_0,
         hidden_0, gain_ffn, w_out, w_up, w_down,
     )
-    ffn_0 = Halving(plan, every, stays, leaves)
+    ffn_0 = Halving(plan, crossed, stays, leaves)
     got = ffn_0.send()
     leaving = ffn_1.add()
     got += ffn_1.send()

time: 280 us -> 268 us (0.957)
  Pallas kernels: 134 us -> 129 us
    ppermute x18, waiting for transfers between devices: 26.6 us -> 21.5 us  [swap(): return lax.ppermute(value, axis, [(n, n ^ bit) for n in range(count)])]
    ppermute x18, starting transfers between devices: 25.8 us -> 21.5 us  [swap(): return lax.ppermute(value, axis, [(n, n ^ bit) for n in range(count)])]
    unnamed x70 -> x72, local copies, waits for them, and re-layouts: 8.59 us -> 9.83 us
  transfers between devices with their start and end apart: 43 -> 43, of which waited for: 14 -> 17; matrix products, arithmetic and copies ran while one was open for 9% -> 8% of each run, Pallas kernels for 38% -> 37%
where the time goes in v4:
time: 268 us; the launch traced here: 263 us
  Pallas kernels  129 us (48%)
  starting transfers between devices  52.3 us (20%)
  waiting for transfers between devices  34.3 us (13%)
  other arithmetic  18.4 us (7%)
  local copies, waits for them, and re-layouts  14.8 us (6%)
  between operations  14.8 us (6%)
    pallas_call x2, Pallas kernels, attention_back_call(): call(functools.partial(attention_back_kernel, rows, members), (shape((cou...  23.2 us
    ppermute x16, starting transfers between devices, exchange(): moves.append(lax.ppermute(piece, AXES, perm))  22.5 us
    pallas_call x1, Pallas kernels, forward_call(): call(functools.partial(forward_kernel, layer, rows, members), (shape((cou...  21.9 us
    ppermute x18, starting transfers between devices, swap(): return lax.ppermute(value, axis, [(n, n ^ bit) for n in range(count)])  21.5 us
    ppermute x18, waiting for transfers between devices, swap(): return lax.ppermute(value, axis, [(n, n ^ bit) for n in range(count)])  21.5 us
    pallas_call x1, Pallas kernels, ffn_back_call(): call(functools.partial(ffn_back_kernel, layer, rows, members, packs), pac...  20.5 us
    pallas_call x1, Pallas kernels, middle_call(): call(functools.partial(middle_kernel, layer, rows, members, packs), (shap...  16.6 us
    pallas_call x1, Pallas kernels, embed_back_call(): call(functools.partial(embed_back_kernel, layer, members, cuts, packs), p...  14.8 us
  transfers between devices with their start and end apart: 43, of which 17 were waited for; matrix products, arithmetic and copies ran while one was open for 8% of the time, Pallas kernels for 37%

profile of v4, /device:TPU:0, one launch (start us, length us, event | category | flops | bytes accessed | tf_op | source)
XLA Modules:
  0.0 263.4 jit_solution(10018849563498165645)
XLA Ops:
  8.1 4.1 %collective-permute-start.1 = (s32[192]{0:T(256)S(1)}, s32[192]{0:T(256)S(1)}, u32[]{:S(2)}, u32[]{:S(2)}) collective-permute-start(s32[192]{0:T(256)S(1)} %bitcast.78), channel_id=1, source_target_pairs={{0,16},{1,20},{4,17},{5,21},{8,24},{9,28},{12,25},{13,29},{16,0},{... | collective-permute-start | bytes 2312 | tf_op jit(solution)/shard_map/ppermute | solution.py:1187
  19.8 6.0 %shard_map.194 = (bf16[768,512]{1,0:T(8,128)(2,1)}, bf16[768,512]{1,0:T(8,128)(2,1)}, bf16[2,768,512]{2,1,0:T(8,128)(2,1)}) custom-call(s32[1,768]{1,0:T(1,128)} %reshape.100.tokens.refs_10_, bf16[256,512]{1,0:T(8,128)(2,1)} %embed.1, bf16[2,512]{1,0:T(2,128)(2,1)} %refs_8_.3, bf16[2,512,1536]{2,1,0:T(8,128)(2,1)} %refs_9_.1, ...), custom_call_target="tpu_custom_call" | custom-call | tf_op jit(solution)/shard_map/pallas_call | solution.py:330
  27.6 3.5 %collective-permute-start.8 = (bf16[64,512]{1,0:T(8,128)(2,1)S(1)}, bf16[64,512]{1,0:T(8,128)(2,1)S(1)}, u32[]{:S(2)}, u32[]{:S(2)}) collective-permute-start(bf16[64,512]{1,0:T(8,128)(2,1)S(1)} %get-tuple-element.189), channel_id=1, source_target_pairs={{0,24},{1,28},{4,25},{5,29},{8,16},{9,20},{12,17},{13,21},{16,8},{... | collective-permute-start | bytes 196616 | tf_op jit(solution)/shard_map/ppermute | solution.py:1187
  34.9 21.9 %shard_map.195 = (bf16[768,512]{1,0:T(8,128)(2,1)}, bf16[8,512]{1,0:T(8,128)(2,1)}, bf16[768,512]{1,0:T(8,128)(2,1)}, bf16[768,512]{1,0:T(8,128)(2,1)}, f32[2,76...) custom-call(s32[3]{0:T(128)} %pad_add_fusion.1.me, bf16[768,512]{1,0:T(8,128)(2,1)} %get-tuple-element.88.inputs, ...), custom_call_target="tpu_custom_call" | custom-call | tf_op jit(solution)/shard_map/pallas_call | solution.py:748
  56.8 3.2 %collective-permute-start.9 = (bf16[8,512]{1,0:T(8,128)(2,1)}, bf16[8,512]{1,0:T(8,128)(2,1)S(1)}, u32[]{:S(2)}, u32[]{:S(2)}) collective-permute-start(bf16[8,512]{1,0:T(8,128)(2,1)} %get-tuple-element.93), channel_id=1, source_target_pairs={{0,1},{1,0},{4,5},{5,4},{8,9},{9,8},{12,13},{13,12},{16,17},{17,16... | collective-permute-start | bytes 24584 | tf_op jit(solution)/shard_map/ppermute | solution.py:1206
  61.9 5.5 %shard_map.196 = (bf16[256,1536]{1,0:T(8,128)(2,1)}, f32[256,512]{1,0:T(8,128)}, bf16[256,512]{1,0:T(8,128)(2,1)}, bf16[2,256,512]{2,1,0:T(8,128)(2,1)}) custom-call(s32[3]{0:T(128)} %pad_add_fusion.1.me, bf16[768,512]{1,0:T(8,128)(2,1)} %get-tuple-element.92.first, bf16[8,512]{1,0:T(8,128)(2,1)} %copy-done.31, bf16[1536,512]{1,0:T(8,128)(2,1)} %refs_8_.2, ...), custom_call_target="tpu_custom_call" | custom-call | tf_op jit(solution)/shard_map/pallas_call | solution.py:375
  70.3 16.6 %shard_map.197 = (bf16[256,512]{1,0:T(8,128)(2,1)}, bf16[18432,128]{1,0:T(8,128)(2,1)}, f32[1,512]{1,0:T(1,128)}, f32[256,512]{1,0:T(8,128)}, bf16[256,512]{1,0:...) custom-call(s32[3]{0:T(128)} %pad_add_fusion.1.me, f32[256,512]{1,0:T(8,128)} %get-tuple-element.94.inputs, ...), custom_call_target="tpu_custom_call" | custom-call | tf_op jit(solution)/shard_map/pallas_call | solution.py:944
  90.6 9.3 %shard_map.198 = (bf16[12288,128]{1,0:T(8,128)(2,1)}, f32[1,512]{1,0:T(1,128)}, bf16[768,512]{1,0:T(8,128)(2,1)}, bf16[8,512]{1,0:T(8,128)(2,1)}) custom-call(s32[3]{0:T(128)} %pad_add_fusion.1.me, f32[256,512]{1,0:T(8,128)} %get-tuple-element.94.inputs, bf16[256,512]{1,0:T(8,128)(2,1)} %get-tuple-element.101.refs_0_, ...), custom_call_target="tpu_custom_call" | custom-call | tf_op jit(solution)/shard_map/pallas_call | solution.py:1132
  104.0 2.6 collective-permute-start.16
  106.6 4.2 %collective-permute-done.13 = bf16[256,512]{1,0:T(8,128)(2,1)S(1)} collective-permute-done((bf16[256,512]{1,0:T(8,128)(2,1)S(1)}, bf16[256,512]{1,0:T(8,128)(2,1)S(1)}, u32[]{:S(2)}, u32[]{:S(2)}) %collective-permute-start.13) | collective-permute-done | bytes 262176 | tf_op jit(solution)/shard_map/ppermute | solution.py:1187
  111.5 20.5 %shard_map.199 = (bf16[9216,128]{1,0:T(8,128)(2,1)}, bf16[9216,128]{1,0:T(8,128)(2,1)}, f32[1,512]{1,0:T(1,128)}, f32[768,512]{1,0:T(8,128)}, bf16[768,512]{1,0:T(8,128)(2,1)}) custom-call(s32[3]{0:T(128)} %pad_add_fusion.1.me, bf16[768,512]{1,0:T(8,128)(2,1)} %get-tuple-element.107.grad_ref, bf16[8,512]{1,0:T(8,128)(2,1)} %copy-done.32, ...), custom_call_target="tpu_custom_call" | custom-call | tf_op jit(solution)/shard_map/pallas_call | solution.py:874
  141.1 11.5 %shard_map.200 = (bf16[768,256]{1,0:T(8,128)(2,1)}, bf16[2,768,256]{2,1,0:T(8,128)(2,1)}, bf16[2,768,256]{2,1,0:T(8,128)(2,1)}) custom-call(s32[3]{0:T(128)} %pad_add_fusion.1.me, bf16[768,512]{1,0:T(8,128)(2,1)} %get-tuple-element.98.queries, bf16[2,768,512]{2,1,0:T(8,128)(2,1)} %get-tuple-element.90.own, bf16[2,768,512]{2,1,0:T(8,128)(2,1)} %copy-done, ...), custom_call_target="tpu_custom_call" | custom-call | tf_op jit(solution)/shard_map/pallas_call | solution.py:606
  163.5 11.7 %shard_map.201 = (bf16[768,256]{1,0:T(8,128)(2,1)}, bf16[2,768,256]{2,1,0:T(8,128)(2,1)}, bf16[2,768,256]{2,1,0:T(8,128)(2,1)}) custom-call(s32[3]{0:T(128)} %pad_add_fusion.1.me, bf16[768,512]{1,0:T(8,128)(2,1)} %get-tuple-element.98.queries, bf16[2,768,512]{2,1,0:T(8,128)(2,1)} %get-tuple-element.90.own, bf16[2,768,512]{2,1,0:T(8,128)(2,1)} %copy-done, ...), custom_call_target="tpu_custom_call" | custom-call | tf_op jit(solution)/shard_map/pallas_call | solution.py:606
  179.5 2.5 collective-permute-start.24
  183.2 14.8 %shard_map.202 = (bf16[4096,128]{1,0:T(8,128)(2,1)}, bf16[4128,128]{1,0:T(8,128)(2,1)}, f32[16,128]{1,0:T(8,128)}, bf16[768,512]{1,0:T(8,128)(2,1)}) custom-call(s32[3]{0:T(128)} %pad_add_fusion.1.me, bf16[768,512]{1,0:T(8,128)(2,1)} %get-tuple-element.88.inputs, bf16[768,256]{1,0:T(8,128)(2,1)} %get-tuple-element.123.refs_0_, ...), custom_call_target="tpu_custom_call" | custom-call | tf_op jit(solution)/shard_map/pallas_call | solution.py:1068
  203.1 2.9 %shard_map.203 = (bf16[2048,128]{1,0:T(8,128)(2,1)}, bf16[2080,128]{1,0:T(8,128)(2,1)}, f32[16,128]{1,0:T(8,128)}) custom-call(bf16[4096,128]{1,0:T(8,128)(2,1)} %get-tuple-element.134.kept, bf16[4128,128]{1,0:T(8,128)(2,1)} %collective-permute-done.26.got, f32[16,128]{1,0:T(8,128)} %get-tuple-element.137.sums), custom_call_target="tpu_custom_call" | custom-call | tf_op jit(solution)/shard_map/pallas_call | solution.py:222
  211.5 3.2 %collective-permute-done.35.refs_11_ = bf16[1536,128]{1,0:T(8,128)(2,1)S(1)} collective-permute-done((bf16[1536,128]{1,0:T(8,128)(2,1)S(1)}, bf16[1536,128]{1,0:T(8,128)(2,1)S(1)}, u32[]{:S(2)}, u32[]{:S(2)}) %collective-permute-start.35) | collective-permute-done | bytes 393248 | tf_op jit(solution)/shard_map/ppermute | solution.py:1213
  216.8 3.3 %collective-permute-done.31.got = bf16[2080,128]{1,0:T(8,128)(2,1)S(1)} collective-permute-done((bf16[2080,128]{1,0:T(8,128)(2,1)}, bf16[2080,128]{1,0:T(8,128)(2,1)S(1)}, u32[]{:S(2)}, u32[]{:S(2)}) %collective-permute-start.31) | collective-permute-done | bytes 532512 | tf_op jit(solution)/shard_map/ppermute | solution.py:1213
  226.3 2.8 %collective-permute-start.38 = (bf16[1056,128]{1,0:T(8,128)(2,1)}, bf16[1056,128]{1,0:T(8,128)(2,1)S(1)}, u32[]{:S(2)}, u32[]{:S(2)}) collective-permute-start(bf16[1056,128]{1,0:T(8,128)(2,1)} %get-tuple-element.143), channel_id=1, source_target_pairs={{0,4},{4,0},{8,12},{12,8},{16,20},{20,16},{24,28},{28,24},{1,5},{5... | collective-permute-start | bytes 811016 | tf_op jit(solution)/shard_map/ppermute | solution.py:1213
  229.2 2.4 collective-permute-done.36.refs_12_
  232.7 3.0 %collective-permute-done.38.got = bf16[1056,128]{1,0:T(8,128)(2,1)S(1)} collective-permute-done((bf16[1056,128]{1,0:T(8,128)(2,1)}, bf16[1056,128]{1,0:T(8,128)(2,1)S(1)}, u32[]{:S(2)}, u32[]{:S(2)}) %collective-permute-start.38) | collective-permute-done | bytes 270368 | tf_op jit(solution)/shard_map/ppermute | solution.py:1213
  241.0 2.4 collective-permute-done.39.got
  248.8 3.2 %collective-permute-done.34.refs_5_ = bf16[576,128]{1,0:T(8,128)(2,1)S(1)} collective-permute-done((bf16[576,128]{1,0:T(8,128)(2,1)S(1)}, bf16[576,128]{1,0:T(8,128)(2,1)S(1)}, u32[]{:S(2)}, u32[]{:S(2)}) %collective-permute-start.34) | collective-permute-done | bytes 147488 | tf_op jit(solution)/shard_map/ppermute | solution.py:1213
  253.7 2.6 shard_map.207
  (190 shorter events, 84.9 us)
Async XLA Ops:
  7.2 128.8 %reduce-scatter.3.cloned.1.call-start = ((), (), s32[]{:S(2)}) async-start(), calls=%async_computation.2 | async-start | bytes 5898240 | tf_op jit(solution)/shard_map/reduce_scatter | solution.py:1290
  27.6 33.6 %collective-permute-start.8 = (bf16[64,512]{1,0:T(8,128)(2,1)S(1)}, bf16[64,512]{1,0:T(8,128)(2,1)S(1)}, u32[]{:S(2)}, u32[]{:S(2)}) collective-permute-start(bf16[64,512]{1,0:T(8,128)(2,1)S(1)} %get-tuple-element.189), channel_id=1, source_target_pairs={{0,24},{1,28},{4,25},{5,29},{8,16},{9,20},{12,17},{13,21},{16,8},{... | collective-permute-start | bytes 196616 | tf_op jit(solution)/shard_map/ppermute | solution.py:1187
  31.0 30.2 %collective-permute-start.7 = (bf16[64,512]{1,0:T(8,128)(2,1)S(1)}, bf16[64,512]{1,0:T(8,128)(2,1)S(1)}, u32[]{:S(2)}, u32[]{:S(2)}) collective-permute-start(bf16[64,512]{1,0:T(8,128)(2,1)S(1)} %get-tuple-element.190), channel_id=1, source_target_pairs={{0,16},{1,20},{4,17},{5,21},{8,24},{9,28},{12,25},{13,29},{16,0},{... | collective-permute-start | bytes 196616 | tf_op jit(solution)/shard_map/ppermute | solution.py:1187
  31.0 30.2 %collective-permute-start.6 = (bf16[64,512]{1,0:T(8,128)(2,1)S(1)}, bf16[64,512]{1,0:T(8,128)(2,1)S(1)}, u32[]{:S(2)}, u32[]{:S(2)}) collective-permute-start(bf16[64,512]{1,0:T(8,128)(2,1)S(1)} %get-tuple-element.191), channel_id=1, source_target_pairs={{0,8},{1,12},{4,9},{5,13},{8,0},{9,4},{12,1},{13,5},{16,24},{17,28... | collective-permute-start | bytes 196616 | tf_op jit(solution)/shard_map/ppermute | solution.py:1187
  32.0 29.2 %collective-permute-start.5 = (bf16[64,512]{1,0:T(8,128)(2,1)S(1)}, bf16[64,512]{1,0:T(8,128)(2,1)S(1)}, u32[]{:S(2)}, u32[]{:S(2)}) collective-permute-start(bf16[64,512]{1,0:T(8,128)(2,1)S(1)} %get-tuple-element.192), channel_id=1, source_target_pairs={{0,0},{1,4},{4,1},{5,5},{8,8},{9,12},{12,9},{13,13},{16,16},{17,20... | collective-permute-start | bytes 196616 | tf_op jit(solution)/shard_map/ppermute | solution.py:1187
  86.9 113.6 %reduce-scatter.5.cloned.1.call-start = ((), (), s32[]{:S(2)}) async-start(), calls=%async_computation.3 | async-start | bytes 3932160 | tf_op jit(solution)/shard_map/reduce_scatter | solution.py:1290
  132.0 21.8 %collective-permute-start.17 = (bf16[9216,128]{1,0:T(8,128)(2,1)}, bf16[9216,128]{1,0:T(8,128)(2,1)}, u32[]{:S(2)}, u32[]{:S(2)}) collective-permute-start(bf16[9216,128]{1,0:T(8,128)(2,1)} %get-tuple-element.115), channel_id=1, source_target_pairs={{0,1},{1,0},{2,3},{3,2},{4,5},{5,4},{6,7},{7,6},{8,9},{9,8},{10,11... | collective-permute-start | bytes 7077896 | tf_op jit(solution)/shard_map/ppermute | solution.py:1213
  137.1 17.9 %collective-permute-start.18 = (bf16[2304,128]{1,0:T(8,128)(2,1)S(1)}, bf16[2304,128]{1,0:T(8,128)(2,1)S(1)}, u32[]{:S(2)}, u32[]{:S(2)}) collective-permute-start(bf16[2304,128]{1,0:T(8,128)(2,1)S(1)} %slice.129), channel_id=1, source_target_pairs={{0,4},{4,0},{8,12},{12,8},{16,20},{20,16},{24,28},{28,24},{1,5},{5... | collective-permute-start | bytes 1769480 | tf_op jit(solution)/shard_map/ppermute | solution.py:1213
  138.7 15.1 %collective-permute-start.12 = (bf16[256,512]{1,0:T(8,128)(2,1)S(1)}, bf16[256,512]{1,0:T(8,128)(2,1)S(1)}, u32[]{:S(2)}, u32[]{:S(2)}) collective-permute-start(bf16[256,512]{1,0:T(8,128)(2,1)S(1)} %get-tuple-element.175), channel_id=1, source_target_pairs={{0,16},{1,20},{4,17},{5,21},{8,24},{9,28},{12,25},{13,29},{16,0},{... | collective-permute-start | bytes 786440 | tf_op jit(solution)/shard_map/ppermute | solution.py:1187
  156.9 19.1 %collective-permute-start.19 = (bf16[2304,128]{1,0:T(8,128)(2,1)S(1)}, bf16[2304,128]{1,0:T(8,128)(2,1)S(1)}, u32[]{:S(2)}, u32[]{:S(2)}) collective-permute-start(bf16[2304,128]{1,0:T(8,128)(2,1)S(1)} %get-tuple-element.168), channel_id=1, source_target_pairs={{0,4},{4,0},{8,12},{12,8},{16,20},{20,16},{24,28},{28,24},{1,5},{5... | collective-permute-start | bytes 1769480 | tf_op jit(solution)/shard_map/ppermute | solution.py:1213
  159.4 16.2 %collective-permute-start.20 = (bf16[1152,128]{1,0:T(8,128)(2,1)S(1)}, bf16[1152,128]{1,0:T(8,128)(2,1)S(1)}, u32[]{:S(2)}, u32[]{:S(2)}) collective-permute-start(bf16[1152,128]{1,0:T(8,128)(2,1)S(1)} %add_convert_fusion.5), channel_id=1, source_target_pairs={{0,8},{4,12},{8,0},{12,4},{16,24},{20,28},{24,16},{28,20},{1,9},{5... | collective-permute-start | bytes 884744 | tf_op jit(solution)/shard_map/ppermute | solution.py:1213
  161.0 14.2 %collective-permute-start.11 = (bf16[256,512]{1,0:T(8,128)(2,1)}, bf16[256,512]{1,0:T(8,128)(2,1)S(1)}, u32[]{:S(2)}, u32[]{:S(2)}) collective-permute-start(bf16[256,512]{1,0:T(8,128)(2,1)} %get-tuple-element.174), channel_id=1, source_target_pairs={{0,24},{1,28},{4,25},{5,29},{8,16},{9,20},{12,17},{13,21},{16,8},{... | collective-permute-start | bytes 786440 | tf_op jit(solution)/shard_map/ppermute | solution.py:1187
  163.4 18.6 %collective-permute-start.21 = (bf16[2,768,256]{2,1,0:T(8,128)(2,1)}, bf16[2,768,256]{2,1,0:T(8,128)(2,1)S(1)}, u32[]{:S(2)}, u32[]{:S(2)}) collective-permute-start(bf16[2,768,256]{2,1,0:T(8,128)(2,1)} %get-tuple-element.126), channel_id=1, source_target_pairs={{0,1},{1,0},{4,5},{5,4},{8,9},{9,8},{12,13},{13,12},{16,17},{17,16... | collective-permute-start | bytes 2359304 | tf_op jit(solution)/shard_map/ppermute | solution.py:1206
  163.5 34.5 %collective-permute-start.23 = (bf16[2304,128]{1,0:T(8,128)(2,1)S(1)}, bf16[2304,128]{1,0:T(8,128)(2,1)S(1)}, u32[]{:S(2)}, u32[]{:S(2)}) collective-permute-start(bf16[2304,128]{1,0:T(8,128)(2,1)S(1)} %get-tuple-element.167), channel_id=1, source_target_pairs={{0,4},{4,0},{8,12},{12,8},{16,20},{20,16},{24,28},{28,24},{1,5},{5... | collective-permute-start | bytes 1769480 | tf_op jit(solution)/shard_map/ppermute | solution.py:1213
  178.0 20.0 %collective-permute-start.25 = (bf16[1152,128]{1,0:T(8,128)(2,1)S(1)}, bf16[1152,128]{1,0:T(8,128)(2,1)S(1)}, u32[]{:S(2)}, u32[]{:S(2)}) collective-permute-start(bf16[1152,128]{1,0:T(8,128)(2,1)S(1)} %get-tuple-element.166), channel_id=1, source_target_pairs={{0,2},{1,3},{2,0},{3,1},{4,6},{5,7},{6,4},{7,5},{8,10},{9,11},{10,... | collective-permute-start | bytes 884744 | tf_op jit(solution)/shard_map/ppermute | solution.py:1213
  179.5 18.6 %collective-permute-start.24 = (bf16[576,128]{1,0:T(8,128)(2,1)S(1)}, bf16[576,128]{1,0:T(8,128)(2,1)S(1)}, u32[]{:S(2)}, u32[]{:S(2)}) collective-permute-start(bf16[576,128]{1,0:T(8,128)(2,1)S(1)} %add_convert_fusion.8), channel_id=1, source_target_pairs={{0,16},{4,20},{8,24},{12,28},{16,0},{20,4},{24,8},{28,12},{1,17},{... | collective-permute-start | bytes 442376 | tf_op jit(solution)/shard_map/ppermute | solution.py:1213
  206.0 14.0 %collective-permute-start.31 = (bf16[2080,128]{1,0:T(8,128)(2,1)}, bf16[2080,128]{1,0:T(8,128)(2,1)S(1)}, u32[]{:S(2)}, u32[]{:S(2)}) collective-permute-start(bf16[2080,128]{1,0:T(8,128)(2,1)} %get-tuple-element.138), channel_id=1, source_target_pairs={{0,2},{1,3},{2,0},{3,1},{4,6},{5,7},{6,4},{7,5},{8,10},{9,11},{10,... | collective-permute-start | bytes 1597448 | tf_op jit(solution)/shard_map/ppermute | solution.py:1213
  207.6 16.1 %collective-permute-start.29 = (bf16[192,512]{1,0:T(8,128)(2,1)S(1)}, bf16[192,512]{1,0:T(8,128)(2,1)S(1)}, u32[]{:S(2)}, u32[]{:S(2)}) collective-permute-start(bf16[192,512]{1,0:T(8,128)(2,1)S(1)} %get-tuple-element.181), channel_id=1, source_target_pairs={{0,8},{1,12},{4,9},{5,13},{8,0},{9,4},{12,1},{13,5},{16,24},{17,28... | collective-permute-start | bytes 589832 | tf_op jit(solution)/shard_map/ppermute | solution.py:1187
  209.1 16.0 %collective-permute-start.30 = (bf16[192,512]{1,0:T(8,128)(2,1)S(1)}, bf16[192,512]{1,0:T(8,128)(2,1)S(1)}, u32[]{:S(2)}, u32[]{:S(2)}) collective-permute-start(bf16[192,512]{1,0:T(8,128)(2,1)S(1)} %get-tuple-element.182), channel_id=1, source_target_pairs={{0,0},{1,4},{4,1},{5,5},{8,8},{9,12},{12,9},{13,13},{16,16},{17,20... | collective-permute-start | bytes 589832 | tf_op jit(solution)/shard_map/ppermute | solution.py:1187
  209.8 16.5 %collective-permute-start.28 = (bf16[192,512]{1,0:T(8,128)(2,1)S(1)}, bf16[192,512]{1,0:T(8,128)(2,1)S(1)}, u32[]{:S(2)}, u32[]{:S(2)}) collective-permute-start(bf16[192,512]{1,0:T(8,128)(2,1)S(1)} %get-tuple-element.183), channel_id=1, source_target_pairs={{0,16},{1,20},{4,17},{5,21},{8,24},{9,28},{12,25},{13,29},{16,0},{... | collective-permute-start | bytes 589832 | tf_op jit(solution)/shard_map/ppermute | solution.py:1187
  214.7 14.4 %collective-permute-start.27 = (bf16[192,512]{1,0:T(8,128)(2,1)S(1)}, bf16[192,512]{1,0:T(8,128)(2,1)S(1)}, u32[]{:S(2)}, u32[]{:S(2)}) collective-permute-start(bf16[192,512]{1,0:T(8,128)(2,1)S(1)} %get-tuple-element.184), channel_id=1, source_target_pairs={{0,24},{1,28},{4,25},{5,29},{8,16},{9,20},{12,17},{13,21},{16,8},{... | collective-permute-start | bytes 589832 | tf_op jit(solution)/shard_map/ppermute | solution.py:1187
  220.1 18.2 %collective-permute-start.32 = (bf16[1152,128]{1,0:T(8,128)(2,1)S(1)}, bf16[1152,128]{1,0:T(8,128)(2,1)S(1)}, u32[]{:S(2)}, u32[]{:S(2)}) collective-permute-start(bf16[1152,128]{1,0:T(8,128)(2,1)S(1)} %copy-done.16), channel_id=1, source_target_pairs={{0,2},{1,3},{2,0},{3,1},{4,6},{5,7},{6,4},{7,5},{8,10},{9,11},{10,... | collective-permute-start | bytes 884744 | tf_op jit(solution)/shard_map/ppermute | solution.py:1213
  225.2 14.3 %collective-permute-start.33 = (bf16[1152,128]{1,0:T(8,128)(2,1)S(1)}, bf16[1152,128]{1,0:T(8,128)(2,1)S(1)}, u32[]{:S(2)}, u32[]{:S(2)}) collective-permute-start(bf16[1152,128]{1,0:T(8,128)(2,1)S(1)} %add_convert_fusion.2), channel_id=1, source_target_pairs={{0,8},{4,12},{8,0},{12,4},{16,24},{20,28},{24,16},{28,20},{1,9},{5... | collective-permute-start | bytes 884744 | tf_op jit(solution)/shard_map/ppermute | solution.py:1213
  232.6 16.1 %collective-permute-start.37 = (bf16[384,128]{1,0:T(8,128)(2,1)S(1)}, bf16[384,128]{1,0:T(8,128)(2,1)S(1)}, u32[]{:S(2)}, u32[]{:S(2)}) collective-permute-start(bf16[384,128]{1,0:T(8,128)(2,1)S(1)} %add_convert_fusion.9), channel_id=1, source_target_pairs={{0,16},{4,20},{8,24},{12,28},{16,0},{20,4},{24,8},{28,12},{1,17},{... | collective-permute-start | bytes 294920 | tf_op jit(solution)/shard_map/ppermute | solution.py:1213
  (55 other events, 424.1 us)
Sparse Core Ops, SparseCore 0:
  87.0 48.9 reduce-scatter.2
  138.7 37.9 reduce-scatter.4

commit v5 on v4

--- a/solution.py
+++ b/solution.py
@@ -1345,8 +1345,8 @@
         else:
             leaving = ffn_1.add()
             got = late + ffn_1.send()
-            leaving += ffn_0.add(2)
-            got.append(ffn_0.send()[0])
+            leaving += ffn_0.add()
+            got += ffn_0.send()
     stays, leaves, sums, grad_inputs = embed_back_call(
         0, batches, seqs, every, me, inputs, [behind(grad, *leaving) for grad in grad_queries], sources,
         grad_middle, first_angles, gain_attn, w_qkv, token_line, gain_attn_1, gain_ffn_0, gain_ffn_1,

time: 268 us -> 267 us (level)
  starting transfers between devices: 52.3 us -> 48.1 us
  waiting for transfers between devices: 34.3 us -> 37.2 us
    reduce_scatter x2, waiting for transfers between devices: 1.73 us -> 8.96 us  [scatter(): return lax.psum_scatter(value, axis, scatter_dimension=0, tiled=True)]
    ppermute x18 -> x17, starting transfers between devices: 21.5 us -> 18 us  [swap(): return lax.ppermute(value, axis, [(n, n ^ bit) for n in range(count)])]
    ppermute x16, waiting for transfers between devices: 7.98 us -> 4.64 us  [exchange(): moves.append(lax.ppermute(piece, AXES, perm))]
    unnamed x72 -> x74, local copies, waits for them, and re-layouts: 9.83 us -> 8.77 us
    ppermute x18 -> x17, waiting for transfers between devices: 21.5 us -> 21.4 us  [swap(): return lax.ppermute(value, axis, [(n, n ^ bit) for n in range(count)])]
  transfers between devices with their start and end apart: 43 -> 42, of which waited for: 17 -> 15; matrix products, arithmetic and copies ran while one was open for 8% -> 8% of each run, Pallas kernels for 37% -> 38%
where the time goes in v5:
time: 267 us; the launch traced here: 262 us
  Pallas kernels  131 us (49%)
  starting transfers between devices  48.1 us (18%)
  waiting for transfers between devices  37.2 us (14%)
  other arithmetic  17.7 us (7%)
  between operations  14.9 us (6%)
  local copies, waits for them, and re-layouts  13.8 us (5%)
    pallas_call x2, Pallas kernels, attention_back_call(): call(functools.partial(attention_back_kernel, rows, members), (shape((cou...  23.2 us
    ppermute x16, starting transfers between devices, exchange(): moves.append(lax.ppermute(piece, AXES, perm))  22.9 us
    pallas_call x1, Pallas kernels, forward_call(): call(functools.partial(forward_kernel, layer, rows, members), (shape((cou...  21.9 us
    ppermute x17, waiting for transfers between devices, swap(): return lax.ppermute(value, axis, [(n, n ^ bit) for n in range(count)])  21.4 us
    pallas_call x1, Pallas kernels, ffn_back_call(): call(functools.partial(ffn_back_kernel, layer, rows, members, packs), pac...  20.8 us
    ppermute x17, starting transfers between devices, swap(): return lax.ppermute(value, axis, [(n, n ^ bit) for n in range(count)])  18 us
    pallas_call x1, Pallas kernels, middle_call(): call(functools.partial(middle_kernel, layer, rows, members, packs), (shap...  16.5 us
    pallas_call x1, Pallas kernels, embed_back_call(): call(functools.partial(embed_back_kernel, layer, members, cuts, packs), p...  14.8 us
  transfers between devices with their start and end apart: 42, of which 15 were waited for; matrix products, arithmetic and copies ran while one was open for 8% of the time, Pallas kernels for 38%

profile of v5, /device:TPU:0, one launch (start us, length us, event | category | flops | bytes accessed | tf_op | source)
XLA Modules:
  0.0 262.4 jit_solution(17043169839374644991)
XLA Ops:
  8.1 4.1 %collective-permute-start.1 = (s32[192]{0:T(256)S(1)}, s32[192]{0:T(256)S(1)}, u32[]{:S(2)}, u32[]{:S(2)}) collective-permute-start(s32[192]{0:T(256)S(1)} %bitcast.78), channel_id=1, source_target_pairs={{0,16},{1,20},{4,17},{5,21},{8,24},{9,28},{12,25},{13,29},{16,0},{... | collective-permute-start | bytes 2312 | tf_op jit(solution)/shard_map/ppermute | solution.py:1187
  14.8 2.4 fusion.table.refs_1_.refs_7_
  19.8 6.0 %shard_map.194 = (bf16[768,512]{1,0:T(8,128)(2,1)}, bf16[768,512]{1,0:T(8,128)(2,1)}, bf16[2,768,512]{2,1,0:T(8,128)(2,1)}) custom-call(s32[1,768]{1,0:T(1,128)} %reshape.100.tokens.refs_10_, bf16[256,512]{1,0:T(8,128)(2,1)} %embed.1, bf16[2,512]{1,0:T(2,128)(2,1)} %refs_8_.3, bf16[2,512,1536]{2,1,0:T(8,128)(2,1)} %refs_9_.1, ...), custom_call_target="tpu_custom_call" | custom-call | tf_op jit(solution)/shard_map/pallas_call | solution.py:330
  27.6 3.5 %collective-permute-start.8 = (bf16[64,512]{1,0:T(8,128)(2,1)S(1)}, bf16[64,512]{1,0:T(8,128)(2,1)S(1)}, u32[]{:S(2)}, u32[]{:S(2)}) collective-permute-start(bf16[64,512]{1,0:T(8,128)(2,1)S(1)} %get-tuple-element.187), channel_id=1, source_target_pairs={{0,24},{1,28},{4,25},{5,29},{8,16},{9,20},{12,17},{13,21},{16,8},{... | collective-permute-start | bytes 196616 | tf_op jit(solution)/shard_map/ppermute | solution.py:1187
  34.9 21.9 %shard_map.195 = (bf16[768,512]{1,0:T(8,128)(2,1)}, bf16[8,512]{1,0:T(8,128)(2,1)}, bf16[768,512]{1,0:T(8,128)(2,1)}, bf16[768,512]{1,0:T(8,128)(2,1)}, f32[2,76...) custom-call(s32[3]{0:T(128)} %pad_add_fusion.1.me, bf16[768,512]{1,0:T(8,128)(2,1)} %get-tuple-element.88.inputs, ...), custom_call_target="tpu_custom_call" | custom-call | tf_op jit(solution)/shard_map/pallas_call | solution.py:748
  56.8 3.2 %collective-permute-start.9 = (bf16[8,512]{1,0:T(8,128)(2,1)}, bf16[8,512]{1,0:T(8,128)(2,1)S(1)}, u32[]{:S(2)}, u32[]{:S(2)}) collective-permute-start(bf16[8,512]{1,0:T(8,128)(2,1)} %get-tuple-element.93), channel_id=1, source_target_pairs={{0,1},{1,0},{4,5},{5,4},{8,9},{9,8},{12,13},{13,12},{16,17},{17,16... | collective-permute-start | bytes 24584 | tf_op jit(solution)/shard_map/ppermute | solution.py:1206
  61.8 5.5 %shard_map.196 = (bf16[256,1536]{1,0:T(8,128)(2,1)}, f32[256,512]{1,0:T(8,128)}, bf16[256,512]{1,0:T(8,128)(2,1)}, bf16[2,256,512]{2,1,0:T(8,128)(2,1)}) custom-call(s32[3]{0:T(128)} %pad_add_fusion.1.me, bf16[768,512]{1,0:T(8,128)(2,1)} %get-tuple-element.92.first, bf16[8,512]{1,0:T(8,128)(2,1)} %copy-done.33, bf16[1536,512]{1,0:T(8,128)(2,1)} %refs_8_.2, ...), custom_call_target="tpu_custom_call" | custom-call | tf_op jit(solution)/shard_map/pallas_call | solution.py:375
  70.2 16.5 %shard_map.197 = (bf16[256,512]{1,0:T(8,128)(2,1)}, bf16[18432,128]{1,0:T(8,128)(2,1)}, f32[1,512]{1,0:T(1,128)}, f32[256,512]{1,0:T(8,128)}, bf16[256,512]{1,0:...) custom-call(s32[3]{0:T(128)} %pad_add_fusion.1.me, f32[256,512]{1,0:T(8,128)} %get-tuple-element.94.inputs, ...), custom_call_target="tpu_custom_call" | custom-call | tf_op jit(solution)/shard_map/pallas_call | solution.py:944
  91.8 10.9 %shard_map.198 = (bf16[12288,128]{1,0:T(8,128)(2,1)}, f32[1,512]{1,0:T(1,128)}, bf16[768,512]{1,0:T(8,128)(2,1)}, bf16[8,512]{1,0:T(8,128)(2,1)}) custom-call(s32[3]{0:T(128)} %pad_add_fusion.1.me, f32[256,512]{1,0:T(8,128)} %get-tuple-element.94.inputs, bf16[256,512]{1,0:T(8,128)(2,1)} %get-tuple-element.101.refs_0_, ...), custom_call_target="tpu_custom_call" | custom-call | tf_op jit(solution)/shard_map/pallas_call | solution.py:1132
  105.8 20.8 %shard_map.199 = (bf16[9216,128]{1,0:T(8,128)(2,1)}, bf16[9216,128]{1,0:T(8,128)(2,1)}, f32[1,512]{1,0:T(1,128)}, f32[768,512]{1,0:T(8,128)}, bf16[768,512]{1,0:T(8,128)(2,1)}) custom-call(s32[3]{0:T(128)} %pad_add_fusion.1.me, bf16[768,512]{1,0:T(8,128)(2,1)} %get-tuple-element.107.grad_ref, bf16[8,512]{1,0:T(8,128)(2,1)} %copy-done.34, ...), custom_call_target="tpu_custom_call" | custom-call | tf_op jit(solution)/shard_map/pallas_call | solution.py:874
  127.1 9.0 %reduce-scatter.3.cloned.1.call-done.refs_6_ = bf16[4608,128]{1,0:T(8,128)(2,1)} async-done(((bf16[18432,128]{1,0:T(8,128)(2,1)}), bf16[4608,128]{1,0:T(8,128)(2,1)}) %reduce-scatter.3.cloned.1.call-update) | async-done | bytes 1179664 | tf_op jit(solution)/shard_map/reduce_scatter | solution.py:1290
  138.7 2.4 collective-permute-start.12
  141.1 11.4 %shard_map.200 = (bf16[768,256]{1,0:T(8,128)(2,1)}, bf16[2,768,256]{2,1,0:T(8,128)(2,1)}, bf16[2,768,256]{2,1,0:T(8,128)(2,1)}) custom-call(s32[3]{0:T(128)} %pad_add_fusion.1.me, bf16[768,512]{1,0:T(8,128)(2,1)} %get-tuple-element.98.queries, bf16[2,768,512]{2,1,0:T(8,128)(2,1)} %get-tuple-element.90.own, bf16[2,768,512]{2,1,0:T(8,128)(2,1)} %copy-done, ...), custom_call_target="tpu_custom_call" | custom-call | tf_op jit(solution)/shard_map/pallas_call | solution.py:606
  161.0 2.4 collective-permute-start.11
  163.5 11.8 %shard_map.201 = (bf16[768,256]{1,0:T(8,128)(2,1)}, bf16[2,768,256]{2,1,0:T(8,128)(2,1)}, bf16[2,768,256]{2,1,0:T(8,128)(2,1)}) custom-call(s32[3]{0:T(128)} %pad_add_fusion.1.me, bf16[768,512]{1,0:T(8,128)(2,1)} %get-tuple-element.98.queries, bf16[2,768,512]{2,1,0:T(8,128)(2,1)} %get-tuple-element.90.own, bf16[2,768,512]{2,1,0:T(8,128)(2,1)} %copy-done, ...), custom_call_target="tpu_custom_call" | custom-call | tf_op jit(solution)/shard_map/pallas_call | solution.py:606
  179.0 2.6 collective-permute-start.24
  182.7 14.8 %shard_map.202 = (bf16[4096,128]{1,0:T(8,128)(2,1)}, bf16[4128,128]{1,0:T(8,128)(2,1)}, f32[16,128]{1,0:T(8,128)}, bf16[768,512]{1,0:T(8,128)(2,1)}) custom-call(s32[3]{0:T(128)} %pad_add_fusion.1.me, bf16[768,512]{1,0:T(8,128)(2,1)} %get-tuple-element.88.inputs, bf16[768,256]{1,0:T(8,128)(2,1)} %get-tuple-element.123.refs_0_, ...), custom_call_target="tpu_custom_call" | custom-call | tf_op jit(solution)/shard_map/pallas_call | solution.py:1068
  202.6 2.9 %shard_map.203 = (bf16[2048,128]{1,0:T(8,128)(2,1)}, bf16[2080,128]{1,0:T(8,128)(2,1)}, f32[16,128]{1,0:T(8,128)}) custom-call(bf16[4096,128]{1,0:T(8,128)(2,1)} %get-tuple-element.134.kept, bf16[4128,128]{1,0:T(8,128)(2,1)} %collective-permute-done.26.got, f32[16,128]{1,0:T(8,128)} %get-tuple-element.137.sums), custom_call_target="tpu_custom_call" | custom-call | tf_op jit(solution)/shard_map/pallas_call | solution.py:222
  211.0 2.9 %collective-permute-done.34.refs_11_ = bf16[1536,128]{1,0:T(8,128)(2,1)S(1)} collective-permute-done((bf16[1536,128]{1,0:T(8,128)(2,1)S(1)}, bf16[1536,128]{1,0:T(8,128)(2,1)S(1)}, u32[]{:S(2)}, u32[]{:S(2)}) %collective-permute-start.34) | collective-permute-done | bytes 393248 | tf_op jit(solution)/shard_map/ppermute | solution.py:1213
  216.5 2.9 %collective-permute-done.31.got = bf16[2080,128]{1,0:T(8,128)(2,1)S(1)} collective-permute-done((bf16[2080,128]{1,0:T(8,128)(2,1)}, bf16[2080,128]{1,0:T(8,128)(2,1)S(1)}, u32[]{:S(2)}, u32[]{:S(2)}) %collective-permute-start.31) | collective-permute-done | bytes 532512 | tf_op jit(solution)/shard_map/ppermute | solution.py:1213
  225.9 4.9 %collective-permute-done.35.refs_12_ = bf16[768,128]{1,0:T(8,128)(2,1)S(1)} collective-permute-done((bf16[768,128]{1,0:T(8,128)(2,1)S(1)}, bf16[768,128]{1,0:T(8,128)(2,1)S(1)}, u32[]{:S(2)}, u32[]{:S(2)}) %collective-permute-start.35) | collective-permute-done | bytes 196640 | tf_op jit(solution)/shard_map/ppermute | solution.py:1213
  236.6 2.6 collective-permute-done.32.refs_4_
  247.3 3.3 %collective-permute-done.33.refs_5_ = bf16[576,128]{1,0:T(8,128)(2,1)S(1)} collective-permute-done((bf16[576,128]{1,0:T(8,128)(2,1)S(1)}, bf16[576,128]{1,0:T(8,128)(2,1)S(1)}, u32[]{:S(2)}, u32[]{:S(2)}) %collective-permute-start.33) | collective-permute-done | bytes 147488 | tf_op jit(solution)/shard_map/ppermute | solution.py:1213
  252.7 2.6 shard_map.207
  (190 shorter events, 76.3 us)
Async XLA Ops:
  7.2 128.8 %reduce-scatter.3.cloned.1.call-start = ((), (), s32[]{:S(2)}) async-start(), calls=%async_computation.2 | async-start | bytes 5898240 | tf_op jit(solution)/shard_map/reduce_scatter | solution.py:1290
  27.6 33.6 %collective-permute-start.8 = (bf16[64,512]{1,0:T(8,128)(2,1)S(1)}, bf16[64,512]{1,0:T(8,128)(2,1)S(1)}, u32[]{:S(2)}, u32[]{:S(2)}) collective-permute-start(bf16[64,512]{1,0:T(8,128)(2,1)S(1)} %get-tuple-element.187), channel_id=1, source_target_pairs={{0,24},{1,28},{4,25},{5,29},{8,16},{9,20},{12,17},{13,21},{16,8},{... | collective-permute-start | bytes 196616 | tf_op jit(solution)/shard_map/ppermute | solution.py:1187
  31.0 30.2 %collective-permute-start.7 = (bf16[64,512]{1,0:T(8,128)(2,1)S(1)}, bf16[64,512]{1,0:T(8,128)(2,1)S(1)}, u32[]{:S(2)}, u32[]{:S(2)}) collective-permute-start(bf16[64,512]{1,0:T(8,128)(2,1)S(1)} %get-tuple-element.188), channel_id=1, source_target_pairs={{0,16},{1,20},{4,17},{5,21},{8,24},{9,28},{12,25},{13,29},{16,0},{... | collective-permute-start | bytes 196616 | tf_op jit(solution)/shard_map/ppermute | solution.py:1187
  31.0 30.2 %collective-permute-start.6 = (bf16[64,512]{1,0:T(8,128)(2,1)S(1)}, bf16[64,512]{1,0:T(8,128)(2,1)S(1)}, u32[]{:S(2)}, u32[]{:S(2)}) collective-permute-start(bf16[64,512]{1,0:T(8,128)(2,1)S(1)} %get-tuple-element.189), channel_id=1, source_target_pairs={{0,8},{1,12},{4,9},{5,13},{8,0},{9,4},{12,1},{13,5},{16,24},{17,28... | collective-permute-start | bytes 196616 | tf_op jit(solution)/shard_map/ppermute | solution.py:1187
  32.0 29.2 %collective-permute-start.5 = (bf16[64,512]{1,0:T(8,128)(2,1)S(1)}, bf16[64,512]{1,0:T(8,128)(2,1)S(1)}, u32[]{:S(2)}, u32[]{:S(2)}) collective-permute-start(bf16[64,512]{1,0:T(8,128)(2,1)S(1)} %get-tuple-element.190), channel_id=1, source_target_pairs={{0,0},{1,4},{4,1},{5,5},{8,8},{9,12},{12,9},{13,13},{16,16},{17,20... | collective-permute-start | bytes 196616 | tf_op jit(solution)/shard_map/ppermute | solution.py:1187
  86.9 113.3 %reduce-scatter.5.cloned.1.call-start = ((), (), s32[]{:S(2)}) async-start(), calls=%async_computation.3 | async-start | bytes 3932160 | tf_op jit(solution)/shard_map/reduce_scatter | solution.py:1290
  88.9 15.2 %collective-permute-start.13 = (bf16[256,512]{1,0:T(8,128)(2,1)S(1)}, bf16[256,512]{1,0:T(8,128)(2,1)S(1)}, u32[]{:S(2)}, u32[]{:S(2)}) collective-permute-start(bf16[256,512]{1,0:T(8,128)(2,1)S(1)} %get-tuple-element.171), channel_id=1, source_target_pairs={{0,8},{1,12},{4,9},{5,13},{8,0},{9,4},{12,1},{13,5},{16,24},{17,28... | collective-permute-start | bytes 786440 | tf_op jit(solution)/shard_map/ppermute | solution.py:1187
  90.3 13.8 %collective-permute-start.14 = (bf16[256,512]{1,0:T(8,128)(2,1)S(1)}, bf16[256,512]{1,0:T(8,128)(2,1)S(1)}, u32[]{:S(2)}, u32[]{:S(2)}) collective-permute-start(bf16[256,512]{1,0:T(8,128)(2,1)S(1)} %get-tuple-element.174), channel_id=1, source_target_pairs={{0,0},{1,4},{4,1},{5,5},{8,8},{9,12},{12,9},{13,13},{16,16},{17,20... | collective-permute-start | bytes 786440 | tf_op jit(solution)/shard_map/ppermute | solution.py:1187
  126.6 27.2 %collective-permute-start.17 = (bf16[9216,128]{1,0:T(8,128)(2,1)}, bf16[9216,128]{1,0:T(8,128)(2,1)}, u32[]{:S(2)}, u32[]{:S(2)}) collective-permute-start(bf16[9216,128]{1,0:T(8,128)(2,1)} %get-tuple-element.115), channel_id=1, source_target_pairs={{0,1},{1,0},{2,3},{3,2},{4,5},{5,4},{6,7},{7,6},{8,9},{9,8},{10,11... | collective-permute-start | bytes 7077896 | tf_op jit(solution)/shard_map/ppermute | solution.py:1213
  137.1 17.9 %collective-permute-start.18 = (bf16[2304,128]{1,0:T(8,128)(2,1)S(1)}, bf16[2304,128]{1,0:T(8,128)(2,1)S(1)}, u32[]{:S(2)}, u32[]{:S(2)}) collective-permute-start(bf16[2304,128]{1,0:T(8,128)(2,1)S(1)} %slice.117), channel_id=1, source_target_pairs={{0,4},{4,0},{8,12},{12,8},{16,20},{20,16},{24,28},{28,24},{1,5},{5... | collective-permute-start | bytes 1769480 | tf_op jit(solution)/shard_map/ppermute | solution.py:1213
  138.7 15.1 %collective-permute-start.12 = (bf16[256,512]{1,0:T(8,128)(2,1)S(1)}, bf16[256,512]{1,0:T(8,128)(2,1)S(1)}, u32[]{:S(2)}, u32[]{:S(2)}) collective-permute-start(bf16[256,512]{1,0:T(8,128)(2,1)S(1)} %get-tuple-element.173), channel_id=1, source_target_pairs={{0,16},{1,20},{4,17},{5,21},{8,24},{9,28},{12,25},{13,29},{16,0},{... | collective-permute-start | bytes 786440 | tf_op jit(solution)/shard_map/ppermute | solution.py:1187
  156.9 19.1 %collective-permute-start.19 = (bf16[2304,128]{1,0:T(8,128)(2,1)S(1)}, bf16[2304,128]{1,0:T(8,128)(2,1)S(1)}, u32[]{:S(2)}, u32[]{:S(2)}) collective-permute-start(bf16[2304,128]{1,0:T(8,128)(2,1)S(1)} %get-tuple-element.166), channel_id=1, source_target_pairs={{0,4},{4,0},{8,12},{12,8},{16,20},{20,16},{24,28},{28,24},{1,5},{5... | collective-permute-start | bytes 1769480 | tf_op jit(solution)/shard_map/ppermute | solution.py:1213
  159.4 16.3 %collective-permute-start.20 = (bf16[1152,128]{1,0:T(8,128)(2,1)S(1)}, bf16[1152,128]{1,0:T(8,128)(2,1)S(1)}, u32[]{:S(2)}, u32[]{:S(2)}) collective-permute-start(bf16[1152,128]{1,0:T(8,128)(2,1)S(1)} %add_convert_fusion.4), channel_id=1, source_target_pairs={{0,8},{4,12},{8,0},{12,4},{16,24},{20,28},{24,16},{28,20},{1,9},{5... | collective-permute-start | bytes 884744 | tf_op jit(solution)/shard_map/ppermute | solution.py:1213
  161.0 14.3 %collective-permute-start.11 = (bf16[256,512]{1,0:T(8,128)(2,1)}, bf16[256,512]{1,0:T(8,128)(2,1)S(1)}, u32[]{:S(2)}, u32[]{:S(2)}) collective-permute-start(bf16[256,512]{1,0:T(8,128)(2,1)} %get-tuple-element.172), channel_id=1, source_target_pairs={{0,24},{1,28},{4,25},{5,29},{8,16},{9,20},{12,17},{13,21},{16,8},{... | collective-permute-start | bytes 786440 | tf_op jit(solution)/shard_map/ppermute | solution.py:1187
  163.4 18.2 %collective-permute-start.21 = (bf16[2,768,256]{2,1,0:T(8,128)(2,1)}, bf16[2,768,256]{2,1,0:T(8,128)(2,1)S(1)}, u32[]{:S(2)}, u32[]{:S(2)}) collective-permute-start(bf16[2,768,256]{2,1,0:T(8,128)(2,1)} %get-tuple-element.126), channel_id=1, source_target_pairs={{0,1},{1,0},{4,5},{5,4},{8,9},{9,8},{12,13},{13,12},{16,17},{17,16... | collective-permute-start | bytes 2359304 | tf_op jit(solution)/shard_map/ppermute | solution.py:1206
  163.5 34.1 %collective-permute-start.23 = (bf16[2304,128]{1,0:T(8,128)(2,1)S(1)}, bf16[2304,128]{1,0:T(8,128)(2,1)S(1)}, u32[]{:S(2)}, u32[]{:S(2)}) collective-permute-start(bf16[2304,128]{1,0:T(8,128)(2,1)S(1)} %get-tuple-element.165), channel_id=1, source_target_pairs={{0,4},{4,0},{8,12},{12,8},{16,20},{20,16},{24,28},{28,24},{1,5},{5... | collective-permute-start | bytes 1769480 | tf_op jit(solution)/shard_map/ppermute | solution.py:1213
  177.3 20.2 %collective-permute-start.25 = (bf16[2304,128]{1,0:T(8,128)(2,1)S(1)}, bf16[2304,128]{1,0:T(8,128)(2,1)S(1)}, u32[]{:S(2)}, u32[]{:S(2)}) collective-permute-start(bf16[2304,128]{1,0:T(8,128)(2,1)S(1)} %add_convert_fusion), channel_id=1, source_target_pairs={{0,2},{1,3},{2,0},{3,1},{4,6},{5,7},{6,4},{7,5},{8,10},{9,11},{10,... | collective-permute-start | bytes 1769480 | tf_op jit(solution)/shard_map/ppermute | solution.py:1213
  179.0 18.6 %collective-permute-start.24 = (bf16[576,128]{1,0:T(8,128)(2,1)S(1)}, bf16[576,128]{1,0:T(8,128)(2,1)S(1)}, u32[]{:S(2)}, u32[]{:S(2)}) collective-permute-start(bf16[576,128]{1,0:T(8,128)(2,1)S(1)} %add_convert_fusion.7), channel_id=1, source_target_pairs={{0,16},{4,20},{8,24},{12,28},{16,0},{20,4},{24,8},{28,12},{1,17},{... | collective-permute-start | bytes 442376 | tf_op jit(solution)/shard_map/ppermute | solution.py:1213
  205.5 13.9 %collective-permute-start.31 = (bf16[2080,128]{1,0:T(8,128)(2,1)}, bf16[2080,128]{1,0:T(8,128)(2,1)S(1)}, u32[]{:S(2)}, u32[]{:S(2)}) collective-permute-start(bf16[2080,128]{1,0:T(8,128)(2,1)} %get-tuple-element.138), channel_id=1, source_target_pairs={{0,2},{1,3},{2,0},{3,1},{4,6},{5,7},{6,4},{7,5},{8,10},{9,11},{10,... | collective-permute-start | bytes 1597448 | tf_op jit(solution)/shard_map/ppermute | solution.py:1213
  207.1 16.0 %collective-permute-start.29 = (bf16[192,512]{1,0:T(8,128)(2,1)S(1)}, bf16[192,512]{1,0:T(8,128)(2,1)S(1)}, u32[]{:S(2)}, u32[]{:S(2)}) collective-permute-start(bf16[192,512]{1,0:T(8,128)(2,1)S(1)} %get-tuple-element.179), channel_id=1, source_target_pairs={{0,8},{1,12},{4,9},{5,13},{8,0},{9,4},{12,1},{13,5},{16,24},{17,28... | collective-permute-start | bytes 589832 | tf_op jit(solution)/shard_map/ppermute | solution.py:1187
  208.6 15.2 %collective-permute-start.30 = (bf16[192,512]{1,0:T(8,128)(2,1)S(1)}, bf16[192,512]{1,0:T(8,128)(2,1)S(1)}, u32[]{:S(2)}, u32[]{:S(2)}) collective-permute-start(bf16[192,512]{1,0:T(8,128)(2,1)S(1)} %get-tuple-element.180), channel_id=1, source_target_pairs={{0,0},{1,4},{4,1},{5,5},{8,8},{9,12},{12,9},{13,13},{16,16},{17,20... | collective-permute-start | bytes 589832 | tf_op jit(solution)/shard_map/ppermute | solution.py:1187
  209.3 16.5 %collective-permute-start.28 = (bf16[192,512]{1,0:T(8,128)(2,1)S(1)}, bf16[192,512]{1,0:T(8,128)(2,1)S(1)}, u32[]{:S(2)}, u32[]{:S(2)}) collective-permute-start(bf16[192,512]{1,0:T(8,128)(2,1)S(1)} %get-tuple-element.181), channel_id=1, source_target_pairs={{0,16},{1,20},{4,17},{5,21},{8,24},{9,28},{12,25},{13,29},{16,0},{... | collective-permute-start | bytes 589832 | tf_op jit(solution)/shard_map/ppermute | solution.py:1187
  223.0 16.1 %collective-permute-start.32 = (bf16[1152,128]{1,0:T(8,128)(2,1)S(1)}, bf16[1152,128]{1,0:T(8,128)(2,1)S(1)}, u32[]{:S(2)}, u32[]{:S(2)}) collective-permute-start(bf16[1152,128]{1,0:T(8,128)(2,1)S(1)} %add_convert_fusion.3), channel_id=1, source_target_pairs={{0,8},{4,12},{8,0},{12,4},{16,24},{20,28},{24,16},{28,20},{1,9},{5... | collective-permute-start | bytes 884744 | tf_op jit(solution)/shard_map/ppermute | solution.py:1213
  231.8 15.5 %collective-permute-start.36 = (bf16[384,128]{1,0:T(8,128)(2,1)S(1)}, bf16[384,128]{1,0:T(8,128)(2,1)S(1)}, u32[]{:S(2)}, u32[]{:S(2)}) collective-permute-start(bf16[384,128]{1,0:T(8,128)(2,1)S(1)} %add_convert_fusion.8), channel_id=1, source_target_pairs={{0,16},{4,20},{8,24},{12,28},{16,0},{20,4},{24,8},{28,12},{1,17},{... | collective-permute-start | bytes 294920 | tf_op jit(solution)/shard_map/ppermute | solution.py:1213
  (55 other events, 426.9 us)
Sparse Core Ops, SparseCore 0:
  87.0 48.9 reduce-scatter.2
  138.7 37.9 reduce-scatter.4
